TPU v7x, 32 devices: a whole 2x2x4 slice. The times are simulated.
32 devices in a mesh: ctx: 8 (over z, y), fsdp: 4 (over x, core).
Axes of the slice: x: 2, y: 2, z: 4, core: 2. Of those that a mesh axis runs over, the one named last changes fastest.
Arguments:
- inputs: bfloat16 [4, 1024, 1024], P('fsdp', 'ctx'), may hold values from -6 to 6
- out_grad: bfloat16 [4, 1024, 1024], P('fsdp', 'ctx'), may hold values from -6 to 6
- segments: int32 [4, 1024], P('fsdp', 'ctx'), may hold values from 0 to 1, never falling along the last dimension, each value on 1 to 768 neighbouring positions
- pairs: int32 [4, 8], P('fsdp', 'ctx'), may hold values from 0 to 7, each once within a row
- w_qkv: float32 [1024, 3072], P(('ctx', 'fsdp')), may hold values from -0.1875 to 0.1875
- w_out: float32 [1024, 1024], P(('ctx', 'fsdp')), may hold values from -0.5 to 0.5
- w_up: float32 [1024, 4096], P(('ctx', 'fsdp'))
- w_down: float32 [4096, 1024], P(('ctx', 'fsdp')), may hold values from -0.09375 to 0.09375
- up_bias: float32 [4096], P(('ctx', 'fsdp'))
- vectors: float32 [8, 1024], P(None, ('ctx', 'fsdp')), as said below
- first_qkv: float32 [1024, 3072], P(('ctx', 'fsdp'))
- first_out: float32 [1024, 1024], P(('ctx', 'fsdp'))
- first_up: float32 [1024, 4096], P(('ctx', 'fsdp'))
- first_down: float32 [4096, 1024], P(('ctx', 'fsdp'))
- first_bias: float32 [4096], P(('ctx', 'fsdp'))
- first_vectors: float32 [8, 1024], P(None, ('ctx', 'fsdp'))
- second_qkv: float32 [1024, 3072], P(('ctx', 'fsdp')), as said below
- second_out: float32 [1024, 1024], P(('ctx', 'fsdp')), as said below
- second_up: float32 [1024, 4096], P(('ctx', 'fsdp')), as said below
- second_down: float32 [4096, 1024], P(('ctx', 'fsdp')), as said below
- second_bias: float32 [4096], P(('ctx', 'fsdp')), as said below
- second_vectors: float32 [8, 1024], P(None, ('ctx', 'fsdp')), as said below
Outputs:
- outputs: bfloat16 [4, 1024, 1024], P('fsdp', 'ctx')
- in_grad: float32 [4, 1024, 1024], P('fsdp', 'ctx')
- grad_norm: float32 [], replicated
- grad_qkv: float32 [1024, 3072], P(('ctx', 'fsdp'))
- update_qkv: float32 [1024, 3072], P(('ctx', 'fsdp'))
- next_first_qkv: float32 [1024, 3072], P(('ctx', 'fsdp'))
- next_second_qkv: float32 [1024, 3072], P(('ctx', 'fsdp'))
- grad_out: float32 [1024, 1024], P(('ctx', 'fsdp'))
- update_out: float32 [1024, 1024], P(('ctx', 'fsdp'))
- next_first_out: float32 [1024, 1024], P(('ctx', 'fsdp'))
- next_second_out: float32 [1024, 1024], P(('ctx', 'fsdp'))
- grad_up: float32 [1024, 4096], P(('ctx', 'fsdp'))
- update_up: float32 [1024, 4096], P(('ctx', 'fsdp'))
- next_first_up: float32 [1024, 4096], P(('ctx', 'fsdp'))
- next_second_up: float32 [1024, 4096], P(('ctx', 'fsdp'))
- grad_down: float32 [4096, 1024], P(('ctx', 'fsdp'))
- update_down: float32 [4096, 1024], P(('ctx', 'fsdp'))
- next_first_down: float32 [4096, 1024], P(('ctx', 'fsdp'))
- next_second_down: float32 [4096, 1024], P(('ctx', 'fsdp'))
- grad_bias: float32 [4096], P(('ctx', 'fsdp'))
- update_bias: float32 [4096], P(('ctx', 'fsdp'))
- next_first_bias: float32 [4096], P(('ctx', 'fsdp'))
- next_second_bias: float32 [4096], P(('ctx', 'fsdp'))
- grad_vectors: float32 [8, 1024], P(None, ('ctx', 'fsdp'))
- update_vectors: float32 [8, 1024], P(None, ('ctx', 'fsdp'))
- next_first_vectors: float32 [8, 1024], P(None, ('ctx', 'fsdp'))
- next_second_vectors: float32 [8, 1024], P(None, ('ctx', 'fsdp'))
Inputs may be any that keep to these rules, and one draw needn't show every extreme that they name: `segments`: in each sequence the numbers never fall; every document spans 1 to 768 positions. `pairs`: each row is a permutation. `vectors`: rows 0 and 2 are positive. `second_qkv`: positive. `second_out`: positive. `second_up`: positive. `second_down`: positive. `second_bias`: positive. `second_vectors`: positive.
All inputs are finite; a program needn't handle non-finite values.
Results may differ from a plain program's by a relative error of at most 0.023.
Values may be sent and summed in bfloat16 or wider, within the bound.
No kernel may reach another device: no remote copies, remote signals or barrier semaphores. Data moves between devices by JAX's collectives and lax.ppermute only.
A program may use at most 256 MiB of HBM per device.

v0:
```python
import functools
import math

import jax
import jax.numpy as jnp
from jax import lax
from jax.experimental import pallas as pl
from jax.experimental.pallas import tpu as pltpu
from jax.sharding import Mesh
from jax.sharding import PartitionSpec as P

HEADS = 16
HD = 64


norm_eps = 1e-05
beta_one = 0.9
beta_two = 0.95
adam_eps = 1e-08
learn_rate = 0.02
weight_decay = 0.1
adam_step = 10
max_norm = 1.0
masked = -1e30
group_heads = 2


def layer_norm(field, gain, shift):
    center = field - jnp.mean(field, -1, keepdims=True)
    spread = jnp.mean(center * center, -1, keepdims=True)
    return center * lax.rsqrt(spread + norm_eps) * gain + shift


def gelu_exact(field):
    return jax.nn.gelu(field, approximate=False)


def contract(left, right, left_dim, right_dim):
    return lax.dot_general(
        left, right, (((left_dim,), (right_dim,)), ((), ())), preferred_element_type=jnp.float32
    )


def place(pair_ids, block, n_ctx):
    blocks = jnp.stack([pair_ids, 2 * n_ctx - 1 - pair_ids], 1).reshape(-1)
    offsets = jnp.arange(block, dtype=jnp.int32)
    return (blocks[:, None] * block + offsets[None, :]).reshape(-1)


def pick(array, first):
    return lax.dynamic_slice_in_dim(array, first, group_heads, 1)


def adamw(weight, grad, first, second, clip):
    clipped = grad * clip
    first_new = beta_one * first + (1.0 - beta_one) * clipped
    second_new = beta_two * second + (1.0 - beta_two) * clipped * clipped
    first_hat = first_new / (1.0 - beta_one**adam_step)
    second_hat = second_new / (1.0 - beta_two**adam_step)
    update = -learn_rate * (first_hat / (jnp.sqrt(second_hat) + adam_eps) + weight_decay * weight)
    return (update, first_new, second_new)


def local(
    inputs,
    out_grad,
    segments,
    pairs,
    w_qkv,
    w_out,
    w_up,
    w_down,
    up_bias,
    vectors,
    first_qkv,
    first_out,
    first_up,
    first_down,
    first_bias,
    first_vectors,
    second_qkv,
    second_out,
    second_up,
    second_down,
    second_bias,
    second_vectors,
):
    low_type = jnp.bfloat16
    n_ctx = lax.axis_size("ctx")
    field = inputs[0].astype(jnp.float32)
    tokens = field.shape[0]
    block = tokens // 2
    width = field.shape[1]
    seq_len = tokens * n_ctx
    scale = HD ** (-0.5)
    groups = HEADS // group_heads
    slope = 2.0 ** (-8.0 * (jnp.arange(HEADS, dtype=jnp.float32) + 1.0) / HEADS)
    qkv_w, out_w, vec_low = (
        lax.all_gather(w_qkv.astype(low_type), ("ctx", "fsdp"), axis=0, tiled=True),
        lax.all_gather(w_out.astype(low_type), ("ctx", "fsdp"), axis=0, tiled=True),
        lax.all_gather(vectors.astype(low_type), ("ctx", "fsdp"), axis=1, tiled=True),
    )
    vec = vec_low.astype(jnp.float32)
    gain_one, shift_one, gain_two, shift_two = (vec[0], vec[1], vec[2], vec[3])
    bias_query, bias_value, bias_out, bias_down = (vec[4], vec[5], vec[6], vec[7])
    normed_one = layer_norm(field, gain_one, shift_one)
    attn_in = normed_one.astype(low_type)
    mixed = jnp.dot(attn_in, qkv_w, preferred_element_type=jnp.float32)
    query = (mixed[:, :width] + bias_query).astype(low_type)
    keys = mixed[:, width : 2 * width].astype(low_type)
    values = (mixed[:, 2 * width :] + bias_value).astype(low_type)
    pair_ids = pairs[0]
    kv_all, pair_all, seg_all = (
        lax.all_gather(jnp.concatenate([keys, values], 1), "ctx", axis=0, tiled=True),
        lax.all_gather(pair_ids, "ctx", axis=0, tiled=True),
        lax.all_gather(segments[0], "ctx", axis=0, tiled=True),
    )
    pos_query = place(pair_ids, block, n_ctx)
    pos_key = place(pair_all, block, n_ctx)
    seg_query = jnp.take(seg_all, pos_query)
    seg_key = jnp.take(seg_all, pos_key)
    relative = (pos_key[None, :] - pos_query[:, None]).astype(jnp.float32)
    allowed = (seg_query[:, None] == seg_key[None, :]) & (pos_key[None, :] <= pos_query[:, None])
    query_heads = query.reshape(tokens, HEADS, HD)
    key_heads = kv_all[:, :width].reshape(seq_len, HEADS, HD)
    value_heads = kv_all[:, width:].reshape(seq_len, HEADS, HD)

    def scores_of(query_part, key_part, first, offsets, visible):
        slopes = lax.dynamic_slice_in_dim(slope, first, group_heads, 0)
        raw = (
            jnp.einsum("rhe,khe->hrk", query_part, key_part, preferred_element_type=jnp.float32)
            * scale
        )
        raw = raw + slopes[:, None, None] * offsets[None]
        return jnp.where(visible[None], raw, masked)

    def forward_group(index, carry):
        attended, log_total = carry
        first = index * group_heads
        scores = scores_of(
            pick(query_heads, first), pick(key_heads, first), first, relative, allowed
        )
        top = jnp.max(scores, -1, keepdims=True)
        expo = jnp.exp(scores - top)
        total = jnp.sum(expo, -1, keepdims=True)
        chance_low = (expo / total).astype(low_type)
        part_out = jnp.einsum(
            "hrk,khe->rhe", chance_low, pick(value_heads, first), preferred_element_type=jnp.float32
        )
        attended = lax.dynamic_update_slice_in_dim(attended, part_out, first, 1)
        log_total = lax.dynamic_update_slice_in_dim(
            log_total, (top + jnp.log(total))[:, :, 0].T, first, 1
        )
        return (attended, log_total)

    attended, log_total = lax.fori_loop(
        0,
        groups,
        forward_group,
        (jnp.zeros((tokens, HEADS, HD), jnp.float32), jnp.zeros((tokens, HEADS), jnp.float32)),
    )
    attended_low = attended.reshape(tokens, width).astype(low_type)
    resid = field + jnp.dot(attended_low, out_w, preferred_element_type=jnp.float32) + bias_out
    normed_two = layer_norm(resid, gain_two, shift_two)
    mlp_in = normed_two.astype(low_type)
    up_w, down_w, up_low = (
        lax.all_gather(w_up.astype(low_type), ("ctx", "fsdp"), axis=0, tiled=True),
        lax.all_gather(w_down.astype(low_type), ("ctx", "fsdp"), axis=0, tiled=True),
        lax.all_gather(up_bias.astype(low_type), ("ctx", "fsdp"), axis=0, tiled=True),
    )
    pre = jnp.dot(mlp_in, up_w, preferred_element_type=jnp.float32) + up_low.astype(jnp.float32)
    hidden = gelu_exact(pre).astype(low_type)
    result = resid + jnp.dot(hidden, down_w, preferred_element_type=jnp.float32) + bias_down
    cotangent_low = out_grad[0]
    cotangent = cotangent_low.astype(jnp.float32)
    up_back, down_back = (
        lax.all_gather(w_up.astype(low_type), ("ctx", "fsdp"), axis=0, tiled=True),
        lax.all_gather(w_down.astype(low_type), ("ctx", "fsdp"), axis=0, tiled=True),
    )
    grad_down_term = contract(hidden, cotangent_low, 0, 0)
    grad_bias_down = jnp.sum(cotangent, 0)
    grad_hidden = contract(cotangent_low, down_back, 1, 1)
    gelu_back = jax.vjp(gelu_exact, pre)[1]
    grad_pre = gelu_back(grad_hidden)[0].astype(low_type)
    grad_up_bias = jnp.sum(grad_pre.astype(jnp.float32), 0)
    grad_up_term = contract(mlp_in, grad_pre, 0, 0)
    grad_normed_two = contract(grad_pre, up_back, 1, 1)
    norm_two_back = jax.vjp(layer_norm, resid, gain_two, shift_two)[1]
    grad_resid_norm, grad_gain_two, grad_shift_two = norm_two_back(grad_normed_two)
    grad_resid = cotangent + grad_resid_norm
    grad_up_own, grad_down_own, grad_bias_own = (
        lax.psum_scatter(grad_up_term, ("ctx", "fsdp"), scatter_dimension=0, tiled=True),
        lax.psum_scatter(grad_down_term, ("ctx", "fsdp"), scatter_dimension=0, tiled=True),
        lax.psum_scatter(grad_up_bias, ("ctx", "fsdp"), scatter_dimension=0, tiled=True),
    )
    qkv_back, out_back = (
        lax.all_gather(w_qkv.astype(low_type), ("ctx", "fsdp"), axis=0, tiled=True),
        lax.all_gather(w_out.astype(low_type), ("ctx", "fsdp"), axis=0, tiled=True),
    )
    grad_bias_out = jnp.sum(grad_resid, 0)
    resid_low = grad_resid.astype(low_type)
    grad_out_term = contract(attended_low, resid_low, 0, 0)
    back_low = contract(resid_low, out_back, 1, 1).astype(low_type)
    back_heads = back_low.reshape(tokens, HEADS, HD)

    def backward_group(index, carry):
        grad_query, grad_key, grad_value = carry
        first = index * group_heads
        query_part = pick(query_heads, first)
        key_part = pick(key_heads, first)
        value_part = pick(value_heads, first)
        back_part = pick(back_heads, first)
        scores = scores_of(query_part, key_part, first, relative, allowed)
        logsum = lax.dynamic_slice_in_dim(log_total, first, group_heads, 1).T
        chance = jnp.exp(scores - logsum[:, :, None])
        pushed = jnp.einsum(
            "rhe,khe->hrk", back_part, value_part, preferred_element_type=jnp.float32
        )
        centre = jnp.sum(chance * pushed, -1, keepdims=True)
        dscore = (chance * (pushed - centre)).astype(low_type)
        chance_low = chance.astype(low_type)
        part_query = (
            jnp.einsum("hrk,khe->rhe", dscore, key_part, preferred_element_type=jnp.float32) * scale
        )
        part_key = (
            jnp.einsum("hrk,rhe->khe", dscore, query_part, preferred_element_type=jnp.float32)
            * scale
        )
        part_value = jnp.einsum(
            "hrk,rhe->khe", chance_low, back_part, preferred_element_type=jnp.float32
        )
        grad_query = lax.dynamic_update_slice_in_dim(grad_query, part_query, first, 1)
        grad_key = lax.dynamic_update_slice_in_dim(grad_key, part_key, first, 1)
        grad_value = lax.dynamic_update_slice_in_dim(grad_value, part_value, first, 1)
        return (grad_query, grad_key, grad_value)

    zero_keys = jnp.zeros((seq_len, HEADS, HD), jnp.float32)
    grad_query, grad_key, grad_value = lax.fori_loop(
        0,
        groups,
        backward_group,
        (jnp.zeros((tokens, HEADS, HD), jnp.float32), zero_keys, zero_keys),
    )
    own_key, own_value = (
        lax.psum_scatter(
            grad_key.reshape(seq_len, width).astype(jnp.bfloat16),
            "ctx",
            scatter_dimension=0,
            tiled=True,
        ).astype(jnp.float32),
        lax.psum_scatter(
            grad_value.reshape(seq_len, width).astype(jnp.bfloat16),
            "ctx",
            scatter_dimension=0,
            tiled=True,
        ).astype(jnp.float32),
    )
    grad_query_low = grad_query.reshape(tokens, width).astype(low_type)
    grad_key_low = own_key.astype(low_type)
    grad_value_low = own_value.astype(low_type)
    grad_mixed = jnp.concatenate([grad_query_low, grad_key_low, grad_value_low], 1)
    grad_bias_query = jnp.sum(grad_query_low.astype(jnp.float32), 0)
    grad_bias_value = jnp.sum(grad_value_low.astype(jnp.float32), 0)
    grad_qkv_term = contract(attn_in, grad_mixed, 0, 0)
    grad_normed_one = contract(grad_mixed, qkv_back, 1, 1)
    norm_one_back = jax.vjp(layer_norm, field, gain_one, shift_one)[1]
    grad_field_norm, grad_gain_one, grad_shift_one = norm_one_back(grad_normed_one)
    in_grad = grad_resid + grad_field_norm
    grad_vec_term = jnp.stack(
        [
            grad_gain_one,
            grad_shift_one,
            grad_gain_two,
            grad_shift_two,
            grad_bias_query,
            grad_bias_value,
            grad_bias_out,
            grad_bias_down,
        ],
        0,
    )
    grad_qkv_own, grad_out_own, grad_vec_own = (
        lax.psum_scatter(grad_qkv_term, ("ctx", "fsdp"), scatter_dimension=0, tiled=True),
        lax.psum_scatter(grad_out_term, ("ctx", "fsdp"), scatter_dimension=0, tiled=True),
        lax.psum_scatter(grad_vec_term, ("ctx", "fsdp"), scatter_dimension=1, tiled=True),
    )
    grads = (grad_qkv_own, grad_out_own, grad_up_own, grad_down_own, grad_bias_own, grad_vec_own)
    local_squares = sum([jnp.sum(item * item) for item in grads])
    grad_norm = jnp.sqrt(lax.psum(local_squares, ("ctx", "fsdp")))
    clip = jnp.minimum(1.0, max_norm / (grad_norm + 1e-06))
    masters = (w_qkv, w_out, w_up, w_down, up_bias, vectors)
    firsts = (first_qkv, first_out, first_up, first_down, first_bias, first_vectors)
    seconds = (second_qkv, second_out, second_up, second_down, second_bias, second_vectors)
    results = []
    for weight, grad, first, second in zip(masters, grads, firsts, seconds):
        update, first_new, second_new = adamw(weight, grad, first, second, clip)
        results = results + [grad, update, first_new, second_new]
    return (
        result.astype(low_type)[None],
        in_grad[None],
        grad_norm,
        results[0],
        results[1],
        results[2],
        results[3],
        results[4],
        results[5],
        results[6],
        results[7],
        results[8],
        results[9],
        results[10],
        results[11],
        results[12],
        results[13],
        results[14],
        results[15],
        results[16],
        results[17],
        results[18],
        results[19],
        results[20],
        results[21],
        results[22],
        results[23],
    )


def exchange(v, axis):
    return lax.ppermute(v, axis, [(0, 1), (1, 0)])


def shift(v, axis, n_line, k):
    return lax.ppermute(v, axis, [(i, (i - k) % n_line) for i in range(n_line)])


def swap(v, axes):
    return lax.all_to_all(v, axes, 0, 0, tiled=True)


def gate(*values):
    return lax.optimization_barrier(values)


def after(v, *others):
    return lax.optimization_barrier((v,) + others)[0]


def order_two(own, other, axis, dim):
    first = lax.axis_index(axis) == 0
    return jnp.stack([jnp.where(first, own, other), jnp.where(first, other, own)], dim)


def split_two(part, axis, dim):
    me = lax.axis_index(axis)
    keep = lax.dynamic_index_in_dim(part, me, dim, keepdims=False)
    return keep, lax.dynamic_index_in_dim(part, 1 - me, dim, keepdims=False)


def add_low(keep, got):
    return (keep.astype(jnp.float32) + got.astype(jnp.float32)).astype(jnp.bfloat16)


def line_gives(part, axis, n_line):
    me = lax.axis_index(axis)
    blocks = [lax.dynamic_index_in_dim(part, (me + k) % n_line, 0, keepdims=False) for k in range(n_line)]
    return blocks[0], [shift(blocks[k], axis, n_line, -k) for k in range(1, n_line)]


def line_order(parts, axis):
    n_line = len(parts)
    first = (n_line - lax.axis_index(axis)) % n_line
    return lax.dynamic_slice_in_dim(jnp.concatenate([jnp.stack(parts)] * 2, 0), first, n_line, 0)


def lanes_of(head, shape):
    return lax.broadcasted_iota(jnp.int32, shape, 1) // HD == head


def head_parts(query, keys, slope, head):
    seq = keys.shape[0]
    lane = lax.broadcasted_iota(jnp.int32, keys.shape, 1)
    own = lane // HD == head
    spot = lane - (1 - head) * HD
    bias = lax.broadcasted_iota(jnp.int32, (seq, 1), 0).astype(jnp.float32) * (slope * HD**0.5)
    high = bias.astype(jnp.bfloat16)
    rest = bias - high.astype(jnp.float32)
    middle = rest.astype(jnp.bfloat16)
    small = (rest - middle.astype(jnp.float32)).astype(jnp.bfloat16)
    zero = jnp.zeros_like(keys)
    extra = jnp.where(spot == 0, high, jnp.where(spot == 1, middle, jnp.where(spot == 2, small, zero)))
    ones = jnp.where((spot >= 0) & (spot <= 2), jnp.ones_like(keys), zero)
    return jnp.where(own, query, ones), jnp.where(own, keys, extra)


def visible(start, tile, at, size):
    key = lax.broadcasted_iota(jnp.int32, (size, tile), 0)
    seen = key >= start
    return seen & (key <= lax.broadcasted_iota(jnp.int32, (size, tile), 1) + at)


def forward_kernel(n_refs, meta, slopes, *refs):
    pieces = refs[n_refs : n_refs + 4]
    start_ref = refs[n_refs + 4]
    att_ref, att_t, qkv_ref, lse_ref, normed, x_ref, w_ref, vec_ref, extra = refs[n_refs + 5 :]
    n_line = (n_refs - 3) // 2 + 1
    own, pair, pair_line = refs[0], refs[1], refs[2]
    line, rest = refs[3 : 2 + n_line], refs[2 + n_line : 1 + 2 * n_line]
    n_blocks = 2 * n_line
    cut = line[0].shape[1]

    def block_part(b, span):
        z, other = b % n_line, b // n_line
        if z == 0:
            return (pair if other else own)[span, :]
        first = pair_line[z - 1, span, :] if other else line[z - 1][span, :]
        return jnp.concatenate([first, rest[z - 1][other, span, :]], 1)

    f32, low = jnp.float32, jnp.bfloat16
    n_ctx, rows, _ = pieces[0].shape
    tokens, width = own.shape
    half = tokens // 2
    seq = tokens * n_blocks
    cols = qkv_ref.shape[1] // 3
    spans = 2 * n_blocks
    for c in range(n_ctx):
        for p in range(4):
            piece = pieces[p][c]
            to = pl.ds(pl.multiple_of(c * 4 * rows + meta[2 * spans + p] * rows, rows), rows)
            w_ref[to, :] = piece[:, : 3 * cols]
            extra[to, :] = piece[:, 3 * cols :]
    pick_rows = (
        lax.broadcasted_iota(jnp.int32, (8, 128), 0) == lax.broadcasted_iota(jnp.int32, (8, 128), 1)
    ).astype(low)
    vec = contract(pick_rows, extra[...], 1, 1)
    vec_ref[...] = vec
    gain, move = vec[0:1], vec[1:2]
    for j in range(spans):
        part = block_part(j // 2, slice((j % 2) * half, (j % 2 + 1) * half))
        to = pl.ds(pl.multiple_of(meta[j] * half, half), half)
        x_ref[to, :] = part
        normed[to, :] = layer_norm(part.astype(f32), gain, move).astype(low)
    at = pl.ds(pl.multiple_of(meta[2 * spans + 4] * cols, cols), cols)
    bias_q, bias_v = vec_ref[4:5, at], vec_ref[5:6, at]
    tile = min(256, seq)
    for t in range(seq // tile):
        span = pl.ds(t * tile, tile)
        mixed = jnp.dot(normed[span, :], w_ref[...], preferred_element_type=f32)
        qkv_ref[span, :cols] = (mixed[:, :cols] + bias_q).astype(low)
        qkv_ref[span, cols : 2 * cols] = mixed[:, cols : 2 * cols].astype(low)
        qkv_ref[span, 2 * cols :] = (mixed[:, 2 * cols :] + bias_v).astype(low)
    factor = HD**-0.5 * 1.4426950408889634
    query, keys, values = qkv_ref[:, :cols], qkv_ref[:, cols : 2 * cols], qkv_ref[:, 2 * cols :]
    lse_ref[...] = jnp.zeros_like(lse_ref)
    for h in range(cols // HD):
        q_h, k_h = head_parts(query, keys, slopes[h], h)
        v_h = jnp.where(lanes_of(h, values.shape), values, jnp.zeros_like(values))
        for t in range(seq // tile):
            size = (t + 1) * tile
            span = slice(t * tile, (t + 1) * tile)
            score = contract(k_h[:size], q_h[span], 1, 1) * factor
            score = jnp.where(visible(start_ref[:, span], tile, t * tile, size), score, masked)
            top = jnp.max(score, 0, keepdims=True)
            expo = jnp.exp2(score - top)
            total = jnp.sum(expo, 0, keepdims=True)
            lse_ref[h : h + 1, span] = top + jnp.log2(total)
            part = contract(v_h[:size], expo.astype(low), 0, 0) / total
            att_t[:, span] = part if h == 0 else att_t[:, span] + part
    for t in range(seq // tile):
        span = slice(t * tile, (t + 1) * tile)
        x_tile = att_t[:, span].T.astype(low)
        for u in range(tile // half):
            b = t * (tile // half) + u
            to = meta[spans + b]
            att_ref[pl.ds(pl.multiple_of(to * half, half), half), :] = x_tile[u * half : (u + 1) * half]


def pack_kernel(pairs, w_qkv, vectors, segments, up_bias, w_up, w_down, w_out, first_ref, up_ref, down_ref, out_ref):
    low, f32 = jnp.bfloat16, jnp.float32
    n_ctx, rows, wide = first_ref.shape
    cols = (wide - 128) // 3
    width = n_ctx * cols
    row = lax.broadcasted_iota(jnp.int32, (rows, 128), 0)
    lane = lax.broadcasted_iota(jnp.int32, (rows, 128), 1)
    one_hot = lax.broadcasted_iota(jnp.int32, (8, 128), 0) == lax.broadcasted_iota(jnp.int32, (8, 128), 1)
    columns = contract(vectors[...].astype(low), one_hot.astype(low), 0, 0)
    seg, bias = segments[...].astype(f32), up_bias[...]
    lines = [pltpu.roll(seg, 64, 1), seg, pltpu.roll(bias, 64, 1), bias]
    extra = jnp.where(lane < 8, columns, 0.0)
    for k in range(4):
        extra = jnp.where((row == k) & (lane >= 64), lines[k], extra)
    extra = jnp.where((row == 4) & (lane >= 64), pairs[0, 0].astype(f32), extra).astype(low)
    for c in range(n_ctx):
        for k in range(3):
            first_ref[c, :, k * cols : (k + 1) * cols] = w_qkv[:, k * width + c * cols : k * width + (c + 1) * cols].astype(low)
        first_ref[c, :, 3 * cols :] = extra
    n_plane, _, ff = up_ref.shape
    own = ff // (n_ctx // 2)
    for r in range(n_plane):
        for k in range(n_ctx // 2):
            up_ref[r, :, k * own : (k + 1) * own] = w_up[:, (k * n_plane + r) * own : (k * n_plane + r + 1) * own].astype(low)
    for k in range(down_ref.shape[0]):
        down_ref[k] = w_down[:, k * ff : (k + 1) * ff].astype(low)
    wide_out = out_ref.shape[1]
    for k in range(out_ref.shape[0] // rows):
        out_ref[k * rows : (k + 1) * rows, :] = w_out[:, k * wide_out : (k + 1) * wide_out].astype(low)


def project_kernel(table, att, own_ref, x_ref, c_ref, cx_ref, field, vec, resid_ref, mlp_ref, w_ref):
    low, f32 = jnp.bfloat16, jnp.float32
    n_ctx, tokens, cols = att.shape
    n_line = own_ref.shape[1]
    rows = w_ref.shape[0] // (8 * n_line)
    wide = own_ref.shape[3]
    at = 4 * n_ctx + 5
    zi, yi, xi, ci = (table[at + k] for k in range(4))
    for q, ref in enumerate((own_ref, x_ref, c_ref, cx_ref)):
        for p in range(2):
            for k in range(n_line):
                z = lax.rem(zi + k, n_line)
                y = lax.rem(yi + p, 2)
                x = lax.rem(xi + q % 2, 2)
                to = ((z * 2 + y) * 4 + x * 2 + lax.rem(ci + q // 2, 2)) * rows
                for part in range(tokens // rows):
                    spot = (pl.ds(pl.multiple_of(to, rows), rows), slice(part * wide, (part + 1) * wide))
                    w_ref[spot] = ref[p, k, part * rows : (part + 1) * rows, :]
    heads = jnp.concatenate([att[c] for c in range(n_ctx)], 1)
    moved = jnp.dot(heads, w_ref[...], preferred_element_type=f32)
    resid = field[...].astype(f32) + moved + vec[6:7]
    resid_ref[...] = resid
    mlp_ref[...] = layer_norm(resid, vec[2:3], vec[3:4]).astype(low)


def down_of(ff_all, down):
    n_line, own = ff_all.shape[0], down.shape[0] // ff_all.shape[0]
    ff = down.shape[0]
    up_rows = ff_all.shape[1] - down.shape[1] * own // ff
    for k in range(n_line):
        for h in range(down.shape[1] // ff):
            down[k * own : (k + 1) * own, h * ff : (h + 1) * ff] = ff_all[k, up_rows + h * own : up_rows + (h + 1) * own, :]


def feed_kernel(*refs):
    low, f32 = jnp.bfloat16, jnp.float32
    m_own, m_y, m_x, m_d0, m_d1, m_c, m_cyx, m_cd = refs[:8]
    cots, ff_all, bias = refs[8:12], refs[12], refs[13]
    keep_ref, give_ref, hidden_ref, pre_ref, mlp_ref, down, up = refs[14:]
    tokens, width = m_own.shape
    half = tokens // 2
    ff = hidden_ref.shape[1]
    n_line = ff_all.shape[0]
    up_rows = width // n_line
    for k in range(n_line):
        up[k * up_rows : (k + 1) * up_rows, :] = ff_all[k, :up_rows, :]
    down_of(ff_all, down)
    blocks = (m_own[...], m_y[...], m_x[...], None, m_c[...], m_cyx[0], m_cyx[1])
    for b, block in enumerate(blocks):
        if block is not None:
            mlp_ref[b * tokens : (b + 1) * tokens, :] = block
    mlp_ref[3 * tokens : 3 * tokens + half, :] = m_d0[...]
    mlp_ref[3 * tokens + half : 4 * tokens, :] = m_d1[...]
    mlp_ref[7 * tokens : 7 * tokens + half, :] = m_cd[0]
    mlp_ref[7 * tokens + half : 8 * tokens, :] = m_cd[1]
    for t in range(4):
        span = slice(2 * t * tokens, 2 * (t + 1) * tokens)
        pre = jnp.dot(mlp_ref[span, :], up[...], preferred_element_type=f32) + bias[...]
        cdf = 0.5 * (1.0 + lax.erf(pre * 0.7071067811865476))
        pdf = jnp.exp(-0.5 * pre * pre) * 0.3989422804014327
        hidden_ref[span, :] = (pre * cdf).astype(low)
        cot = cots[t][...].reshape(2 * tokens, width)
        grad = (contract(cot, down[...], 1, 1) * (cdf + pre * pdf)).astype(low)
        pre_ref[span, :] = grad
        part = contract(grad, up[...], 1, 1).astype(low).reshape(2, tokens, width)
        to = keep_ref if t < 2 else give_ref
        to[2 * (t % 2) : 2 * (t % 2) + 2] = part


def feed_grad_kernel(mlp_ref, pre_ref, hidden_ref, cot_0, cot_1, cot_2, cot_3, terms_ref):
    low, f32 = jnp.bfloat16, jnp.float32
    seq, width = mlp_ref.shape
    ff = pre_ref.shape[1]
    n_line = terms_ref.shape[0]
    own, up_rows = ff // n_line, width // n_line
    n_half = width // ff
    for k in range(n_line):
        up = contract(mlp_ref[:, k * up_rows : (k + 1) * up_rows], pre_ref[...], 0, 0)
        terms_ref[k, :up_rows, :] = up.astype(low)
        for h in range(n_half):
            part = slice(k * own, (k + 1) * own)
            cut = slice(h * ff, (h + 1) * ff)
            cot = [ref[:, :, cut].reshape(seq // 4, ff) for ref in (cot_0, cot_1, cot_2, cot_3)]
            total = contract(hidden_ref[:, part], jnp.concatenate(cot, 0), 0, 0)
            terms_ref[k, up_rows + h * own : up_rows + (h + 1) * own, :] = total.astype(low)
    sums = jnp.sum(pre_ref[...].astype(f32), 0, keepdims=True)
    pad = terms_ref.shape[1] - up_rows - n_half * own
    for k in range(n_line):
        line = jnp.concatenate([sums[:, k * own : (k + 1) * own], jnp.zeros((1, ff - own), f32)], 1)
        terms_ref[k, up_rows + n_half * own :, :] = jnp.broadcast_to(line, (pad, ff)).astype(low)


def result_kernel(hidden_ref, ff_all, keep_ref, give_ref, down):
    down_of(ff_all, down)
    tokens = keep_ref.shape[1]
    for t in range(4):
        span = slice(2 * t * tokens, 2 * (t + 1) * tokens)
        part = jnp.dot(hidden_ref[span, :], down[...], preferred_element_type=jnp.float32)
        to = keep_ref if t < 2 else give_ref
        to[2 * (t % 2) : 2 * (t % 2) + 2] = part.astype(jnp.bfloat16).reshape(2, tokens, down.shape[1])


def norm_back_kernel(
    table, own, got_x, got_y, resid_ref, cot_ref, vec, w_ref, att, grad_ref, back_ref, sums_ref, keep_ref, give_ref, terms
):
    low, f32 = jnp.bfloat16, jnp.float32
    grad = own[...].astype(f32) + got_x[...].astype(f32) + got_y[...].astype(f32)
    resid = resid_ref[...]
    center = resid - jnp.mean(resid, -1, keepdims=True)
    sharp = lax.rsqrt(jnp.mean(center * center, -1, keepdims=True) + norm_eps)
    unit = center * sharp
    scaled = grad * vec[2:3]
    inner = scaled - jnp.mean(scaled, -1, keepdims=True) - unit * jnp.mean(scaled * unit, -1, keepdims=True)
    cot = cot_ref[...].astype(f32)
    total = cot + inner * sharp
    grad_ref[...] = total
    rounded = total.astype(low)
    back = contract(rounded, w_ref[...], 1, 1).astype(low)
    n_ctx, _, cols = back_ref.shape
    for c in range(n_ctx):
        back_ref[c] = back[:, c * cols : (c + 1) * cols]
    row = lax.broadcasted_iota(jnp.int32, sums_ref.shape, 0)
    sums = jnp.where(row == 2, jnp.sum(grad * unit, 0, keepdims=True), 0.0)
    sums = jnp.where(row == 3, jnp.sum(grad, 0, keepdims=True), sums)
    sums = jnp.where(row == 6, jnp.sum(total, 0, keepdims=True), sums)
    sums_ref[...] = jnp.where(row == 7, jnp.sum(cot, 0, keepdims=True), sums)
    for c in range(n_ctx):
        terms[c * cols : (c + 1) * cols, :] = contract(att[c], rounded, 0, 0).astype(low)
    n_line, rows = keep_ref.shape[2:4]
    at = 4 * n_ctx + 5
    for which, ref in enumerate((keep_ref, give_ref)):
        for q in range(4 * n_line):
            x, y, z = q // (2 * n_line), q // n_line % 2, q % n_line
            chip = (lax.rem(table[at] + z, n_line) * 2 + lax.rem(table[at + 1] + y, 2)) * 4
            to = (chip + lax.rem(table[at + 2] + x, 2) * 2 + lax.rem(table[at + 3] + which, 2)) * rows
            ref[x, y, z] = terms[pl.ds(pl.multiple_of(to, rows), rows), :]


def backward_kernel(
    table, slopes, back_ref, qkv_ref, att_t, lse_ref, start_ref, normed, w_ref, x_ref, sums_ref,
    keep_ref, give_ref, keep_a, give_a, keep_b, give_b, mixed_ref, back, d_key, d_value, moved, made,
):
    f32, low = jnp.float32, jnp.bfloat16
    seq, cols = back_ref.shape
    n_ctx, rows = keep_ref.shape[1:3]
    width = w_ref.shape[0]
    spans = 2 * n_ctx
    half = seq // spans
    for b in range(spans):
        back[b * half : (b + 1) * half, :] = back_ref[pl.ds(pl.multiple_of(table[spans + b] * half, half), half), :]
    factor = HD**-0.5 * 1.4426950408889634
    query, keys, values = qkv_ref[:, :cols], qkv_ref[:, cols : 2 * cols], qkv_ref[:, 2 * cols :]
    grads = back[...]
    product = att_t[...] * grads.astype(f32).T
    tile = min(256, seq)
    d_query = [None] * (seq // tile)
    for h in range(cols // HD):
        q_h, k_h = head_parts(query, keys, slopes[h], h)
        own = lanes_of(h, values.shape)
        zero = jnp.zeros_like(values)
        v_h, g_h = jnp.where(own, values, zero), jnp.where(own, grads, zero)
        qq_h, kk_h = jnp.where(own, query, zero), jnp.where(own, keys, zero)
        delta = jnp.sum(product[h * HD : (h + 1) * HD], 0, keepdims=True)
        for t in reversed(range(seq // tile)):
            size = (t + 1) * tile
            span = slice(t * tile, (t + 1) * tile)
            score = contract(k_h[:size], q_h[span], 1, 1) * factor
            score = jnp.where(visible(start_ref[:, span], tile, t * tile, size), score, masked)
            chance = jnp.exp2(score - lse_ref[h : h + 1, span])
            pushed = contract(v_h[:size], g_h[span], 1, 1)
            dscore = (chance * (pushed - delta[:, span])).astype(low)
            part_v = jnp.dot(chance.astype(low), g_h[span], preferred_element_type=f32)
            part_k = jnp.dot(dscore, qq_h[span], preferred_element_type=f32)
            if h == 0 and t == seq // tile - 1:
                d_value[...] = part_v
                d_key[...] = part_k
            else:
                d_value[:size, :] += part_v
                d_key[:size, :] += part_k
            part_q = contract(kk_h[:size], dscore, 0, 0)
            d_query[t] = part_q if h == 0 else d_query[t] + part_q
    scale = HD**-0.5
    for t in range(seq // tile):
        mixed_ref[t * tile : (t + 1) * tile, :cols] = (d_query[t] * scale).T.astype(low)
    mixed_ref[:, cols : 2 * cols] = (d_key[...] * scale).astype(low)
    mixed_ref[:, 2 * cols :] = d_value[...].astype(low)
    mixed = mixed_ref[...]
    mixed_sums = jnp.sum(mixed.astype(f32), 0, keepdims=True)
    gain_sum = jnp.zeros((1, width), f32)
    shift_sum = jnp.zeros((1, width), f32)
    for t in range(seq // tile):
        grad = contract(mixed_ref[t * tile : (t + 1) * tile, :], w_ref[...], 1, 1)
        field = x_ref[t * tile : (t + 1) * tile, :].astype(f32)
        center = field - jnp.mean(field, -1, keepdims=True)
        unit = center * lax.rsqrt(jnp.mean(center * center, -1, keepdims=True) + norm_eps)
        gain_sum = gain_sum + jnp.sum(grad * unit, 0, keepdims=True)
        shift_sum = shift_sum + jnp.sum(grad, 0, keepdims=True)
        moved[t * tile : (t + 1) * tile, :] = grad.astype(low)
    n_line = spans // 4
    cut = keep_a.shape[2]
    for y, (ref_a, ref_b) in enumerate(((keep_a, keep_b), (give_a, give_b))):
        for z in range(n_line):
            for u in range(2):
                part = pl.ds(pl.multiple_of(table[(y * n_line + z) * 2 + u] * half, half), half)
                to = slice(u * half, (u + 1) * half)
                ref_a[z, to, :] = moved[part, :cut]
                ref_b[z, to, :] = moved[part, cut:]
    row = lax.broadcasted_iota(jnp.int32, (8, width), 0)
    sums = jnp.where(row == 0, gain_sum, jnp.where(row == 1, shift_sum, sums_ref[...]))
    here = table[2 * spans + 4]
    small = lax.broadcasted_iota(jnp.int32, (8, cols), 0)
    bias = jnp.where(small == 4, mixed_sums[:, :cols], jnp.where(small == 5, mixed_sums[:, 2 * cols :], 0.0))
    terms = contract(mixed, normed[...], 0, 0)
    blank = jnp.zeros((rows - 8, cols), f32)
    for c in range(n_ctx):
        part = terms[:, c * 4 * rows : (c + 1) * 4 * rows].T.astype(low)
        block = sums[:, c * cols : (c + 1) * cols] + jnp.where(here == c, bias, 0.0)
        block = jnp.concatenate([block, blank], 0).astype(low)
        for f in range(4):
            made[(c * 4 + f) * rows : (c * 4 + f + 1) * rows, : 3 * cols] = part[f * rows : (f + 1) * rows]
            made[(c * 4 + f) * rows : (c * 4 + f + 1) * rows, 3 * cols :] = block
    at = 2 * spans + 5
    for which, ref in enumerate((keep_ref, give_ref)):
        for x in range(2):
            f = lax.rem(table[at + 2] + x, 2) * 2 + lax.rem(table[at + 3] + which, 2)
            for c in range(n_ctx):
                ref[x, c] = made[pl.ds(pl.multiple_of((c * 4 + f) * rows, rows), rows), :]


def square_kernel(table, qkv_ref, ff_ref, own_out, *refs):
    f32 = jnp.float32
    others, (square_ref, out_ref, vec_ref) = refs[:-3], refs[-3:]
    n_ctx, rows, wide = qkv_ref.shape
    cols = wide // 4
    at = 4 * n_ctx + 5
    out = own_out[...].astype(f32)
    for other in others:
        out = out + other[...].astype(f32)
    out_ref[...] = out
    small = jnp.sum(qkv_ref[:, :, 3 * cols :].astype(f32), 0)[:8]
    mine = table[at + 2] * 2 + table[at + 3]
    picked = jnp.zeros((8, rows), f32)
    for f in range(4):
        picked = picked + jnp.where(mine == f, small[:, f * rows : (f + 1) * rows], 0.0)
    vec_ref[...] = picked
    n_ff = ff_ref.shape[0] - 16
    bias = ff_ref[n_ff:, : 4 * rows].astype(f32)[0:1]
    squared = jnp.sum(jnp.square(bias), keepdims=True) + jnp.sum(jnp.square(picked), keepdims=True)
    squared = squared + jnp.sum(jnp.sum(jnp.square(ff_ref[:n_ff, :].astype(f32)), 0, keepdims=True), keepdims=True)
    squared = squared + jnp.sum(jnp.sum(jnp.square(out), 0, keepdims=True), keepdims=True)
    qkv = jnp.sum(jnp.square(qkv_ref[:, :, : 3 * cols].astype(f32)), 0)
    squared = squared + jnp.sum(jnp.sum(qkv, 0, keepdims=True), keepdims=True)
    square_ref[...] = jnp.broadcast_to(squared, square_ref.shape)


def clip_of(squares):
    norm = jnp.sqrt(jnp.sum(jnp.sum(squares[...], 0, keepdims=True)[:, 0:1], keepdims=True))
    return norm, jnp.minimum(1.0, max_norm / (norm + 1e-06))


def adam_put(refs, spot, grad, clip):
    weight, first, second = refs[:3]
    new = adamw(weight[spot], grad, first[spot], second[spot], clip)
    for ref, value in zip(refs[3:], (grad,) + new):
        ref[spot] = value


def adam_kernel(*refs):
    f32 = jnp.float32
    squares, qkv_ref, out_ref, ff_ref, vec_ref = refs[:5]
    items = [[refs[5 + 5 * m + n] for m in range(3)] + list(refs[21 + 4 * n : 25 + 4 * n]) for n in range(5)]
    norm, clip = clip_of(squares)
    refs[20][...] = norm
    n_ctx, rows, wide = qkv_ref.shape
    cols = wide // 4
    width = n_ctx * cols
    ff = ff_ref.shape[1]
    own = 4 * rows
    n_ff = 8 * rows
    whole = (slice(None), slice(None))
    for c in range(n_ctx):
        for k in range(3):
            spot = (slice(None), slice(k * width + c * cols, k * width + (c + 1) * cols))
            adam_put(items[0], spot, qkv_ref[c, :, k * cols : (k + 1) * cols].astype(f32), clip)
    adam_put(items[1], whole, out_ref[...], clip)
    for h in range(width // ff):
        spot = (slice(None), slice(h * ff, (h + 1) * ff))
        adam_put(items[2], spot, ff_ref[n_ff + h * own : n_ff + (h + 1) * own, :].astype(f32), clip)
    n_down = n_ff + width // ff * own
    adam_put(items[3], whole, ff_ref[n_down:, :own].astype(f32)[0:1], clip)
    adam_put(items[4], whole, vec_ref[...], clip)


def adam_up_kernel(squares, up_ref, *refs):
    _, clip = clip_of(squares)
    n_plane, rows, ff = up_ref.shape
    own = 4 * rows
    for r in range(n_plane):
        for k in range(ff // own):
            spot = (slice(None), slice((k * n_plane + r) * own, (k * n_plane + r + 1) * own))
            adam_put(refs, spot, up_ref[r, :, k * own : (k + 1) * own].astype(jnp.float32), clip)


in_smem = pl.BlockSpec(memory_space=pltpu.SMEM)
in_vmem = pl.BlockSpec(memory_space=pltpu.VMEM)


def call(kernel, n_scalar, args, shapes, scratch=(), cost=1, limit=48):
    return pl.pallas_call(
        kernel,
        out_shape=[jax.ShapeDtypeStruct(s, d) for s, d in shapes],
        in_specs=[in_smem] * n_scalar + [in_vmem] * (len(args) - n_scalar),
        out_specs=[in_vmem] * len(shapes),
        scratch_shapes=[pltpu.VMEM(s, d) for s, d in scratch],
        compiler_params=pltpu.CompilerParams(vmem_limit_bytes=limit * 1024 * 1024),
        cost_estimate=pl.CostEstimate(flops=cost, bytes_accessed=cost, transcendentals=0),
    )(*args)


def attend_forward(table, slopes, blocks, pieces, start, cols):
    tokens, width = blocks[0].shape
    seq = tokens * (len(blocks) - 1)
    f32, low = jnp.float32, jnp.bfloat16
    shapes = [
        ((seq, cols), low), ((cols, seq), f32), ((seq, 3 * cols), low), ((8, seq), f32),
        ((seq, width), low), ((seq, width), low), ((width, 3 * cols), low), ((8, width), f32),
    ]
    args = [table, slopes] + list(blocks) + list(pieces) + [start]
    return call(functools.partial(forward_kernel, len(blocks)), 2, args, shapes, [((width, 128), low)], 9000000000, 60)


def local_split(
    inputs, out_grad, segments, pairs,
    w_qkv, w_out, w_up, w_down, up_bias, vectors,
    first_qkv, first_out, first_up, first_down, first_bias, first_vectors,
    second_qkv, second_out, second_up, second_down, second_bias, second_vectors,
):
    low = jnp.bfloat16
    f32 = jnp.float32
    nz = lax.axis_size("z")
    n_ctx = 2 * nz
    every = ("z", "y", "x", "c")
    ctx = ("z", "y")
    plane = ("y", "x", "c")
    zi, yi, xi, ci = (lax.axis_index(a) for a in every)
    ctx_i = zi * 2 + yi
    tokens, width = inputs.shape[1:]
    half = tokens // 2
    seq_len = tokens * n_ctx
    heads_own = HEADS // n_ctx
    cols = heads_own * HD
    rows = w_qkv.shape[0]
    ff_own = w_down.shape[0]
    ff = nz * ff_own
    n_half = width // ff
    field_low = inputs[0]
    field = field_low.astype(f32)
    cot_low = out_grad[0]

    cut = width - width // 4
    field_cut = field_low[:, :cut]
    line = [shift(field_cut, "z", nz, k) for k in range(1, nz)]
    own_two = exchange(jnp.stack([field_low, cot_low]), "y")
    shapes = [((n_ctx, rows, 3 * cols + 128), low), ((8, rows, ff), low), ((n_half, ff_own, ff), low), ((tokens, width // 4), low)]
    packed = [pairs, w_qkv, vectors, segments, up_bias.reshape(1, ff_own), w_up, w_down, w_out]
    first_send, up_send, down_part, out_low = call(pack_kernel, 1, packed, shapes, limit=60)
    first_got = swap(first_send, ctx)
    up_part = swap(after(up_send, first_got), plane).reshape(8 * rows, ff)
    ff_send = jnp.concatenate([up_part, down_part.reshape(n_half * ff_own, ff)], 0)
    ff_send, first_got, own_two, out_low, *line = gate(ff_send, first_got, own_two, out_low, *line)
    pair_own, cot_y = own_two[0], own_two[1]

    ff_all = lax.all_gather(ff_send, "z", axis=0)
    pair_line = exchange(jnp.stack(line), "y")
    rest_own = jnp.stack([field_low[:, cut:], pair_own[:, cut:], out_low])
    rest = [shift(rest_own, "z", nz, k) for k in range(1, nz)]
    first_x = exchange(first_got, "x")
    first_c = exchange(first_got, "c")
    first_cx = exchange(first_x, "c")
    cot_two = jnp.stack([cot_low, cot_y])
    cot_x = exchange(cot_two, "x")
    seg_all = first_got[:, 0:2, 3 * cols + 64 :].reshape(seq_len).astype(jnp.int32)
    bias_all = first_got[:, 2:4, 3 * cols + 64 :].reshape(nz, 2, ff_own)
    up_low = lax.dynamic_index_in_dim(bias_all, yi, 1, keepdims=False).reshape(1, ff).astype(f32)
    pair_all = first_got[:, 4, 3 * cols + 64].astype(jnp.int32)
    start = jnp.sum((seg_all[:, None] < seg_all[None, :]).astype(jnp.int32), 0, keepdims=True)
    slot_block = jnp.stack([pair_all, 2 * n_ctx - 1 - pair_all], 1)
    near = [((zi + k) % nz) * 2 + yi for k in range(nz)]
    near = jnp.stack(near + [((zi + k) % nz) * 2 + 1 - yi for k in range(nz)])
    ids = jnp.arange(n_ctx)
    near_block = jnp.sum(jnp.where((near[:, None] == ids[None, :])[:, :, None], slot_block[None], 0), 1)
    spans = jnp.arange(2 * n_ctx)
    block_slot = jnp.sum(jnp.where(slot_block.reshape(1, -1) == spans[:, None], spans[None, :], 0), 1)
    piece_f = jnp.stack([xi * 2 + ci, (1 - xi) * 2 + ci, xi * 2 + 1 - ci, (1 - xi) * 2 + 1 - ci])
    here = jnp.stack([ctx_i, zi, yi, xi, ci])
    table = jnp.concatenate([near_block.reshape(-1), block_slot, piece_f, here]).astype(jnp.int32)
    head_ids = (ctx_i * heads_own + jnp.arange(heads_own)).astype(f32)
    slopes = jnp.exp2(-8.0 * (head_ids + 1.0) / HEADS)
    out_z = jnp.stack([out_low] + [v[2] for v in rest])
    first_x, first_c, first_cx, cot_x, table, start, pair_line, slopes, out_z, *rest = gate(
        first_x, first_c, first_cx, cot_x, table, start, pair_line, slopes, out_z, *rest
    )

    out_y = exchange(out_z, "y")
    cot_c = exchange(cot_two, "c")
    pieces = (first_got, first_x, first_c, first_cx)
    blocks = [field_low, pair_own, pair_line] + line + rest
    attended, att_t, qkv_low, lse, normed_one, seq_rows, qkv_w, vec = attend_forward(
        table, slopes, blocks, pieces, start, cols
    )
    attended, out_y, cot_c = gate(attended.reshape(n_ctx, tokens, cols), out_y, cot_c)

    attended_low = swap(attended, ctx)
    out_zy = jnp.stack([out_z, out_y])
    out_x = exchange(out_zy, "x")
    out_c_two = exchange(out_zy, "c")
    cot_cx = exchange(cot_x, "c")
    attended_low, out_x, out_c_two, cot_cx = gate(attended_low, out_x, out_c_two, cot_cx)
    cots = [cot_two, cot_x, cot_c, cot_cx]
    shapes = [((tokens, width), f32), ((tokens, width), low), ((width, width), low)]
    parts = [table, attended_low, out_zy, out_x, out_c_two, exchange(out_x, "c"), field_low, vec]
    resid, mlp_low, out_w = call(project_kernel, 1, parts, shapes)

    mlp_y = exchange(mlp_low, "y")
    mlp_x = exchange(mlp_low, "x")
    mlp_c = exchange(mlp_low, "c")
    mlp_y, mlp_x, mlp_c = gate(mlp_y, mlp_x, mlp_c)
    mlp_d0 = exchange(mlp_x[:half], "y")
    mlp_d1 = exchange(mlp_y[half:], "x")
    mlp_cyx = exchange(jnp.stack([mlp_y, mlp_x]), "c")
    mlp_cd = exchange(jnp.stack([mlp_d0, mlp_d1]), "c")
    four = ((4, tokens, width), low)
    shapes = [four, four, ((8 * tokens, ff), low), ((8 * tokens, ff), low), ((8 * tokens, width), low)]
    scratch = [((ff, width), low), ((width, ff), low)]
    norm_keep, norm_give, hidden, grad_pre, mlp_in = call(
        feed_kernel,
        0,
        [mlp_low, mlp_y, mlp_x, mlp_d0, mlp_d1, mlp_c, mlp_cyx, mlp_cd] + cots + [ff_all, up_low],
        shapes,
        scratch,
        limit=60,
    )

    n_ff = 8 * rows + n_half * ff_own
    ff_terms = call(
        feed_grad_kernel, 0, [mlp_in, grad_pre, hidden] + cots, [((nz, n_ff + 16, ff), low)], (), 1, 60
    )[0]
    norm_c_got = exchange(norm_give, "c")
    norm_c_got, ff_terms = gate(norm_c_got, ff_terms)
    ff_sum = lax.psum_scatter(ff_terms, "z", scatter_dimension=0, tiled=True)[0]

    norm_d0 = exchange(add_low(norm_keep[3, :half], norm_c_got[3, :half]), "y")
    norm_d1 = exchange(add_low(norm_keep[3, half:], norm_c_got[3, half:]), "x")
    norm_own, norm_y, norm_x = (add_low(norm_keep[k], norm_c_got[k]) for k in range(3))
    norm_d0, norm_d1, norm_own, norm_y, norm_x = gate(norm_d0, norm_d1, norm_own, norm_y, norm_x)
    norm_y = exchange(jnp.concatenate([norm_y[:half], add_low(norm_y[half:], norm_d1)], 0), "y")
    norm_x = exchange(jnp.concatenate([add_low(norm_x[:half], norm_d0), norm_x[half:]], 0), "x")
    result_keep, result_give = call(
        result_kernel, 0, [after(hidden, norm_d0), ff_all], [four, four], [((ff, width), low)]
    )
    norm_x, norm_y, result_keep, result_give = gate(norm_x, norm_y, result_keep, result_give)
    shapes = [((tokens, width), f32), ((n_ctx, tokens, cols), low), ((8, width), f32)]
    shapes = shapes + [((2, 2, nz, rows, width), low)] * 2
    grad_resid, back_low, resid_sums, out_keep, out_give = call(
        norm_back_kernel,
        1,
        [table, norm_own, norm_x, norm_y, resid, cot_low, vec, out_w, attended_low],
        shapes,
        [((width, width), low)],
    )

    back_all = swap(back_low, ctx)
    out_c_got = exchange(out_give, "c")
    result_c_got = exchange(result_give, "c")
    back_all, out_c_got, result_c_got = gate(back_all, out_c_got, result_c_got)

    out_x_got = exchange(add_low(out_keep[1], out_c_got[1]), "x")
    shapes = [((2, n_ctx, rows, 4 * cols), low)] * 2
    part = width // 2
    shapes = shapes + [((nz, tokens, part), low)] * 2 + [((nz, tokens, width - part), low)] * 2
    scratch = [((seq_len, 3 * cols), low), ((seq_len, cols), low), ((seq_len, cols), f32), ((seq_len, cols), f32)]
    scratch = scratch + [((seq_len, width), low), ((width, 4 * cols), low)]
    back_all = back_all.reshape(seq_len, cols)
    made = call(
        backward_kernel,
        2,
        [table, slopes, back_all, qkv_low, att_t, lse, start, normed_one, qkv_w, seq_rows, resid_sums],
        shapes,
        scratch,
        9000000000,
        60,
    )
    *made, out_x_got = gate(*made, out_x_got)
    qkv_keep, qkv_give = made[:2]
    in_keep, in_give = made[2::2], made[3::2]

    qkv_c_got = exchange(qkv_give, "c")
    qkv_c = add_low(qkv_keep[0], qkv_c_got[0])
    qkv_x_got = exchange(add_low(qkv_keep[1], qkv_c_got[1]), "x")
    out_c = add_low(out_keep[0], out_c_got[0])
    out_two = add_low(out_c[0], out_x_got[0])
    out_y_got = exchange(add_low(out_c[1], out_x_got[1]), "y")
    in_a = exchange(after(in_give[0], qkv_c), "y")
    result_send = add_low(result_keep[2:], result_c_got[2:])
    result_x = exchange(after(result_send, qkv_c), "x")
    qkv_x_got, qkv_c, out_y_got, result_send = gate(qkv_x_got, qkv_c, out_y_got, result_send)
    qkv_x = add_low(qkv_c, qkv_x_got)

    qkv_got = swap(qkv_x, ctx)
    out_own = add_low(out_two[0], out_y_got[0])
    out_moved = [shift(add_low(out_two[k], out_y_got[k]), "z", nz, -k) for k in range(1, nz)]
    in_b = exchange(after(in_give[1], qkv_c), "y")
    in_a = after(in_a, qkv_x)
    in_za = [shift(add_low(in_keep[0][k], in_a[k]), "z", nz, -k) for k in range(1, nz)]
    up_send = after(ff_sum, qkv_x)[: 8 * rows].reshape(8, rows, ff)
    result_x = after(result_x, qkv_x)
    result_c = add_low(result_keep[:2], result_c_got[:2])
    result_y = exchange(add_low(result_c[1], result_x[1]), "y")
    qkv_got, in_b, up_send, *gated = gate(qkv_got, in_b, up_send, *out_moved, out_own)
    out_moved = gated[: nz - 1]
    shapes = [((8, 128), f32), ((rows, width), f32), ((8, rows), f32)]
    squared, grad_out_own, grad_vec_own = call(
        square_kernel, 1, [table, qkv_got, ff_sum, out_own, *out_moved], shapes
    )

    squares = swap(jnp.broadcast_to(squared[:1], (4 * n_ctx, 128)), every)
    in_zb = [shift(add_low(in_keep[1][k], in_b[k]), "z", nz, -k) for k in range(1, nz)]
    result_y = after(result_y, squared)
    result = resid + result_c[0].astype(f32) + result_x[0].astype(f32) + result_y.astype(f32) + vec[7]
    result, squares = gate(result.astype(low), squares)
    up_got = swap(after(up_send, squares), plane)
    masters = [w_qkv, w_out, w_down, up_bias.reshape(1, ff_own), vectors]
    firsts = [first_qkv, first_out, first_down, first_bias.reshape(1, ff_own), first_vectors]
    seconds = [second_qkv, second_out, second_down, second_bias.reshape(1, ff_own), second_vectors]
    shapes = [((1, 1), f32)]
    for item in masters:
        shapes = shapes + [(item.shape, f32)] * 4
    grads = [squares, qkv_got, grad_out_own, ff_sum, grad_vec_own]
    grad_norm, *results = call(adam_kernel, 0, grads + masters + firsts + seconds, shapes, limit=60)
    for k in range(12, 16):
        results[k] = results[k].reshape(ff_own)
    ups = call(adam_up_kernel, 0, [squares, up_got, w_up, first_up, second_up], [(w_up.shape, f32)] * 4, limit=60)
    results = results[:8] + list(ups) + results[8:]

    *late, _ = gate(*in_za, *in_zb, grad_norm)
    sum_a = in_keep[0][0].astype(f32) + in_a[0].astype(f32)
    sum_b = in_keep[1][0].astype(f32) + in_b[0].astype(f32)
    for k in range(nz - 1):
        sum_a = sum_a + late[k].astype(f32)
        sum_b = sum_b + late[nz - 1 + k].astype(f32)
    own_grads = jnp.concatenate([sum_a, sum_b], 1)
    norm_one_back = jax.vjp(lambda v: layer_norm(v, vec[0], vec[1]), field)[1]
    in_grad = grad_resid + norm_one_back(own_grads)[0]
    return (result[None], in_grad[None], grad_norm[0, 0], *results)


def solution(mesh):
    n_ctx = mesh.shape["ctx"]
    if HEADS % n_ctx == 0 and n_ctx % 2 == 0 and mesh.shape["fsdp"] == 4:
        body = local_split
        ctx, fsdp = ("z", "y"), ("x", "c")
        mesh = Mesh(mesh.devices.reshape(n_ctx // 2, 2, 2, 2), ctx + fsdp)
    else:
        body = local
        ctx, fsdp = ("ctx",), ("fsdp",)
    rows = P(fsdp, ctx, None)
    flat = P(fsdp, ctx)
    mat = P(ctx + fsdp, None)
    vec = P(ctx + fsdp)
    wide = P(None, ctx + fsdp)
    group = (mat, mat, mat, mat, vec, wide)
    outs = ()
    for spec in group:
        outs = outs + (spec,) * 4
    return jax.shard_map(
        body,
        mesh=mesh,
        in_specs=(rows, rows, flat, flat) + group * 3,
        out_specs=(rows, rows, P()) + outs,
        check_vma=False,
    )
```

profile of v0, /device:TPU:11, one launch (start us, length us, event | category | flops | bytes accessed | tf_op | source)
XLA Modules:
  0.0 276.2 jit_solution(8237885760170117343)
XLA Ops:
  7.9 2.4 shard_map.421
  10.3 5.9 %all-to-all-start = ((bf16[8,32,512]{2,1,0:T(8,128)(2,1)}), bf16[8,32,512]{2,1,0:T(8,128)(2,1)S(1)}, u32[]{:S(2)}, u32[]{:S(2)}) async-start(bf16[8,32,512]{2,1,0:T(8,128)(2,1)} %get-tuple-element.166), calls=%async_computation | async-start | bytes 524288 | tf_op jit(solution)/shard_map/all_to_all | solution.py:338
  16.2 2.4 collective-permute-start.2
  18.6 2.1 collective-permute-start.3
  20.7 1.2 collective-permute-start
  22.1 7.0 %all-to-all-done.refs_9_ = bf16[8,32,512]{2,1,0:T(8,128)(2,1)S(1)} async-done(((bf16[8,32,512]{2,1,0:T(8,128)(2,1)}), bf16[8,32,512]{2,1,0:T(8,128)(2,1)S(1)}, u32[]{:S(2)}, u32[]{:S(2)}) %all-to-all-start) | async-done | bytes 262176 | tf_op jit(solution)/shard_map/all_to_all | solution.py:338
  29.1 6.4 %all-to-all-start.1 = ((bf16[8,32,512]{2,1,0:T(8,128)(2,1)}), bf16[8,32,512]{2,1,0:T(8,128)(2,1)S(1)}, u32[]{:S(2)}, u32[]{:S(2)}) async-start(bf16[8,32,512]{2,1,0:T(8,128)(2,1)} %get-tuple-element.167), calls=%async_computation.1 | async-start | bytes 524288 | tf_op jit(solution)/shard_map/all_to_all | solution.py:338
  36.1 4.7 %all-to-all-done.1 = bf16[8,32,512]{2,1,0:T(8,128)(2,1)S(1)} async-done(((bf16[8,32,512]{2,1,0:T(8,128)(2,1)}), bf16[8,32,512]{2,1,0:T(8,128)(2,1)S(1)}, u32[]{:S(2)}, u32[]{:S(2)}) %all-to-all-start.1) | async-done | bytes 262176 | tf_op jit(solution)/shard_map/all_to_all | solution.py:338
  41.9 3.2 %collective-permute-start.10 = (bf16[3,128,256]{2,1,0:T(8,128)(2,1)S(1)}, bf16[3,128,256]{2,1,0:T(8,128)(2,1)}, u32[]{:S(2)}, u32[]{:S(2)}) collective-permute-start(bf16[3,128,256]{2,1,0:T(8,128)(2,1)S(1)} %pad_maximum_fusion.10), channel_id=1, source_target_pairs={{0,16},{8,24},{16,0},{24,8},{1,17},{9,25},{17,1},{25,9},{2,18},{10... | collective-permute-start | bytes 589832 | tf_op jit(solution)/shard_map/ppermute | solution.py:334
  48.6 1.6 collective-permute-start.11
  51.1 6.2 %collective-permute-done.10.refs_7_ = bf16[3,128,256]{2,1,0:T(8,128)(2,1)} collective-permute-done((bf16[3,128,256]{2,1,0:T(8,128)(2,1)S(1)}, bf16[3,128,256]{2,1,0:T(8,128)(2,1)}, u32[]{:S(2)}, u32[]{:S(2)}) %collective-permute-start.10) | collective-permute-done | bytes 196640 | tf_op jit(solution)/shard_map/ppermute | solution.py:334
  57.3 2.3 collective-permute-start.5
  59.7 1.1 convert_reduce_fusion
  61.6 1.3 collective-permute-start.13
  64.8 1.8 collective-permute-start.16
  66.6 11.5 %shard_map.422 = (bf16[1024,128]{1,0:T(8,128)(2,1)}, f32[128,1024]{1,0:T(8,128)}, bf16[1024,384]{1,0:T(8,128)(2,1)}, f32[8,1024]{1,0:T(8,128)}, bf16[1024,1024]{...) custom-call(s32[41]{0:T(128)} %concatenate.16.meta.table, ...), custom_call_target="tpu_custom_call" | custom-call | flops 8999999488 | bytes 8999999488 | tf_op jit(solution)/shard_map/pallas_call | solution.py:817
  80.3 5.9 %all-to-all-start.2 = ((bf16[8,128,128]{2,1,0:T(8,128)(2,1)}), bf16[8,128,128]{2,1,0:T(8,128)(2,1)S(1)}, u32[]{:S(2)}, u32[]{:S(2)}) async-start(bf16[8,128,128]{2,1,0:T(8,128)(2,1)} %bitcast.176), calls=%async_computation.2 | async-start | bytes 524288 | tf_op jit(solution)/shard_map/all_to_all | solution.py:338
  86.2 11.8 %all-to-all-done.2.att = bf16[8,128,128]{2,1,0:T(8,128)(2,1)S(1)} async-done(((bf16[8,128,128]{2,1,0:T(8,128)(2,1)}), bf16[8,128,128]{2,1,0:T(8,128)(2,1)S(1)}, u32[]{:S(2)}, u32[]{:S(2)}) %all-to-all-start.2) | async-done | bytes 262176 | tf_op jit(solution)/shard_map/all_to_all | solution.py:338
  98.0 2.7 collective-permute-start.17
  100.7 1.5 collective-permute-done.17.cx_ref
  103.0 1.4 shard_map.423
  104.4 1.3 copy-done.7
  107.5 5.7 %collective-permute-done.18.refs_1_ = bf16[128,1024]{1,0:T(8,128)(2,1)S(1)} collective-permute-done((bf16[128,1024]{1,0:T(8,128)(2,1)S(1)}, bf16[128,1024]{1,0:T(8,128)(2,1)S(1)}, u32[]{:S(2)}, u32[]{:S(2)}) %collective-permute-start.18) | collective-permute-done | bytes 262176 | tf_op jit(solution)/shard_map/ppermute | solution.py:330
  116.2 2.2 collective-permute-start.23
  118.5 1.6 collective-permute-done.22.refs_4_
  120.1 2.7 collective-permute-start.24
  124.9 9.0 %shard_map.424 = (bf16[4,128,1024]{2,1,0:T(8,128)(2,1)}, bf16[4,128,1024]{2,1,0:T(8,128)(2,1)}, bf16[1024,512]{1,0:T(8,128)(2,1)}, bf16[1024,512]{1,0:T(8,128)(2,1)}, bf16[1024,1024]{1,0:T(8,128)(2,1)}) custom-call(bf16[128,1024]{1,0:T(8,128)(2,1)} %copy-done.10, bf16[128,1024]{1,0:T(8,128)(2,1)} %copy-done.23, bf16[128,1024]{1,0:T(8,128)(2,1)} %copy-done.24, ...), custom_call_target="tpu_custom_call" | custom-call | flops 1 | bytes 1 | tf_op jit(solution)/shard_map/pallas_call | solution.py:817
  134.2 6.6 %shard_map.425 = bf16[4,528,512]{2,1,0:T(8,128)(2,1)} custom-call(bf16[1024,1024]{1,0:T(8,128)(2,1)} %get-tuple-element.205.mlp_ref, bf16[1024,512]{1,0:T(8,128)(2,1)} %get-tuple-element.206.pre_ref, bf16[1024,512]{1,0:T(8,128)(2,1)} %get-tuple-element.213.hidden_ref, bf16[2,128,1024]{2,1,0:T(8,128)(2,1)} %copy-done.20, bf16[2,128,1024]{2,1,0:T(8,128)(2,1)} %copy-done.21, ...), custom_call_target="tpu_custom_call" | custom-call | flops 1 | bytes 1 | tf_op jit(solution)/shard_map/pallas_call | solution.py:817
  142.8 1.5 fusion.13
  144.3 2.5 collective-permute-done.26
  148.8 2.2 shard_map.426
  151.0 2.8 %collective-permute-done.29.got_y = bf16[128,1024]{1,0:T(8,128)(2,1)S(1)} collective-permute-done((bf16[128,1024]{1,0:T(8,128)(2,1)S(1)}, bf16[128,1024]{1,0:T(8,128)(2,1)S(1)}, u32[]{:S(2)}, u32[]{:S(2)}) %collective-permute-start.29) | collective-permute-done | bytes 262176 | tf_op jit(solution)/shard_map/ppermute | solution.py:330
  154.6 4.7 %shard_map.427 = (f32[128,1024]{1,0:T(8,128)S(1)}, bf16[8,128,128]{2,1,0:T(8,128)(2,1)S(1)}, f32[8,1024]{1,0:T(8,128)S(1)}, bf16[2,2,4,32,1024]{4,3,2,1,0:T(8,128)(2,1)S(1)}, bf16[2,2,4,32,1024]{4,3,2,1,0:T(8,128)(2,1)}) custom-call(s32[41]{0:T(128)S(1)} %copy-done.16, bf16[128,1024]{1,0:T(8,128)(2,1)S(1)} %get-tuple-element.217.own, ...), custom_call_target="tpu_custom_call" | custom-call | flops 1 | bytes 1 | tf_op jit(solution)/shard_map/pallas_call | solution.py:817
  161.3 2.5 collective-permute-start.30
  163.9 14.4 %all_to_all.39 = bf16[8,128,128]{2,1,0:T(8,128)(2,1)} all-to-all(bf16[8,128,128]{2,1,0:T(8,128)(2,1)S(1)} %copy-done.12), channel_id=1, replica_groups=mesh['z'=4,'y'=2,'x'=2,'c'=2] {'z','y'}, dimensions={0} | all-to-all | bytes 524288 | tf_op jit(solution)/shard_map/all_to_all | solution.py:338
  178.3 2.4 add_convert_fusion
  181.7 11.8 %shard_map.428 = (bf16[2,8,32,512]{3,2,1,0:T(8,128)(2,1)}, bf16[2,8,32,512]{3,2,1,0:T(8,128)(2,1)}, bf16[4,128,512]{2,1,0:T(8,128)(2,1)}, bf16[4,128,512]{2,1,0:...) custom-call(s32[41]{0:T(128)} %concatenate.16.meta.table, f32[2]{0:T(128)} %multiply_exponential_fusion.slopes, ...), custom_call_target="tpu_custom_call" | custom-call | flops 8999999488 | bytes 8999999488 | tf_op jit(solution)/shard_map/pallas_call | solution.py:817
  193.5 5.5 %collective-permute-start.33 = (bf16[2,8,32,512]{3,2,1,0:T(8,128)(2,1)}, bf16[2,8,32,512]{3,2,1,0:T(8,128)(2,1)S(1)}, u32[]{:S(2)}, u32[]{:S(2)}) collective-permute-start(bf16[2,8,32,512]{3,2,1,0:T(8,128)(2,1)} %get-tuple-element.242), channel_id=1, source_target_pairs={{0,1},{1,0},{2,3},{3,2},{4,5},{5,4},{6,7},{7,6},{8,9},{9,8},{10,11... | collective-permute-start | bytes 1572872 | tf_op jit(solution)/shard_map/ppermute | solution.py:330
  199.4 1.4 collective-permute-done.33
  200.9 1.1 collective-permute-start.35
  202.1 2.4 add_convert_fusion.2
  205.0 2.5 collective-permute-done.36
  207.4 1.2 collective-permute-done.35
  209.7 4.0 %collective-permute-start.40 = (bf16[32,1024]{1,0:T(8,128)(2,1)S(1)}, bf16[32,1024]{1,0:T(8,128)(2,1)S(1)}, u32[]{:S(2)}, u32[]{:S(2)}) collective-permute-start(bf16[32,1024]{1,0:T(8,128)(2,1)S(1)} %get-tuple-element.326), channel_id=1, source_target_pairs={{0,16},{8,24},{16,0},{24,8},{1,17},{9,25},{17,1},{25,9},{2,18},{10... | collective-permute-start | bytes 196616 | tf_op jit(solution)/shard_map/ppermute | solution.py:334
  213.7 1.2 collective-permute-start.38
  215.6 3.5 %all-to-all-start.4 = ((bf16[8,32,512]{2,1,0:T(8,128)(2,1)}), bf16[8,32,512]{2,1,0:T(8,128)(2,1)S(1)}, u32[]{:S(2)}, u32[]{:S(2)}) async-start(bf16[8,32,512]{2,1,0:T(8,128)(2,1)} %add_convert_fusion.5), calls=%async_computation.4 | async-start | bytes 524288 | tf_op jit(solution)/shard_map/all_to_all | solution.py:338
  219.9 2.9 %collective-permute-start.41 = (bf16[32,1024]{1,0:T(8,128)(2,1)S(1)}, bf16[32,1024]{1,0:T(8,128)(2,1)S(1)}, u32[]{:S(2)}, u32[]{:S(2)}) collective-permute-start(bf16[32,1024]{1,0:T(8,128)(2,1)S(1)} %get-tuple-element.325), channel_id=1, source_target_pairs={{0,24},{8,0},{16,8},{24,16},{1,25},{9,1},{17,9},{25,17},{2,26},{10... | collective-permute-start | bytes 196616 | tf_op jit(solution)/shard_map/ppermute | solution.py:334
  223.8 1.2 collective-permute-start.37
  225.0 1.8 fusion.26
  226.8 1.7 slice.278
  228.5 2.3 collective-permute-start.44
  231.7 1.1 copy-done.4
  234.9 2.4 collective-permute-done.37
  238.0 7.5 %all-to-all-start.5 = ((f32[32,1,128]{2,1,0:T(1,128)}), f32[32,1,128]{2,1,0:T(1,128)S(1)}, u32[]{:S(2)}, u32[]{:S(2)}) async-start(f32[32,1,128]{2,1,0:T(1,128)} %broadcast_in_dim.68), calls=%async_computation.6 | async-start | bytes 32768 | tf_op jit(solution)/shard_map/all_to_all | solution.py:338
  245.5 1.8 fusion.29
  247.3 1.2 collective-permute-start.46
  248.6 1.0 collective-permute-start.47
  249.6 1.4 collective-permute-start.48
  251.0 1.9 fusion.9
  252.9 5.1 %all-to-all-start.6 = ((bf16[8,32,512]{2,1,0:T(8,128)(2,1)}), bf16[8,32,512]{2,1,0:T(8,128)(2,1)S(1)}, u32[]{:S(2)}, u32[]{:S(2)}) async-start(bf16[8,32,512]{2,1,0:T(8,128)(2,1)} %bitcast.54), calls=%async_computation.7 | async-start | bytes 524288 | tf_op jit(solution)/shard_map/all_to_all | solution.py:338
  258.0 4.3 %shard_map.430 = (f32[1,1]{1,0:T(1,128)}, f32[32,3072]{1,0:T(8,128)}, f32[32,3072]{1,0:T(8,128)}, f32[32,3072]{1,0:T(8,128)}, f32[32,3072]{1,0:T(8,128)}, /*inde...) custom-call(f32[32,128]{1,0:T(8,128)} %bitcast.186, ...), custom_call_target="tpu_custom_call" | custom-call | flops 1 | bytes 1 | tf_op jit(solution)/shard_map/pallas_call | solution.py:817
  262.4 1.4 fusion.19
  264.3 1.1 add_bitcast_fusion
  266.1 3.2 %shard_map.431 = (f32[32,4096]{1,0:T(8,128)}, f32[32,4096]{1,0:T(8,128)}, f32[32,4096]{1,0:T(8,128)}, f32[32,4096]{1,0:T(8,128)}) custom-call(f32[32,128]{1,0:T(8,128)} %bitcast.187, bf16[8,32,512]{2,1,0:T(8,128)(2,1)} %copy-done.25, f32[32,4096]{1,0:T(8,128)} %refs_0_.1, f32[32,4096]{1,0:T(8,128)} %refs_1_.1, f32[32,4096]{1,0:T(8,128)} %refs_2_.1), custom_call_target="tpu_custom_call" | custom-call | flops 1 | bytes 1 | tf_op jit(solution)/shard_map/pallas_call | solution.py:817
  (221 shorter events, 36.6 us)
Async XLA Ops:
  10.3 30.5 %copy-start.36 = (bf16[2,128,512]{2,1,0:T(8,128)(2,1)S(1)}, bf16[2,128,512]{2,1,0:T(8,128)(2,1)}, u32[]{:S(2)}) copy-start(bf16[2,128,512]{2,1,0:T(8,128)(2,1)} %get-tuple-element.168) | copy-start | bytes 786436
  10.3 18.8 %all-to-all-start = ((bf16[8,32,512]{2,1,0:T(8,128)(2,1)}), bf16[8,32,512]{2,1,0:T(8,128)(2,1)S(1)}, u32[]{:S(2)}, u32[]{:S(2)}) async-start(bf16[8,32,512]{2,1,0:T(8,128)(2,1)} %get-tuple-element.166), calls=%async_computation | async-start | bytes 524288 | tf_op jit(solution)/shard_map/all_to_all | solution.py:338
  16.2 25.6 %copy-start.37 = (bf16[128,256]{1,0:T(8,128)(2,1)S(1)}, bf16[128,256]{1,0:T(8,128)(2,1)}, u32[]{:S(2)}) copy-start(bf16[128,256]{1,0:T(8,128)(2,1)} %get-tuple-element.175) | copy-start | bytes 196612
  16.2 25.5 %collective-permute-start.1 = (bf16[128,768]{1,0:T(8,128)(2,1)S(1)}, bf16[128,768]{1,0:T(8,128)(2,1)S(1)}, u32[]{:S(2)}, u32[]{:S(2)}) collective-permute-start(bf16[128,768]{1,0:T(8,128)(2,1)S(1)} %slice.309), channel_id=1, source_target_pairs={{0,24},{8,0},{16,8},{24,16},{1,25},{9,1},{17,9},{25,17},{2,26},{10... | collective-permute-start | bytes 589832 | tf_op jit(solution)/shard_map/ppermute | solution.py:334
  16.2 25.4 %collective-permute-start.2 = (bf16[128,768]{1,0:T(8,128)(2,1)S(1)}, bf16[128,768]{1,0:T(8,128)(2,1)S(1)}, u32[]{:S(2)}, u32[]{:S(2)}) collective-permute-start(bf16[128,768]{1,0:T(8,128)(2,1)S(1)} %slice.309), channel_id=1, source_target_pairs={{0,16},{8,24},{16,0},{24,8},{1,17},{9,25},{17,1},{25,9},{2,18},{10... | collective-permute-start | bytes 589832 | tf_op jit(solution)/shard_map/ppermute | solution.py:334
  18.6 23.1 %collective-permute-start.3 = (bf16[128,768]{1,0:T(8,128)(2,1)S(1)}, bf16[128,768]{1,0:T(8,128)(2,1)S(1)}, u32[]{:S(2)}, u32[]{:S(2)}) collective-permute-start(bf16[128,768]{1,0:T(8,128)(2,1)S(1)} %slice.309), channel_id=1, source_target_pairs={{0,8},{8,16},{16,24},{24,0},{1,9},{9,17},{17,25},{25,1},{2,10},{10... | collective-permute-start | bytes 589832 | tf_op jit(solution)/shard_map/ppermute | solution.py:334
  20.7 20.9 %collective-permute-start = (bf16[2,128,1024]{2,1,0:T(8,128)(2,1)S(1)}, bf16[2,128,1024]{2,1,0:T(8,128)(2,1)S(1)}, u32[]{:S(2)}, u32[]{:S(2)}) collective-permute-start(bf16[2,128,1024]{2,1,0:T(8,128)(2,1)S(1)} %pad_maximum_fusion.2), channel_id=1, source_target_pairs={{0,4},{4,0},{1,5},{5,1},{2,6},{6,2},{3,7},{7,3},{8,12},{12,8},{9,1... | collective-permute-start | bytes 1572872 | tf_op jit(solution)/shard_map/ppermute | solution.py:330
  29.1 28.2 %copy-start.34 = (bf16[8,32,512]{2,1,0:T(8,128)(2,1)}, bf16[8,32,512]{2,1,0:T(8,128)(2,1)S(1)}, u32[]{:S(2)}) copy-start(bf16[8,32,512]{2,1,0:T(8,128)(2,1)S(1)} %all-to-all-done.refs_9_) | copy-start | bytes 786436
  29.1 11.7 %all-to-all-start.1 = ((bf16[8,32,512]{2,1,0:T(8,128)(2,1)}), bf16[8,32,512]{2,1,0:T(8,128)(2,1)S(1)}, u32[]{:S(2)}, u32[]{:S(2)}) async-start(bf16[8,32,512]{2,1,0:T(8,128)(2,1)} %get-tuple-element.167), calls=%async_computation.1 | async-start | bytes 524288 | tf_op jit(solution)/shard_map/all_to_all | solution.py:338
  35.5 88.6 %all-gather.3.cloned.1.call-start = ((), (), s32[]{:S(2)}) async-start(), calls=%async_computation.9 | async-start | bytes 2621440 | tf_op jit(solution)/shard_map/all_gather | solution.py:881
  41.8 6.8 %collective-permute-start.9 = (bf16[3,128,256]{2,1,0:T(8,128)(2,1)S(1)}, bf16[3,128,256]{2,1,0:T(8,128)(2,1)S(1)}, u32[]{:S(2)}, u32[]{:S(2)}) collective-permute-start(bf16[3,128,256]{2,1,0:T(8,128)(2,1)S(1)} %pad_maximum_fusion.10), channel_id=1, source_target_pairs={{0,24},{8,0},{16,8},{24,16},{1,25},{9,1},{17,9},{25,17},{2,26},{10... | collective-permute-start | bytes 589832 | tf_op jit(solution)/shard_map/ppermute | solution.py:334
  41.9 15.4 %collective-permute-start.10 = (bf16[3,128,256]{2,1,0:T(8,128)(2,1)S(1)}, bf16[3,128,256]{2,1,0:T(8,128)(2,1)}, u32[]{:S(2)}, u32[]{:S(2)}) collective-permute-start(bf16[3,128,256]{2,1,0:T(8,128)(2,1)S(1)} %pad_maximum_fusion.10), channel_id=1, source_target_pairs={{0,16},{8,24},{16,0},{24,8},{1,17},{9,25},{17,1},{25,9},{2,18},{10... | collective-permute-start | bytes 589832 | tf_op jit(solution)/shard_map/ppermute | solution.py:334
  45.4 14.2 %collective-permute-start.4 = (bf16[8,32,512]{2,1,0:T(8,128)(2,1)S(1)}, bf16[8,32,512]{2,1,0:T(8,128)(2,1)}, u32[]{:S(2)}, u32[]{:S(2)}) collective-permute-start(bf16[8,32,512]{2,1,0:T(8,128)(2,1)S(1)} %all-to-all-done.refs_9_), channel_id=1, source_target_pairs={{0,2},{2,0},{1,3},{3,1},{4,6},{6,4},{5,7},{7,5},{8,10},{10,8},{9,1... | collective-permute-start | bytes 786440 | tf_op jit(solution)/shard_map/ppermute | solution.py:330
  46.1 17.8 %collective-permute-start.8 = (bf16[3,128,768]{2,1,0:T(8,128)(2,1)S(1)}, bf16[3,128,768]{2,1,0:T(8,128)(2,1)}, u32[]{:S(2)}, u32[]{:S(2)}) collective-permute-start(bf16[3,128,768]{2,1,0:T(8,128)(2,1)S(1)} %pad_maximum_fusion), channel_id=1, source_target_pairs={{0,4},{4,0},{1,5},{5,1},{2,6},{6,2},{3,7},{7,3},{8,12},{12,8},{9,1... | collective-permute-start | bytes 1769480 | tf_op jit(solution)/shard_map/ppermute | solution.py:330
  46.5 31.7 %copy-start.20 = (bf16[2,128,1024]{2,1,0:T(8,128)(2,1)}, bf16[2,128,1024]{2,1,0:T(8,128)(2,1)S(1)}, u32[]{:S(2)}) copy-start(bf16[2,128,1024]{2,1,0:T(8,128)(2,1)S(1)} %pad_maximum_fusion.3.refs_8_.cot_0) | copy-start | bytes 1572868
  46.5 17.4 %collective-permute-start.7 = (bf16[2,128,1024]{2,1,0:T(8,128)(2,1)S(1)}, bf16[2,128,1024]{2,1,0:T(8,128)(2,1)S(1)}, u32[]{:S(2)}, u32[]{:S(2)}) collective-permute-start(bf16[2,128,1024]{2,1,0:T(8,128)(2,1)S(1)} %pad_maximum_fusion.3.refs_8_.cot_0), channel_id=1, source_target_pairs={{0,2},{2,0},{1,3},{3,1},{4,6},{6,4},{5,7},{7,5},{8,10},{10,8},{9,1... | collective-permute-start | bytes 1572872 | tf_op jit(solution)/shard_map/ppermute | solution.py:330
  48.6 13.1 %collective-permute-start.11 = (bf16[3,128,256]{2,1,0:T(8,128)(2,1)S(1)}, bf16[3,128,256]{2,1,0:T(8,128)(2,1)}, u32[]{:S(2)}, u32[]{:S(2)}) collective-permute-start(bf16[3,128,256]{2,1,0:T(8,128)(2,1)S(1)} %pad_maximum_fusion.10), channel_id=1, source_target_pairs={{0,8},{8,16},{16,24},{24,0},{1,9},{9,17},{17,25},{25,1},{2,10},{10... | collective-permute-start | bytes 589832 | tf_op jit(solution)/shard_map/ppermute | solution.py:334
  57.3 6.5 %collective-permute-start.5 = (bf16[8,32,512]{2,1,0:T(8,128)(2,1)S(1)}, bf16[8,32,512]{2,1,0:T(8,128)(2,1)S(1)}, u32[]{:S(2)}, u32[]{:S(2)}) collective-permute-start(bf16[8,32,512]{2,1,0:T(8,128)(2,1)S(1)} %all-to-all-done.refs_9_), channel_id=1, source_target_pairs={{0,1},{1,0},{2,3},{3,2},{4,5},{5,4},{6,7},{7,6},{8,9},{9,8},{10,11... | collective-permute-start | bytes 786440 | tf_op jit(solution)/shard_map/ppermute | solution.py:330
  59.6 4.2 %collective-permute-start.6 = (bf16[8,32,512]{2,1,0:T(8,128)(2,1)}, bf16[8,32,512]{2,1,0:T(8,128)(2,1)S(1)}, u32[]{:S(2)}, u32[]{:S(2)}) collective-permute-start(bf16[8,32,512]{2,1,0:T(8,128)(2,1)} %collective-permute-done.4.refs_10_), channel_id=1, source_target_pairs={{0,1},{1,0},{2,3},{3,2},{4,5},{5,4},{6,7},{7,6},{8,9},{9,8},{10,11... | collective-permute-start | bytes 786440 | tf_op jit(solution)/shard_map/ppermute | solution.py:330
  61.6 16.5 %collective-permute-start.13 = (bf16[2,128,1024]{2,1,0:T(8,128)(2,1)S(1)}, bf16[2,128,1024]{2,1,0:T(8,128)(2,1)S(1)}, u32[]{:S(2)}, u32[]{:S(2)}) collective-permute-start(bf16[2,128,1024]{2,1,0:T(8,128)(2,1)S(1)} %pad_maximum_fusion.3.refs_8_.cot_0), channel_id=1, source_target_pairs={{0,1},{1,0},{2,3},{3,2},{4,5},{5,4},{6,7},{7,6},{8,9},{9,8},{10,11... | collective-permute-start | bytes 1572872 | tf_op jit(solution)/shard_map/ppermute | solution.py:330
  64.6 37.6 %copy-start.1 = (bf16[1,128,1024]{2,1,0:T(8,128)(2,1)S(1)}, bf16[1,128,1024]{2,1,0:T(8,128)(2,1)}, u32[]{:S(2)}) copy-start(bf16[1,128,1024]{2,1,0:T(8,128)(2,1)} %param.22) | copy-start | bytes 786436
  64.6 37.6 %copy-start.16 = (s32[41]{0:T(128)S(1)}, s32[41]{0:T(128)}, u32[]{:S(2)}) copy-start(s32[41]{0:T(128)} %concatenate.16.meta.table) | copy-start | bytes 496
  64.6 13.5 %collective-permute-start.12 = (bf16[4,128,256]{2,1,0:T(8,128)(2,1)S(1)}, bf16[4,128,256]{2,1,0:T(8,128)(2,1)S(1)}, u32[]{:S(2)}, u32[]{:S(2)}) collective-permute-start(bf16[4,128,256]{2,1,0:T(8,128)(2,1)S(1)} %pad_maximum_fusion.6), channel_id=1, source_target_pairs={{0,4},{4,0},{1,5},{5,1},{2,6},{6,2},{3,7},{7,3},{8,12},{12,8},{9,1... | collective-permute-start | bytes 786440 | tf_op jit(solution)/shard_map/ppermute | solution.py:330
  64.8 21.5 %collective-permute-start.16 = (bf16[2,128,1024]{2,1,0:T(8,128)(2,1)S(1)}, bf16[2,128,1024]{2,1,0:T(8,128)(2,1)}, u32[]{:S(2)}, u32[]{:S(2)}) collective-permute-start(bf16[2,128,1024]{2,1,0:T(8,128)(2,1)S(1)} %collective-permute-done.7.refs_9_.cot_1), channel_id=1, source_target_pairs={{0,1},{1,0},{2,3},{3,2},{4,5},{5,4},{6,7},{7,6},{8,9},{9,8},{10,11... | collective-permute-start | bytes 1572872 | tf_op jit(solution)/shard_map/ppermute | solution.py:330
  79.0 19.1 %collective-permute-start.14 = (bf16[2,4,128,256]{3,2,1,0:T(8,128)(2,1)S(1)}, bf16[2,4,128,256]{3,2,1,0:T(8,128)(2,1)S(1)}, u32[]{:S(2)}, u32[]{:S(2)}) collective-permute-start(bf16[2,4,128,256]{3,2,1,0:T(8,128)(2,1)S(1)} %pad_maximum_fusion.4.own_ref), channel_id=1, source_target_pairs={{0,2},{2,0},{1,3},{3,1},{4,6},{6,4},{5,7},{7,5},{8,10},{10,8},{9,1... | collective-permute-start | bytes 1572872 | tf_op jit(solution)/shard_map/ppermute | solution.py:330
  79.6 18.4 %collective-permute-start.15 = (bf16[2,4,128,256]{3,2,1,0:T(8,128)(2,1)S(1)}, bf16[2,4,128,256]{3,2,1,0:T(8,128)(2,1)S(1)}, u32[]{:S(2)}, u32[]{:S(2)}) collective-permute-start(bf16[2,4,128,256]{3,2,1,0:T(8,128)(2,1)S(1)} %pad_maximum_fusion.4.own_ref), channel_id=1, source_target_pairs={{0,1},{1,0},{2,3},{3,2},{4,5},{5,4},{6,7},{7,6},{8,9},{9,8},{10,11... | collective-permute-start | bytes 1572872 | tf_op jit(solution)/shard_map/ppermute | solution.py:330
  80.3 17.7 %all-to-all-start.2 = ((bf16[8,128,128]{2,1,0:T(8,128)(2,1)}), bf16[8,128,128]{2,1,0:T(8,128)(2,1)S(1)}, u32[]{:S(2)}, u32[]{:S(2)}) async-start(bf16[8,128,128]{2,1,0:T(8,128)(2,1)} %bitcast.176), calls=%async_computation.2 | async-start | bytes 524288 | tf_op jit(solution)/shard_map/all_to_all | solution.py:338
  86.2 140.6 %reduce-scatter.2.cloned.1.call-start = ((), (), s32[]{:S(2)}) async-start(), calls=%async_computation.8 | async-start | bytes 2703360 | tf_op jit(solution)/shard_map/reduce_scatter | solution.py:958
  98.0 4.2 %collective-permute-start.17 = (bf16[2,4,128,256]{3,2,1,0:T(8,128)(2,1)S(1)}, bf16[2,4,128,256]{3,2,1,0:T(8,128)(2,1)S(1)}, u32[]{:S(2)}, u32[]{:S(2)}) collective-permute-start(bf16[2,4,128,256]{3,2,1,0:T(8,128)(2,1)S(1)} %collective-permute-done.14.x_ref), channel_id=1, source_target_pairs={{0,1},{1,0},{2,3},{3,2},{4,5},{5,4},{6,7},{7,6},{8,9},{9,8},{10,11... | collective-permute-start | bytes 1572872 | tf_op jit(solution)/shard_map/ppermute | solution.py:330
  105.7 7.5 %collective-permute-start.18 = (bf16[128,1024]{1,0:T(8,128)(2,1)S(1)}, bf16[128,1024]{1,0:T(8,128)(2,1)S(1)}, u32[]{:S(2)}, u32[]{:S(2)}) collective-permute-start(bf16[128,1024]{1,0:T(8,128)(2,1)S(1)} %get-tuple-element.196.refs_0_), channel_id=1, source_target_pairs={{0,4},{4,0},{1,5},{5,1},{2,6},{6,2},{3,7},{7,3},{8,12},{12,8},{9,1... | collective-permute-start | bytes 786440 | tf_op jit(solution)/shard_map/ppermute | solution.py:330
  106.2 7.2 %collective-permute-start.19 = (bf16[128,1024]{1,0:T(8,128)(2,1)S(1)}, bf16[128,1024]{1,0:T(8,128)(2,1)S(1)}, u32[]{:S(2)}, u32[]{:S(2)}) collective-permute-start(bf16[128,1024]{1,0:T(8,128)(2,1)S(1)} %get-tuple-element.196.refs_0_), channel_id=1, source_target_pairs={{0,2},{2,0},{1,3},{3,1},{4,6},{6,4},{5,7},{7,5},{8,10},{10,8},{9,1... | collective-permute-start | bytes 786440 | tf_op jit(solution)/shard_map/ppermute | solution.py:330
  106.6 6.9 %collective-permute-start.20 = (bf16[128,1024]{1,0:T(8,128)(2,1)S(1)}, bf16[128,1024]{1,0:T(8,128)(2,1)S(1)}, u32[]{:S(2)}, u32[]{:S(2)}) collective-permute-start(bf16[128,1024]{1,0:T(8,128)(2,1)S(1)} %get-tuple-element.196.refs_0_), channel_id=1, source_target_pairs={{0,1},{1,0},{2,3},{3,2},{4,5},{5,4},{6,7},{7,6},{8,9},{9,8},{10,11... | collective-permute-start | bytes 786440 | tf_op jit(solution)/shard_map/ppermute | solution.py:330
  114.2 4.3 %collective-permute-start.21 = (bf16[64,1024]{1,0:T(8,128)(2,1)}, bf16[64,1024]{1,0:T(8,128)(2,1)S(1)}, u32[]{:S(2)}, u32[]{:S(2)}) collective-permute-start(bf16[64,1024]{1,0:T(8,128)(2,1)} %slice.243), channel_id=1, source_target_pairs={{0,4},{4,0},{1,5},{5,1},{2,6},{6,2},{3,7},{7,3},{8,12},{12,8},{9,1... | collective-permute-start | bytes 393224 | tf_op jit(solution)/shard_map/ppermute | solution.py:330
  115.7 4.3 %collective-permute-start.22 = (bf16[64,1024]{1,0:T(8,128)(2,1)}, bf16[64,1024]{1,0:T(8,128)(2,1)S(1)}, u32[]{:S(2)}, u32[]{:S(2)}) collective-permute-start(bf16[64,1024]{1,0:T(8,128)(2,1)} %slice.244), channel_id=1, source_target_pairs={{0,2},{2,0},{1,3},{3,1},{4,6},{6,4},{5,7},{7,5},{8,10},{10,8},{9,1... | collective-permute-start | bytes 393224 | tf_op jit(solution)/shard_map/ppermute | solution.py:330
  116.2 7.9 %collective-permute-start.23 = (bf16[2,128,1024]{2,1,0:T(8,128)(2,1)S(1)}, bf16[2,128,1024]{2,1,0:T(8,128)(2,1)S(1)}, u32[]{:S(2)}, u32[]{:S(2)}) collective-permute-start(bf16[2,128,1024]{2,1,0:T(8,128)(2,1)S(1)} %pad_maximum_fusion.5), channel_id=1, source_target_pairs={{0,1},{1,0},{2,3},{3,2},{4,5},{5,4},{6,7},{7,6},{8,9},{9,8},{10,11... | collective-permute-start | bytes 1572872 | tf_op jit(solution)/shard_map/ppermute | solution.py:330
  120.1 4.0 %collective-permute-start.24 = (bf16[2,64,1024]{2,1,0:T(8,128)(2,1)S(1)}, bf16[2,64,1024]{2,1,0:T(8,128)(2,1)}, u32[]{:S(2)}, u32[]{:S(2)}) collective-permute-start(bf16[2,64,1024]{2,1,0:T(8,128)(2,1)S(1)} %pad_maximum_fusion.7), channel_id=1, source_target_pairs={{0,1},{1,0},{2,3},{3,2},{4,5},{5,4},{6,7},{7,6},{8,9},{9,8},{10,11... | collective-permute-start | bytes 786440 | tf_op jit(solution)/shard_map/ppermute | solution.py:330
  133.9 6.9 %collective-permute-start.25 = (bf16[4,128,1024]{2,1,0:T(8,128)(2,1)}, bf16[4,128,1024]{2,1,0:T(8,128)(2,1)}, u32[]{:S(2)}, u32[]{:S(2)}) collective-permute-start(bf16[4,128,1024]{2,1,0:T(8,128)(2,1)} %get-tuple-element.204), channel_id=1, source_target_pairs={{0,1},{1,0},{2,3},{3,2},{4,5},{5,4},{6,7},{7,6},{8,9},{9,8},{10,11... | collective-permute-start | bytes 3145736 | tf_op jit(solution)/shard_map/ppermute | solution.py:330
  141.8 5.0 %collective-permute-start.26 = (bf16[64,1024]{1,0:T(8,128)(2,1)S(1)}, bf16[64,1024]{1,0:T(8,128)(2,1)S(1)}, u32[]{:S(2)}, u32[]{:S(2)}) collective-permute-start(bf16[64,1024]{1,0:T(8,128)(2,1)S(1)} %get-tuple-element.313), channel_id=1, source_target_pairs={{0,4},{4,0},{1,5},{5,1},{2,6},{6,2},{3,7},{7,3},{8,12},{12,8},{9,1... | collective-permute-start | bytes 393224 | tf_op jit(solution)/shard_map/ppermute | solution.py:330
  142.5 4.6 %collective-permute-start.27 = (bf16[64,1024]{1,0:T(8,128)(2,1)S(1)}, bf16[64,1024]{1,0:T(8,128)(2,1)S(1)}, u32[]{:S(2)}, u32[]{:S(2)}) collective-permute-start(bf16[64,1024]{1,0:T(8,128)(2,1)S(1)} %get-tuple-element.312), channel_id=1, source_target_pairs={{0,2},{2,0},{1,3},{3,1},{4,6},{6,4},{5,7},{7,5},{8,10},{10,8},{9,1... | collective-permute-start | bytes 393224 | tf_op jit(solution)/shard_map/ppermute | solution.py:330
  147.2 6.6 %collective-permute-start.29 = (bf16[128,1024]{1,0:T(8,128)(2,1)S(1)}, bf16[128,1024]{1,0:T(8,128)(2,1)S(1)}, u32[]{:S(2)}, u32[]{:S(2)}) collective-permute-start(bf16[128,1024]{1,0:T(8,128)(2,1)S(1)} %pad_maximum_fusion.9), channel_id=1, source_target_pairs={{0,4},{4,0},{1,5},{5,1},{2,6},{6,2},{3,7},{7,3},{8,12},{12,8},{9,1... | collective-permute-start | bytes 786440 | tf_op jit(solution)/shard_map/ppermute | solution.py:330
  148.3 6.3 %collective-permute-start.28 = (bf16[128,1024]{1,0:T(8,128)(2,1)S(1)}, bf16[128,1024]{1,0:T(8,128)(2,1)S(1)}, u32[]{:S(2)}, u32[]{:S(2)}) collective-permute-start(bf16[128,1024]{1,0:T(8,128)(2,1)S(1)} %pad_maximum_fusion.8), channel_id=1, source_target_pairs={{0,2},{2,0},{1,3},{3,1},{4,6},{6,4},{5,7},{7,5},{8,10},{10,8},{9,1... | collective-permute-start | bytes 786440 | tf_op jit(solution)/shard_map/ppermute | solution.py:330
  161.3 17.0 %collective-permute-start.30 = (bf16[2,2,4,32,1024]{4,3,2,1,0:T(8,128)(2,1)}, bf16[2,2,4,32,1024]{4,3,2,1,0:T(8,128)(2,1)}, u32[]{:S(2)}, u32[]{:S(2)}) collective-permute-start(bf16[2,2,4,32,1024]{4,3,2,1,0:T(8,128)(2,1)} %get-tuple-element.222), channel_id=1, source_target_pairs={{0,1},{1,0},{2,3},{3,2},{4,5},{5,4},{6,7},{7,6},{8,9},{9,8},{10,11... | collective-permute-start | bytes 3145736 | tf_op jit(solution)/shard_map/ppermute | solution.py:330
  163.8 14.5 %collective-permute-start.31 = (bf16[4,128,1024]{2,1,0:T(8,128)(2,1)}, bf16[4,128,1024]{2,1,0:T(8,128)(2,1)}, u32[]{:S(2)}, u32[]{:S(2)}) collective-permute-start(bf16[4,128,1024]{2,1,0:T(8,128)(2,1)} %get-tuple-element.223), channel_id=1, source_target_pairs={{0,1},{1,0},{2,3},{3,2},{4,5},{5,4},{6,7},{7,6},{8,9},{9,8},{10,11... | collective-permute-start | bytes 3145736 | tf_op jit(solution)/shard_map/ppermute | solution.py:330
  180.7 12.8 %collective-permute-start.32 = (bf16[2,4,32,1024]{3,2,1,0:T(8,128)(2,1)}, bf16[2,4,32,1024]{3,2,1,0:T(8,128)(2,1)S(1)}, u32[]{:S(2)}, u32[]{:S(2)}) collective-permute-start(bf16[2,4,32,1024]{3,2,1,0:T(8,128)(2,1)} %get-tuple-element.306), channel_id=1, source_target_pairs={{0,2},{2,0},{1,3},{3,1},{4,6},{6,4},{5,7},{7,5},{8,10},{10,8},{9,1... | collective-permute-start | bytes 1572872 | tf_op jit(solution)/shard_map/ppermute | solution.py:330
  193.5 7.3 %collective-permute-start.33 = (bf16[2,8,32,512]{3,2,1,0:T(8,128)(2,1)}, bf16[2,8,32,512]{3,2,1,0:T(8,128)(2,1)S(1)}, u32[]{:S(2)}, u32[]{:S(2)}) collective-permute-start(bf16[2,8,32,512]{3,2,1,0:T(8,128)(2,1)} %get-tuple-element.242), channel_id=1, source_target_pairs={{0,1},{1,0},{2,3},{3,2},{4,5},{5,4},{6,7},{7,6},{8,9},{9,8},{10,11... | collective-permute-start | bytes 1572872 | tf_op jit(solution)/shard_map/ppermute | solution.py:330
  199.3 8.1 %collective-permute-start.36 = (bf16[4,32,1024]{2,1,0:T(8,128)(2,1)S(1)}, bf16[4,32,1024]{2,1,0:T(8,128)(2,1)S(1)}, u32[]{:S(2)}, u32[]{:S(2)}) collective-permute-start(bf16[4,32,1024]{2,1,0:T(8,128)(2,1)S(1)} %get-tuple-element.321), channel_id=1, source_target_pairs={{0,4},{4,0},{1,5},{5,1},{2,6},{6,2},{3,7},{7,3},{8,12},{12,8},{9,1... | collective-permute-start | bytes 786440 | tf_op jit(solution)/shard_map/ppermute | solution.py:330
  200.9 7.7 %collective-permute-start.35 = (bf16[8,32,512]{2,1,0:T(8,128)(2,1)S(1)}, bf16[8,32,512]{2,1,0:T(8,128)(2,1)S(1)}, u32[]{:S(2)}, u32[]{:S(2)}) collective-permute-start(bf16[8,32,512]{2,1,0:T(8,128)(2,1)S(1)} %get-tuple-element.322), channel_id=1, source_target_pairs={{0,2},{2,0},{1,3},{3,1},{4,6},{6,4},{5,7},{7,5},{8,10},{10,8},{9,1... | collective-permute-start | bytes 786440 | tf_op jit(solution)/shard_map/ppermute | solution.py:330
  204.5 15.4 %collective-permute-start.34 = (bf16[2,128,1024]{2,1,0:T(8,128)(2,1)}, bf16[2,128,1024]{2,1,0:T(8,128)(2,1)}, u32[]{:S(2)}, u32[]{:S(2)}) collective-permute-start(bf16[2,128,1024]{2,1,0:T(8,128)(2,1)} %get-tuple-element.243), channel_id=1, source_target_pairs={{0,2},{2,0},{1,3},{3,1},{4,6},{6,4},{5,7},{7,5},{8,10},{10,8},{9,1... | collective-permute-start | bytes 1572872 | tf_op jit(solution)/shard_map/ppermute | solution.py:330
  204.9 18.9 %collective-permute-start.42 = (bf16[4,128,512]{2,1,0:T(8,128)(2,1)}, bf16[4,128,512]{2,1,0:T(8,128)(2,1)}, u32[]{:S(2)}, u32[]{:S(2)}) collective-permute-start(bf16[4,128,512]{2,1,0:T(8,128)(2,1)} %get-tuple-element.263), channel_id=1, source_target_pairs={{0,4},{4,0},{1,5},{5,1},{2,6},{6,2},{3,7},{7,3},{8,12},{12,8},{9,1... | collective-permute-start | bytes 1572872 | tf_op jit(solution)/shard_map/ppermute | solution.py:330
  208.7 19.8 %collective-permute-start.39 = (bf16[32,1024]{1,0:T(8,128)(2,1)S(1)}, bf16[32,1024]{1,0:T(8,128)(2,1)S(1)}, u32[]{:S(2)}, u32[]{:S(2)}) collective-permute-start(bf16[32,1024]{1,0:T(8,128)(2,1)S(1)} %get-tuple-element.327), channel_id=1, source_target_pairs={{0,8},{8,16},{16,24},{24,0},{1,9},{9,17},{17,25},{25,1},{2,10},{10... | collective-permute-start | bytes 196616 | tf_op jit(solution)/shard_map/ppermute | solution.py:334
  209.7 18.8 %collective-permute-start.40 = (bf16[32,1024]{1,0:T(8,128)(2,1)S(1)}, bf16[32,1024]{1,0:T(8,128)(2,1)S(1)}, u32[]{:S(2)}, u32[]{:S(2)}) collective-permute-start(bf16[32,1024]{1,0:T(8,128)(2,1)S(1)} %get-tuple-element.326), channel_id=1, source_target_pairs={{0,16},{8,24},{16,0},{24,8},{1,17},{9,25},{17,1},{25,9},{2,18},{10... | collective-permute-start | bytes 196616 | tf_op jit(solution)/shard_map/ppermute | solution.py:334
  213.7 18.0 %collective-permute-start.38 = (bf16[4,128,512]{2,1,0:T(8,128)(2,1)}, bf16[4,128,512]{2,1,0:T(8,128)(2,1)}, u32[]{:S(2)}, u32[]{:S(2)}) collective-permute-start(bf16[4,128,512]{2,1,0:T(8,128)(2,1)} %get-tuple-element.249), channel_id=1, source_target_pairs={{0,4},{4,0},{1,5},{5,1},{2,6},{6,2},{3,7},{7,3},{8,12},{12,8},{9,1... | collective-permute-start | bytes 1572872 | tf_op jit(solution)/shard_map/ppermute | solution.py:330
  215.6 29.9 %copy-start.28 = (bf16[4,128,512]{2,1,0:T(8,128)(2,1)S(1)}, bf16[4,128,512]{2,1,0:T(8,128)(2,1)}, u32[]{:S(2)}) copy-start(bf16[4,128,512]{2,1,0:T(8,128)(2,1)} %get-tuple-element.265) | copy-start | bytes 1572868
  215.6 16.1 %all-to-all-start.4 = ((bf16[8,32,512]{2,1,0:T(8,128)(2,1)}), bf16[8,32,512]{2,1,0:T(8,128)(2,1)S(1)}, u32[]{:S(2)}, u32[]{:S(2)}) async-start(bf16[8,32,512]{2,1,0:T(8,128)(2,1)} %add_convert_fusion.5), calls=%async_computation.4 | async-start | bytes 524288 | tf_op jit(solution)/shard_map/all_to_all | solution.py:338
  219.9 10.9 %collective-permute-start.41 = (bf16[32,1024]{1,0:T(8,128)(2,1)S(1)}, bf16[32,1024]{1,0:T(8,128)(2,1)S(1)}, u32[]{:S(2)}, u32[]{:S(2)}) collective-permute-start(bf16[32,1024]{1,0:T(8,128)(2,1)S(1)} %get-tuple-element.325), channel_id=1, source_target_pairs={{0,24},{8,0},{16,8},{24,16},{1,25},{9,1},{17,9},{25,17},{2,26},{10... | collective-permute-start | bytes 196616 | tf_op jit(solution)/shard_map/ppermute | solution.py:334
  223.8 13.6 %collective-permute-start.37 = (bf16[128,1024]{1,0:T(8,128)(2,1)S(1)}, bf16[128,1024]{1,0:T(8,128)(2,1)}, u32[]{:S(2)}, u32[]{:S(2)}) collective-permute-start(bf16[128,1024]{1,0:T(8,128)(2,1)S(1)} %fusion.16), channel_id=1, source_target_pairs={{0,4},{4,0},{1,5},{5,1},{2,6},{6,2},{3,7},{7,3},{8,12},{12,8},{9,1... | collective-permute-start | bytes 786440 | tf_op jit(solution)/shard_map/ppermute | solution.py:330
  228.5 21.1 %collective-permute-start.43 = (bf16[128,512]{1,0:T(8,128)(2,1)}, bf16[128,512]{1,0:T(8,128)(2,1)S(1)}, u32[]{:S(2)}, u32[]{:S(2)}) collective-permute-start(bf16[128,512]{1,0:T(8,128)(2,1)} %get-tuple-element.319), channel_id=1, source_target_pairs={{0,8},{8,16},{16,24},{24,0},{1,9},{9,17},{17,25},{25,1},{2,10},{10... | collective-permute-start | bytes 393224 | tf_op jit(solution)/shard_map/ppermute | solution.py:334
  228.5 33.9 %collective-permute-start.44 = (bf16[128,512]{1,0:T(8,128)(2,1)}, bf16[128,512]{1,0:T(8,128)(2,1)S(1)}, u32[]{:S(2)}, u32[]{:S(2)}) collective-permute-start(bf16[128,512]{1,0:T(8,128)(2,1)} %get-tuple-element.318), channel_id=1, source_target_pairs={{0,16},{8,24},{16,0},{24,8},{1,17},{9,25},{17,1},{25,9},{2,18},{10... | collective-permute-start | bytes 393224 | tf_op jit(solution)/shard_map/ppermute | solution.py:334
  230.8 31.6 %collective-permute-start.45 = (bf16[128,512]{1,0:T(8,128)(2,1)}, bf16[128,512]{1,0:T(8,128)(2,1)}, u32[]{:S(2)}, u32[]{:S(2)}) collective-permute-start(bf16[128,512]{1,0:T(8,128)(2,1)} %get-tuple-element.317), channel_id=1, source_target_pairs={{0,24},{8,0},{16,8},{24,16},{1,25},{9,1},{17,9},{25,17},{2,26},{10... | collective-permute-start | bytes 393224 | tf_op jit(solution)/shard_map/ppermute | solution.py:334
  238.0 14.9 %all-to-all-start.5 = ((f32[32,1,128]{2,1,0:T(1,128)}), f32[32,1,128]{2,1,0:T(1,128)S(1)}, u32[]{:S(2)}, u32[]{:S(2)}) async-start(f32[32,1,128]{2,1,0:T(1,128)} %broadcast_in_dim.68), calls=%async_computation.6 | async-start | bytes 32768 | tf_op jit(solution)/shard_map/all_to_all | solution.py:338
  247.3 15.1 %collective-permute-start.46 = (bf16[128,512]{1,0:T(8,128)(2,1)}, bf16[128,512]{1,0:T(8,128)(2,1)S(1)}, u32[]{:S(2)}, u32[]{:S(2)}) collective-permute-start(bf16[128,512]{1,0:T(8,128)(2,1)} %get-tuple-element.316), channel_id=1, source_target_pairs={{0,8},{8,16},{16,24},{24,0},{1,9},{9,17},{17,25},{25,1},{2,10},{10... | collective-permute-start | bytes 393224 | tf_op jit(solution)/shard_map/ppermute | solution.py:334
  248.6 13.8 %collective-permute-start.47 = (bf16[128,512]{1,0:T(8,128)(2,1)}, bf16[128,512]{1,0:T(8,128)(2,1)}, u32[]{:S(2)}, u32[]{:S(2)}) collective-permute-start(bf16[128,512]{1,0:T(8,128)(2,1)} %get-tuple-element.315), channel_id=1, source_target_pairs={{0,16},{8,24},{16,0},{24,8},{1,17},{9,25},{17,1},{25,9},{2,18},{10... | collective-permute-start | bytes 393224 | tf_op jit(solution)/shard_map/ppermute | solution.py:334
  249.6 12.8 %collective-permute-start.48 = (bf16[128,512]{1,0:T(8,128)(2,1)}, bf16[128,512]{1,0:T(8,128)(2,1)}, u32[]{:S(2)}, u32[]{:S(2)}) collective-permute-start(bf16[128,512]{1,0:T(8,128)(2,1)} %get-tuple-element.314), channel_id=1, source_target_pairs={{0,24},{8,0},{16,8},{24,16},{1,25},{9,1},{17,9},{25,17},{2,26},{10... | collective-permute-start | bytes 393224 | tf_op jit(solution)/shard_map/ppermute | solution.py:334
  252.9 12.5 %all-to-all-start.6 = ((bf16[8,32,512]{2,1,0:T(8,128)(2,1)}), bf16[8,32,512]{2,1,0:T(8,128)(2,1)S(1)}, u32[]{:S(2)}, u32[]{:S(2)}) async-start(bf16[8,32,512]{2,1,0:T(8,128)(2,1)} %bitcast.54), calls=%async_computation.7 | async-start | bytes 524288 | tf_op jit(solution)/shard_map/all_to_all | solution.py:338
  (38 other events, 267.8 us)
Sparse Core Ops, SparseCore 0:
  50.6 51.3 all-gather.2
  164.0 49.8 reduce-scatter.1
where the time goes:
time: 279 us; the launch traced here: 276 us
  starting transfers between devices  94.1 us (34%)
  Pallas kernels  57.8 us (21%)
  waiting for transfers between devices  55.8 us (20%)
  other arithmetic  22.4 us (8%)
  local copies, waits for them, and re-layouts  16.3 us (6%)
  between operations  15.5 us (6%)
  blocking collectives  14.4 us (5%)
    pallas_call x11, Pallas kernels, call(): pl.pallas_call(kernel, out_shape=[jax.ShapeDtypeStruct(s, d) for s, d in...  57.8 us
    ppermute x34, starting transfers between devices, exchange(): return lax.ppermute(v, axis, [(0, 1), (1, 0)])  36.6 us
    all_to_all x6, starting transfers between devices, swap(): return lax.all_to_all(v, axes, 0, 0, tiled=True)  34.3 us
    all_to_all x6, waiting for transfers between devices, swap(): return lax.all_to_all(v, axes, 0, 0, tiled=True)  24.4 us
    ppermute x34, waiting for transfers between devices, exchange(): return lax.ppermute(v, axis, [(0, 1), (1, 0)])  24.3 us
    ppermute x15, starting transfers between devices, shift(): return lax.ppermute(v, axis, [(i, (i - k) % n_line) for i in range(n_line)])  23.1 us
    all_to_all x1, blocking collectives, swap(): return lax.all_to_all(v, axes, 0, 0, tiled=True)  14.4 us
    convert_element_type x13, other arithmetic, add_low(): (keep.astype(jnp.float32) + got.astype(jnp.float32)).astype(jnp.bfloat16)  13.3 us
  transfers between devices with their start and end apart: 57, of which 20 were waited for; matrix products, arithmetic and copies ran while one was open for 10% of the time, Pallas kernels for 14%

commit v1 on v0

--- a/solution.py
+++ b/solution.py
@@ -531,81 +531,83 @@
     mlp_ref[...] = layer_norm(resid, vec[2:3], vec[3:4]).astype(low)
 
 
-def down_of(ff_all, down):
-    n_line, own = ff_all.shape[0], down.shape[0] // ff_all.shape[0]
-    ff = down.shape[0]
-    up_rows = ff_all.shape[1] - down.shape[1] * own // ff
-    for k in range(n_line):
-        for h in range(down.shape[1] // ff):
-            down[k * own : (k + 1) * own, h * ff : (h + 1) * ff] = ff_all[k, up_rows + h * own : up_rows + (h + 1) * own, :]
-
-
-def feed_kernel(*refs):
+def both_down(parts, down):
+    ff = down.shape[0] // 2
+    n_line = parts[0].shape[0]
+    own = ff // n_line
+    n_half = down.shape[1] // ff
+    up_rows = parts[0].shape[1] - n_half * own
+    for c, part in enumerate(parts):
+        for k in range(n_line):
+            for h in range(n_half):
+                rows = slice(up_rows + h * own, up_rows + (h + 1) * own)
+                down[c * ff + k * own : c * ff + (k + 1) * own, h * ff : (h + 1) * ff] = part[k, rows, :]
+
+
+def feed_kernel(
+    m_own, m_y, m_x, m_d0, m_d1, cot_0, cot_1, ff_own, ff_other, bias_own, bias_other,
+    norm_own, norm_y, norm_x, norm_d, hidden_ref, pre_ref, mlp_ref, down, up,
+):
     low, f32 = jnp.bfloat16, jnp.float32
-    m_own, m_y, m_x, m_d0, m_d1, m_c, m_cyx, m_cd = refs[:8]
-    cots, ff_all, bias = refs[8:12], refs[12], refs[13]
-    keep_ref, give_ref, hidden_ref, pre_ref, mlp_ref, down, up = refs[14:]
     tokens, width = m_own.shape
     half = tokens // 2
-    ff = hidden_ref.shape[1]
-    n_line = ff_all.shape[0]
+    n_line, _, ff = ff_own.shape
     up_rows = width // n_line
-    for k in range(n_line):
-        up[k * up_rows : (k + 1) * up_rows, :] = ff_all[k, :up_rows, :]
-    down_of(ff_all, down)
-    blocks = (m_own[...], m_y[...], m_x[...], None, m_c[...], m_cyx[0], m_cyx[1])
-    for b, block in enumerate(blocks):
-        if block is not None:
-            mlp_ref[b * tokens : (b + 1) * tokens, :] = block
+    for c, part in enumerate((ff_own, ff_other)):
+        for k in range(n_line):
+            up[k * up_rows : (k + 1) * up_rows, c * ff : (c + 1) * ff] = part[k, :up_rows, :]
+    both_down((ff_own, ff_other), down)
+    bias = jnp.concatenate([bias_own[...], bias_other[...]], 1)
+    for n, block in enumerate((m_own, m_y, m_x)):
+        mlp_ref[n * tokens : (n + 1) * tokens, :] = block[...]
     mlp_ref[3 * tokens : 3 * tokens + half, :] = m_d0[...]
-    mlp_ref[3 * tokens + half : 4 * tokens, :] = m_d1[...]
-    mlp_ref[7 * tokens : 7 * tokens + half, :] = m_cd[0]
-    mlp_ref[7 * tokens + half : 8 * tokens, :] = m_cd[1]
-    for t in range(4):
+    mlp_ref[3 * tokens + half :, :] = m_d1[...]
+    for t in range(2):
         span = slice(2 * t * tokens, 2 * (t + 1) * tokens)
-        pre = jnp.dot(mlp_ref[span, :], up[...], preferred_element_type=f32) + bias[...]
-        cdf = 0.5 * (1.0 + lax.erf(pre * 0.7071067811865476))
-        pdf = jnp.exp(-0.5 * pre * pre) * 0.3989422804014327
-        hidden_ref[span, :] = (pre * cdf).astype(low)
-        cot = cots[t][...].reshape(2 * tokens, width)
-        grad = (contract(cot, down[...], 1, 1) * (cdf + pre * pdf)).astype(low)
-        pre_ref[span, :] = grad
-        part = contract(grad, up[...], 1, 1).astype(low).reshape(2, tokens, width)
-        to = keep_ref if t < 2 else give_ref
-        to[2 * (t % 2) : 2 * (t % 2) + 2] = part
-
-
-def feed_grad_kernel(mlp_ref, pre_ref, hidden_ref, cot_0, cot_1, cot_2, cot_3, terms_ref):
+        cot = (cot_0, cot_1)[t][...].reshape(2 * tokens, width)
+        grads = []
+        for c in range(2):
+            cut = slice(c * ff, (c + 1) * ff)
+            pre = jnp.dot(mlp_ref[span, :], up[:, cut], preferred_element_type=f32) + bias[:, cut]
+            cdf = 0.5 * (1.0 + lax.erf(pre * 0.7071067811865476))
+            pdf = jnp.exp(-0.5 * pre * pre) * 0.3989422804014327
+            hidden_ref[span, cut] = (pre * cdf).astype(low)
+            grad = (contract(cot, down[cut, :], 1, 1) * (cdf + pre * pdf)).astype(low)
+            pre_ref[span, cut] = grad
+            grads = grads + [grad]
+        part = contract(jnp.concatenate(grads, 1), up[...], 1, 1).astype(low)
+        first, second = ((norm_own, norm_y), (norm_x, norm_d))[t]
+        first[...] = part[:tokens]
+        second[...] = part[tokens:]
+
+
+def feed_grad_kernel(mlp_ref, pre_ref, hidden_ref, cot_0, cot_1, keep_ref, give_ref):
     low, f32 = jnp.bfloat16, jnp.float32
     seq, width = mlp_ref.shape
-    ff = pre_ref.shape[1]
-    n_line = terms_ref.shape[0]
-    own, up_rows = ff // n_line, width // n_line
-    n_half = width // ff
-    for k in range(n_line):
-        up = contract(mlp_ref[:, k * up_rows : (k + 1) * up_rows], pre_ref[...], 0, 0)
-        terms_ref[k, :up_rows, :] = up.astype(low)
-        for h in range(n_half):
-            part = slice(k * own, (k + 1) * own)
-            cut = slice(h * ff, (h + 1) * ff)
-            cot = [ref[:, :, cut].reshape(seq // 4, ff) for ref in (cot_0, cot_1, cot_2, cot_3)]
-            total = contract(hidden_ref[:, part], jnp.concatenate(cot, 0), 0, 0)
-            terms_ref[k, up_rows + h * own : up_rows + (h + 1) * own, :] = total.astype(low)
-    sums = jnp.sum(pre_ref[...].astype(f32), 0, keepdims=True)
-    pad = terms_ref.shape[1] - up_rows - n_half * own
-    for k in range(n_line):
-        line = jnp.concatenate([sums[:, k * own : (k + 1) * own], jnp.zeros((1, ff - own), f32)], 1)
-        terms_ref[k, up_rows + n_half * own :, :] = jnp.broadcast_to(line, (pad, ff)).astype(low)
-
-
-def result_kernel(hidden_ref, ff_all, keep_ref, give_ref, down):
-    down_of(ff_all, down)
-    tokens = keep_ref.shape[1]
-    for t in range(4):
-        span = slice(2 * t * tokens, 2 * (t + 1) * tokens)
-        part = jnp.dot(hidden_ref[span, :], down[...], preferred_element_type=jnp.float32)
-        to = keep_ref if t < 2 else give_ref
-        to[2 * (t % 2) : 2 * (t % 2) + 2] = part.astype(jnp.bfloat16).reshape(2, tokens, down.shape[1])
+    n_line, _, ff = keep_ref.shape
+    own, up_rows, n_half = ff // n_line, width // n_line, width // ff
+    cot = jnp.concatenate([ref[...].reshape(seq // 2, width) for ref in (cot_0, cot_1)], 0)
+    for c, ref in enumerate((keep_ref, give_ref)):
+        cut = slice(c * ff, (c + 1) * ff)
+        down = contract(hidden_ref[:, cut], cot, 0, 0).astype(low)
+        sums = jnp.sum(pre_ref[:, cut].astype(f32), 0, keepdims=True)
+        pad = ref.shape[1] - up_rows - n_half * own
+        up = contract(mlp_ref[...], pre_ref[:, cut], 0, 0).astype(low)
+        for k in range(n_line):
+            ref[k, :up_rows, :] = up[k * up_rows : (k + 1) * up_rows]
+            for h in range(n_half):
+                part = down[k * own : (k + 1) * own, h * ff : (h + 1) * ff]
+                ref[k, up_rows + h * own : up_rows + (h + 1) * own, :] = part
+            line = jnp.concatenate([sums[:, k * own : (k + 1) * own], jnp.zeros((1, ff - own), f32)], 1)
+            ref[k, up_rows + n_half * own :, :] = jnp.broadcast_to(line, (pad, ff)).astype(low)
+
+
+def result_kernel(hidden_ref, ff_own, ff_other, keep_ref, give_ref, down):
+    both_down((ff_own, ff_other), down)
+    half = hidden_ref.shape[0] // 2
+    for t, ref in enumerate((keep_ref, give_ref)):
+        part = jnp.dot(hidden_ref[t * half : (t + 1) * half, :], down[...], preferred_element_type=jnp.float32)
+        ref[...] = part.astype(jnp.bfloat16).reshape(ref.shape)
 
 
 def norm_back_kernel(
@@ -646,7 +648,7 @@
 
 def backward_kernel(
     table, slopes, back_ref, qkv_ref, att_t, lse_ref, start_ref, normed, w_ref, x_ref, sums_ref,
-    keep_ref, give_ref, keep_a, give_a, keep_b, give_b, mixed_ref, back, d_key, d_value, moved, made,
+    keep_ref, give_ref, in_keep, in_give, mixed_ref, back, d_key, d_value, moved, made,
 ):
     f32, low = jnp.float32, jnp.bfloat16
     seq, cols = back_ref.shape
@@ -705,14 +707,11 @@
         shift_sum = shift_sum + jnp.sum(grad, 0, keepdims=True)
         moved[t * tile : (t + 1) * tile, :] = grad.astype(low)
     n_line = spans // 4
-    cut = keep_a.shape[2]
-    for y, (ref_a, ref_b) in enumerate(((keep_a, keep_b), (give_a, give_b))):
+    for y, ref in enumerate((in_keep, in_give)):
         for z in range(n_line):
             for u in range(2):
                 part = pl.ds(pl.multiple_of(table[(y * n_line + z) * 2 + u] * half, half), half)
-                to = slice(u * half, (u + 1) * half)
-                ref_a[z, to, :] = moved[part, :cut]
-                ref_b[z, to, :] = moved[part, cut:]
+                ref[z, u * half : (u + 1) * half, :] = moved[part, :]
     row = lax.broadcasted_iota(jnp.int32, (8, width), 0)
     sums = jnp.where(row == 0, gain_sum, jnp.where(row == 1, shift_sum, sums_ref[...]))
     here = table[2 * spans + 4]
@@ -758,11 +757,11 @@
     squared = squared + jnp.sum(jnp.sum(jnp.square(out), 0, keepdims=True), keepdims=True)
     qkv = jnp.sum(jnp.square(qkv_ref[:, :, : 3 * cols].astype(f32)), 0)
     squared = squared + jnp.sum(jnp.sum(qkv, 0, keepdims=True), keepdims=True)
-    square_ref[...] = jnp.broadcast_to(squared, square_ref.shape)
+    square_ref[...] = jnp.broadcast_to(squared.reshape(1, 1, 1), square_ref.shape)
 
 
 def clip_of(squares):
-    norm = jnp.sqrt(jnp.sum(jnp.sum(squares[...], 0, keepdims=True)[:, 0:1], keepdims=True))
+    norm = jnp.sqrt(jnp.sum(squares[...], 0)[:, 0:1])
     return norm, jnp.minimum(1.0, max_norm / (norm + 1e-06))
 
 
@@ -813,7 +812,7 @@
 in_vmem = pl.BlockSpec(memory_space=pltpu.VMEM)
 
 
-def call(kernel, n_scalar, args, shapes, scratch=(), cost=1, limit=48):
+def call(kernel, n_scalar, args, shapes, scratch=(), cost=1, limit=60):
     return pl.pallas_call(
         kernel,
         out_shape=[jax.ShapeDtypeStruct(s, d) for s, d in shapes],
@@ -888,8 +887,11 @@
     cot_two = jnp.stack([cot_low, cot_y])
     cot_x = exchange(cot_two, "x")
     seg_all = first_got[:, 0:2, 3 * cols + 64 :].reshape(seq_len).astype(jnp.int32)
-    bias_all = first_got[:, 2:4, 3 * cols + 64 :].reshape(nz, 2, ff_own)
-    up_low = lax.dynamic_index_in_dim(bias_all, yi, 1, keepdims=False).reshape(1, ff).astype(f32)
+    up_low = []
+    for got in (first_got, first_c):
+        bias_all = got[:, 2:4, 3 * cols + 64 :].reshape(nz, 2, ff_own)
+        bias_all = lax.dynamic_index_in_dim(bias_all, yi, 1, keepdims=False)
+        up_low = up_low + [bias_all.reshape(1, ff).astype(f32)]
     pair_all = first_got[:, 4, 3 * cols + 64].astype(jnp.int32)
     start = jnp.sum((seg_all[:, None] < seg_all[None, :]).astype(jnp.int32), 0, keepdims=True)
     slot_block = jnp.stack([pair_all, 2 * n_ctx - 1 - pair_all], 1)
@@ -910,63 +912,53 @@
     )
 
     out_y = exchange(out_z, "y")
-    cot_c = exchange(cot_two, "c")
     pieces = (first_got, first_x, first_c, first_cx)
     blocks = [field_low, pair_own, pair_line] + line + rest
     attended, att_t, qkv_low, lse, normed_one, seq_rows, qkv_w, vec = attend_forward(
         table, slopes, blocks, pieces, start, cols
     )
-    attended, out_y, cot_c = gate(attended.reshape(n_ctx, tokens, cols), out_y, cot_c)
+    attended, out_y = gate(attended.reshape(n_ctx, tokens, cols), out_y)
 
     attended_low = swap(attended, ctx)
     out_zy = jnp.stack([out_z, out_y])
     out_x = exchange(out_zy, "x")
     out_c_two = exchange(out_zy, "c")
-    cot_cx = exchange(cot_x, "c")
-    attended_low, out_x, out_c_two, cot_cx = gate(attended_low, out_x, out_c_two, cot_cx)
-    cots = [cot_two, cot_x, cot_c, cot_cx]
+    attended_low, out_x, out_c_two = gate(attended_low, out_x, out_c_two)
+    cots = [cot_two, cot_x]
     shapes = [((tokens, width), f32), ((tokens, width), low), ((width, width), low)]
     parts = [table, attended_low, out_zy, out_x, out_c_two, exchange(out_x, "c"), field_low, vec]
     resid, mlp_low, out_w = call(project_kernel, 1, parts, shapes)
 
     mlp_y = exchange(mlp_low, "y")
     mlp_x = exchange(mlp_low, "x")
-    mlp_c = exchange(mlp_low, "c")
-    mlp_y, mlp_x, mlp_c = gate(mlp_y, mlp_x, mlp_c)
+    mlp_y, mlp_x = gate(mlp_y, mlp_x)
     mlp_d0 = exchange(mlp_x[:half], "y")
     mlp_d1 = exchange(mlp_y[half:], "x")
-    mlp_cyx = exchange(jnp.stack([mlp_y, mlp_x]), "c")
-    mlp_cd = exchange(jnp.stack([mlp_d0, mlp_d1]), "c")
-    four = ((4, tokens, width), low)
-    shapes = [four, four, ((8 * tokens, ff), low), ((8 * tokens, ff), low), ((8 * tokens, width), low)]
-    scratch = [((ff, width), low), ((width, ff), low)]
-    norm_keep, norm_give, hidden, grad_pre, mlp_in = call(
-        feed_kernel,
-        0,
-        [mlp_low, mlp_y, mlp_x, mlp_d0, mlp_d1, mlp_c, mlp_cyx, mlp_cd] + cots + [ff_all, up_low],
-        shapes,
-        scratch,
-        limit=60,
-    )
-
+    ff_other = exchange(after(ff_all, mlp_low), "c")
+    mlp_d0, mlp_d1, ff_other = gate(mlp_d0, mlp_d1, ff_other)
+    four = 4 * tokens
+    one = ((tokens, width), low)
+    shapes = [one] * 4 + [((four, 2 * ff), low)] * 2 + [((four, width), low)]
+    scratch = [((2 * ff, width), low), ((width, 2 * ff), low)]
+    rows_in = [mlp_low, mlp_y, mlp_x, mlp_d0, mlp_d1] + cots + [ff_all, ff_other] + up_low
+    norm_own, norm_y, norm_x, norm_d, hidden, grad_pre, mlp_in = call(
+        feed_kernel, 0, rows_in, shapes, scratch, limit=60
+    )
+
+    norm_d0 = exchange(norm_d[:half], "y")
+    norm_d1 = exchange(norm_d[half:], "x")
     n_ff = 8 * rows + n_half * ff_own
-    ff_terms = call(
-        feed_grad_kernel, 0, [mlp_in, grad_pre, hidden] + cots, [((nz, n_ff + 16, ff), low)], (), 1, 60
-    )[0]
-    norm_c_got = exchange(norm_give, "c")
-    norm_c_got, ff_terms = gate(norm_c_got, ff_terms)
+    ff_keep, ff_give = call(
+        feed_grad_kernel, 0, [mlp_in, grad_pre, hidden] + cots, [((nz, n_ff + 16, ff), low)] * 2, (), 1, 60
+    )
+    norm_d0, norm_d1, ff_give = gate(norm_d0, norm_d1, ff_give)
+    norm_y = jnp.concatenate([norm_y[:half], add_low(norm_y[half:], norm_d1)], 0)
+    norm_x = jnp.concatenate([add_low(norm_x[:half], norm_d0), norm_x[half:]], 0)
+    norm_y, norm_x, ff_keep = gate(norm_y, norm_x, ff_keep)
+    norm_y, norm_x = exchange(norm_y, "y"), exchange(norm_x, "x")
+    ff_terms = add_low(ff_keep, exchange(ff_give, "c"))
     ff_sum = lax.psum_scatter(ff_terms, "z", scatter_dimension=0, tiled=True)[0]
-
-    norm_d0 = exchange(add_low(norm_keep[3, :half], norm_c_got[3, :half]), "y")
-    norm_d1 = exchange(add_low(norm_keep[3, half:], norm_c_got[3, half:]), "x")
-    norm_own, norm_y, norm_x = (add_low(norm_keep[k], norm_c_got[k]) for k in range(3))
-    norm_d0, norm_d1, norm_own, norm_y, norm_x = gate(norm_d0, norm_d1, norm_own, norm_y, norm_x)
-    norm_y = exchange(jnp.concatenate([norm_y[:half], add_low(norm_y[half:], norm_d1)], 0), "y")
-    norm_x = exchange(jnp.concatenate([add_low(norm_x[:half], norm_d0), norm_x[half:]], 0), "x")
-    result_keep, result_give = call(
-        result_kernel, 0, [after(hidden, norm_d0), ff_all], [four, four], [((ff, width), low)]
-    )
-    norm_x, norm_y, result_keep, result_give = gate(norm_x, norm_y, result_keep, result_give)
+    norm_x, norm_y, ff_terms = gate(norm_x, norm_y, ff_terms)
     shapes = [((tokens, width), f32), ((n_ctx, tokens, cols), low), ((8, width), f32)]
     shapes = shapes + [((2, 2, nz, rows, width), low)] * 2
     grad_resid, back_low, resid_sums, out_keep, out_give = call(
@@ -979,13 +971,18 @@
 
     back_all = swap(back_low, ctx)
     out_c_got = exchange(out_give, "c")
-    result_c_got = exchange(result_give, "c")
-    back_all, out_c_got, result_c_got = gate(back_all, out_c_got, result_c_got)
+    result_keep, result_give = call(
+        result_kernel,
+        0,
+        [after(hidden, back_low), ff_all, ff_other],
+        [((2, tokens, width), low)] * 2,
+        [((2 * ff, width), low)],
+    )
+    back_all, out_c_got, result_keep, result_give = gate(back_all, out_c_got, result_keep, result_give)
 
     out_x_got = exchange(add_low(out_keep[1], out_c_got[1]), "x")
     shapes = [((2, n_ctx, rows, 4 * cols), low)] * 2
-    part = width // 2
-    shapes = shapes + [((nz, tokens, part), low)] * 2 + [((nz, tokens, width - part), low)] * 2
+    shapes = shapes + [((nz, tokens, width), low)] * 2
     scratch = [((seq_len, 3 * cols), low), ((seq_len, cols), low), ((seq_len, cols), f32), ((seq_len, cols), f32)]
     scratch = scratch + [((seq_len, width), low), ((width, 4 * cols), low)]
     back_all = back_all.reshape(seq_len, cols)
@@ -999,8 +996,7 @@
         60,
     )
     *made, out_x_got = gate(*made, out_x_got)
-    qkv_keep, qkv_give = made[:2]
-    in_keep, in_give = made[2::2], made[3::2]
+    qkv_keep, qkv_give, in_keep, in_give = made
 
     qkv_c_got = exchange(qkv_give, "c")
     qkv_c = add_low(qkv_keep[0], qkv_c_got[0])
@@ -1008,34 +1004,26 @@
     out_c = add_low(out_keep[0], out_c_got[0])
     out_two = add_low(out_c[0], out_x_got[0])
     out_y_got = exchange(add_low(out_c[1], out_x_got[1]), "y")
-    in_a = exchange(after(in_give[0], qkv_c), "y")
-    result_send = add_low(result_keep[2:], result_c_got[2:])
-    result_x = exchange(after(result_send, qkv_c), "x")
-    qkv_x_got, qkv_c, out_y_got, result_send = gate(qkv_x_got, qkv_c, out_y_got, result_send)
+    in_got = exchange(after(in_give, qkv_c), "y")
+    result_x = exchange(after(result_give, qkv_c), "x")
+    qkv_x_got, qkv_c, out_y_got = gate(qkv_x_got, qkv_c, out_y_got)
     qkv_x = add_low(qkv_c, qkv_x_got)
 
     qkv_got = swap(qkv_x, ctx)
+    out_y_got = after(out_y_got, qkv_x)
     out_own = add_low(out_two[0], out_y_got[0])
     out_moved = [shift(add_low(out_two[k], out_y_got[k]), "z", nz, -k) for k in range(1, nz)]
-    in_b = exchange(after(in_give[1], qkv_c), "y")
-    in_a = after(in_a, qkv_x)
-    in_za = [shift(add_low(in_keep[0][k], in_a[k]), "z", nz, -k) for k in range(1, nz)]
     up_send = after(ff_sum, qkv_x)[: 8 * rows].reshape(8, rows, ff)
     result_x = after(result_x, qkv_x)
-    result_c = add_low(result_keep[:2], result_c_got[:2])
-    result_y = exchange(add_low(result_c[1], result_x[1]), "y")
-    qkv_got, in_b, up_send, *gated = gate(qkv_got, in_b, up_send, *out_moved, out_own)
-    out_moved = gated[: nz - 1]
-    shapes = [((8, 128), f32), ((rows, width), f32), ((8, rows), f32)]
+    result_y = exchange(add_low(result_keep[1], result_x[1]), "y")
+    qkv_got, in_got, up_send, *out_moved = gate(qkv_got, in_got, up_send, *out_moved)
+    shapes = [((4 * n_ctx, 1, 128), f32), ((rows, width), f32), ((8, rows), f32)]
     squared, grad_out_own, grad_vec_own = call(
-        square_kernel, 1, [table, qkv_got, ff_sum, out_own, *out_moved], shapes
-    )
-
-    squares = swap(jnp.broadcast_to(squared[:1], (4 * n_ctx, 128)), every)
-    in_zb = [shift(add_low(in_keep[1][k], in_b[k]), "z", nz, -k) for k in range(1, nz)]
-    result_y = after(result_y, squared)
-    result = resid + result_c[0].astype(f32) + result_x[0].astype(f32) + result_y.astype(f32) + vec[7]
-    result, squares = gate(result.astype(low), squares)
+        square_kernel, 1, [table, qkv_got, ff_sum, out_own, *out_moved], shapes, limit=48
+    )
+
+    squares = swap(squared, every)
+    in_z = [shift(add_low(in_keep[k], in_got[k]), "z", nz, -k) for k in range(1, nz)]
     up_got = swap(after(up_send, squares), plane)
     masters = [w_qkv, w_out, w_down, up_bias.reshape(1, ff_own), vectors]
     firsts = [first_qkv, first_out, first_down, first_bias.reshape(1, ff_own), first_vectors]
@@ -1050,13 +1038,11 @@
     ups = call(adam_up_kernel, 0, [squares, up_got, w_up, first_up, second_up], [(w_up.shape, f32)] * 4, limit=60)
     results = results[:8] + list(ups) + results[8:]
 
-    *late, _ = gate(*in_za, *in_zb, grad_norm)
-    sum_a = in_keep[0][0].astype(f32) + in_a[0].astype(f32)
-    sum_b = in_keep[1][0].astype(f32) + in_b[0].astype(f32)
-    for k in range(nz - 1):
-        sum_a = sum_a + late[k].astype(f32)
-        sum_b = sum_b + late[nz - 1 + k].astype(f32)
-    own_grads = jnp.concatenate([sum_a, sum_b], 1)
+    result_y = after(result_y, squares)
+    result = (resid + result_keep[0].astype(f32) + result_x[0].astype(f32) + result_y.astype(f32) + vec[7]).astype(low)
+    own_grads = in_keep[0].astype(f32) + in_got[0].astype(f32)
+    for other in gate(*in_z, grad_norm)[:-1]:
+        own_grads = own_grads + other.astype(f32)
     norm_one_back = jax.vjp(lambda v: layer_norm(v, vec[0], vec[1]), field)[1]
     in_grad = grad_resid + norm_one_back(own_grads)[0]
     return (result[None], in_grad[None], grad_norm[0, 0], *results)

time: 279 us -> 277 us (level)
  waiting for transfers between devices: 55.8 us -> 66.8 us
  starting transfers between devices: 94.1 us -> 88.4 us
  Pallas kernels: 57.8 us -> 62.8 us
  other arithmetic: 22.4 us -> 17.4 us
  local copies, waits for them, and re-layouts: 16.3 us -> 12.6 us
    ppermute x15 -> x12, waiting for transfers between devices: 7.01 us -> 22.8 us  [shift(): return lax.ppermute(v, axis, [(i, (i - k) % n_line) for i in range(n_line)])]
    ppermute x15 -> x12, starting transfers between devices: 23.1 us -> 16.5 us  [shift(): return lax.ppermute(v, axis, [(i, (i - k) % n_line) for i in range(n_line)])]
    pallas_call x11, Pallas kernels: 57.8 us -> 62.8 us  [call(): pl.pallas_call(kernel, out_shape=[jax.ShapeDtypeStruct(s, d) for s, d in...]
    convert_element_type x13 -> x10, other arithmetic: 13.3 us -> 9.05 us  [add_low(): (keep.astype(jnp.float32) + got.astype(jnp.float32)).astype(jnp.bfloat16)]
    ppermute x34 -> x28, waiting for transfers between devices: 24.3 us -> 20.7 us  [exchange(): return lax.ppermute(v, axis, [(0, 1), (1, 0)])]
    unnamed x90 -> x84, local copies, waits for them, and re-layouts: 9.61 us -> 6.04 us
    all_to_all x6, starting transfers between devices: 34.3 us -> 37.4 us  [swap(): return lax.all_to_all(v, axes, 0, 0, tiled=True)]
    ppermute x34 -> x28, starting transfers between devices: 36.6 us -> 34.5 us  [exchange(): return lax.ppermute(v, axis, [(0, 1), (1, 0)])]
  transfers between devices with their start and end apart: 57 -> 48, of which waited for: 20 -> 21; matrix products, arithmetic and copies ran while one was open for 10% -> 8% of each run, Pallas kernels for 14% -> 19%
where the time goes in v1:
time: 277 us; the launch traced here: 276 us
  starting transfers between devices  88.4 us (32%)
  waiting for transfers between devices  66.8 us (24%)
  Pallas kernels  62.8 us (23%)
  other arithmetic  17.4 us (6%)
  between operations  15.4 us (6%)
  local copies, waits for them, and re-layouts  12.6 us (5%)
  blocking collectives  12.4 us (4%)
    pallas_call x11, Pallas kernels, call(): pl.pallas_call(kernel, out_shape=[jax.ShapeDtypeStruct(s, d) for s, d in...  62.8 us
    all_to_all x6, starting transfers between devices, swap(): return lax.all_to_all(v, axes, 0, 0, tiled=True)  37.4 us
    ppermute x28, starting transfers between devices, exchange(): return lax.ppermute(v, axis, [(0, 1), (1, 0)])  34.5 us
    all_to_all x6, waiting for transfers between devices, swap(): return lax.all_to_all(v, axes, 0, 0, tiled=True)  23.3 us
    ppermute x12, waiting for transfers between devices, shift(): return lax.ppermute(v, axis, [(i, (i - k) % n_line) for i in range(n_line)])  22.8 us
    ppermute x28, waiting for transfers between devices, exchange(): return lax.ppermute(v, axis, [(0, 1), (1, 0)])  20.7 us
    ppermute x12, starting transfers between devices, shift(): return lax.ppermute(v, axis, [(i, (i - k) % n_line) for i in range(n_line)])  16.5 us
    all_to_all x1, blocking collectives, swap(): return lax.all_to_all(v, axes, 0, 0, tiled=True)  12.4 us
  transfers between devices with their start and end apart: 48, of which 21 were waited for; matrix products, arithmetic and copies ran while one was open for 8% of the time, Pallas kernels for 19%

profile of v1, /device:TPU:11, one launch (start us, length us, event | category | flops | bytes accessed | tf_op | source)
XLA Modules:
  0.0 275.9 jit_solution(5106282748190833041)
XLA Ops:
  7.9 2.4 shard_map.421
  10.3 5.9 %all-to-all-start = ((bf16[8,32,512]{2,1,0:T(8,128)(2,1)}), bf16[8,32,512]{2,1,0:T(8,128)(2,1)S(1)}, u32[]{:S(2)}, u32[]{:S(2)}) async-start(bf16[8,32,512]{2,1,0:T(8,128)(2,1)} %get-tuple-element.159), calls=%async_computation | async-start | bytes 524288 | tf_op jit(solution)/shard_map/all_to_all | solution.py:338
  16.2 2.4 collective-permute-start.2
  18.6 2.1 collective-permute-start.3
  20.7 1.2 collective-permute-start
  22.1 7.0 %all-to-all-done.refs_9_ = bf16[8,32,512]{2,1,0:T(8,128)(2,1)S(1)} async-done(((bf16[8,32,512]{2,1,0:T(8,128)(2,1)}), bf16[8,32,512]{2,1,0:T(8,128)(2,1)S(1)}, u32[]{:S(2)}, u32[]{:S(2)}) %all-to-all-start) | async-done | bytes 262176 | tf_op jit(solution)/shard_map/all_to_all | solution.py:338
  29.1 6.4 %all-to-all-start.1 = ((bf16[8,32,512]{2,1,0:T(8,128)(2,1)}), bf16[8,32,512]{2,1,0:T(8,128)(2,1)S(1)}, u32[]{:S(2)}, u32[]{:S(2)}) async-start(bf16[8,32,512]{2,1,0:T(8,128)(2,1)} %get-tuple-element.160), calls=%async_computation.1 | async-start | bytes 524288 | tf_op jit(solution)/shard_map/all_to_all | solution.py:338
  36.1 4.7 %all-to-all-done.1 = bf16[8,32,512]{2,1,0:T(8,128)(2,1)S(1)} async-done(((bf16[8,32,512]{2,1,0:T(8,128)(2,1)}), bf16[8,32,512]{2,1,0:T(8,128)(2,1)S(1)}, u32[]{:S(2)}, u32[]{:S(2)}) %all-to-all-start.1) | async-done | bytes 262176 | tf_op jit(solution)/shard_map/all_to_all | solution.py:338
  41.9 3.2 %collective-permute-start.10 = (bf16[3,128,256]{2,1,0:T(8,128)(2,1)S(1)}, bf16[3,128,256]{2,1,0:T(8,128)(2,1)}, u32[]{:S(2)}, u32[]{:S(2)}) collective-permute-start(bf16[3,128,256]{2,1,0:T(8,128)(2,1)S(1)} %pad_maximum_fusion.8), channel_id=1, source_target_pairs={{0,16},{8,24},{16,0},{24,8},{1,17},{9,25},{17,1},{25,9},{2,18},{10... | collective-permute-start | bytes 589832 | tf_op jit(solution)/shard_map/ppermute | solution.py:334
  48.6 1.6 collective-permute-start.11
  51.1 6.2 %collective-permute-done.10.refs_7_ = bf16[3,128,256]{2,1,0:T(8,128)(2,1)} collective-permute-done((bf16[3,128,256]{2,1,0:T(8,128)(2,1)S(1)}, bf16[3,128,256]{2,1,0:T(8,128)(2,1)}, u32[]{:S(2)}, u32[]{:S(2)}) %collective-permute-start.10) | collective-permute-done | bytes 196640 | tf_op jit(solution)/shard_map/ppermute | solution.py:334
  57.3 3.5 %collective-permute-start.5 = (bf16[8,32,512]{2,1,0:T(8,128)(2,1)S(1)}, bf16[8,32,512]{2,1,0:T(8,128)(2,1)S(1)}, u32[]{:S(2)}, u32[]{:S(2)}) collective-permute-start(bf16[8,32,512]{2,1,0:T(8,128)(2,1)S(1)} %all-to-all-done.refs_9_), channel_id=1, source_target_pairs={{0,1},{1,0},{2,3},{3,2},{4,5},{5,4},{6,7},{7,6},{8,9},{9,8},{10,11... | collective-permute-start | bytes 786440 | tf_op jit(solution)/shard_map/ppermute | solution.py:330
  62.8 6.6 %collective-permute-done.11.refs_8_ = bf16[3,128,256]{2,1,0:T(8,128)(2,1)S(1)} collective-permute-done((bf16[3,128,256]{2,1,0:T(8,128)(2,1)S(1)}, bf16[3,128,256]{2,1,0:T(8,128)(2,1)S(1)}, u32[]{:S(2)}, u32[]{:S(2)}) %collective-permute-start.11) | collective-permute-done | bytes 196640 | tf_op jit(solution)/shard_map/ppermute | solution.py:334
  70.4 11.5 %shard_map.422 = (bf16[1024,128]{1,0:T(8,128)(2,1)}, f32[128,1024]{1,0:T(8,128)}, bf16[1024,384]{1,0:T(8,128)(2,1)}, f32[8,1024]{1,0:T(8,128)}, bf16[1024,1024]{...) custom-call(s32[41]{0:T(128)} %concatenate.13.meta.table, ...), custom_call_target="tpu_custom_call" | custom-call | flops 8999999488 | bytes 8999999488 | tf_op jit(solution)/shard_map/pallas_call | solution.py:816
  82.7 7.0 %collective-permute-start.14 = (bf16[2,4,128,256]{3,2,1,0:T(8,128)(2,1)S(1)}, bf16[2,4,128,256]{3,2,1,0:T(8,128)(2,1)S(1)}, u32[]{:S(2)}, u32[]{:S(2)}) collective-permute-start(bf16[2,4,128,256]{3,2,1,0:T(8,128)(2,1)S(1)} %pad_maximum_fusion.4.own_ref), channel_id=1, source_target_pairs={{0,1},{1,0},{2,3},{3,2},{4,5},{5,4},{6,7},{7,6},{8,9},{9,8},{10,11... | collective-permute-start | bytes 1572872 | tf_op jit(solution)/shard_map/ppermute | solution.py:330
  89.6 12.4 %all_to_all.35.att = bf16[8,128,128]{2,1,0:T(8,128)(2,1)} all-to-all(bf16[8,128,128]{2,1,0:T(8,128)(2,1)} %bitcast.150), channel_id=1, replica_groups=mesh['z'=4,'y'=2,'x'=2,'c'=2] {'z','y'}, dimensions={0} | all-to-all | bytes 524288 | tf_op jit(solution)/shard_map/all_to_all | solution.py:338
  102.0 2.5 collective-permute-start.15
  104.5 1.5 collective-permute-done.15.cx_ref
  106.8 3.9 %shard_map.423 = (f32[128,1024]{1,0:T(8,128)}, bf16[128,1024]{1,0:T(8,128)(2,1)}, bf16[1024,1024]{1,0:T(8,128)(2,1)}) custom-call(s32[41]{0:T(128)} %concatenate.13.meta.table, bf16[8,128,128]{2,1,0:T(8,128)(2,1)} %all_to_all.35.att, bf16[2,4,128,256]{3,2,1,0:T(8,128)(2,1)} %copy-done.12, bf16[2,4,128,256]{3,2,1,0:T(8,128)(2,1)} %copy-done.20, ...), custom_call_target="tpu_custom_call" | custom-call | flops 1 | bytes 1 | tf_op jit(solution)/shard_map/pallas_call | solution.py:816
  113.6 6.5 %collective-permute-done.16.m_y = bf16[128,1024]{1,0:T(8,128)(2,1)S(1)} collective-permute-done((bf16[128,1024]{1,0:T(8,128)(2,1)}, bf16[128,1024]{1,0:T(8,128)(2,1)S(1)}, u32[]{:S(2)}, u32[]{:S(2)}) %collective-permute-start.16) | collective-permute-done | bytes 262176 | tf_op jit(solution)/shard_map/ppermute | solution.py:330
  120.1 1.2 collective-permute-start.18
  122.7 1.3 collective-permute-done.18.m_d0
  124.0 1.5 collective-permute-done.19.m_d1
  126.9 7.9 %shard_map.424 = (bf16[128,1024]{1,0:T(8,128)(2,1)}, bf16[128,1024]{1,0:T(8,128)(2,1)}, bf16[128,1024]{1,0:T(8,128)(2,1)}, bf16[128,1024]{1,0:T(8,128)(2,1)}, bf...) custom-call(bf16[128,1024]{1,0:T(8,128)(2,1)} %get-tuple-element.188.m_own, ...), custom_call_target="tpu_custom_call" | custom-call | flops 1 | bytes 1 | tf_op jit(solution)/shard_map/pallas_call | solution.py:816
  136.9 5.9 %shard_map.425 = (bf16[4,528,512]{2,1,0:T(8,128)(2,1)}, bf16[4,528,512]{2,1,0:T(8,128)(2,1)}) custom-call(bf16[512,1024]{1,0:T(8,128)(2,1)} %get-tuple-element.200.mlp_ref, bf16[512,1024]{1,0:T(8,128)(2,1)} %get-tuple-element.201.pre_ref, bf16[512,1024]{1,0:T(8,128)(2,1)} %get-tuple-element.217.hidden_ref, bf16[2,128,1024]{2,1,0:T(8,128)(2,1)} %copy-done.8, ...), custom_call_target="tpu_custom_call" | custom-call | flops 1 | bytes 1 | tf_op jit(solution)/shard_map/pallas_call | solution.py:816
  142.8 2.8 %collective-permute-start.25 = (bf16[4,528,512]{2,1,0:T(8,128)(2,1)}, bf16[4,528,512]{2,1,0:T(8,128)(2,1)S(1)}, u32[]{:S(2)}, u32[]{:S(2)}) collective-permute-start(bf16[4,528,512]{2,1,0:T(8,128)(2,1)} %get-tuple-element.211), channel_id=1, source_target_pairs={{0,1},{1,0},{2,3},{3,2},{4,5},{5,4},{6,7},{7,6},{8,9},{9,8},{10,11... | collective-permute-start | bytes 6488072 | tf_op jit(solution)/shard_map/ppermute | solution.py:330
  146.6 1.3 collective-permute-start.24
  148.0 1.8 collective-permute-done.25
  149.8 2.0 add_convert_fusion
  151.7 2.1 collective-permute-done.23.got_x
  154.9 5.6 %shard_map.426 = (f32[128,1024]{1,0:T(8,128)}, bf16[8,128,128]{2,1,0:T(8,128)(2,1)}, f32[8,1024]{1,0:T(8,128)}, bf16[2,2,4,32,1024]{4,3,2,1,0:T(8,128)(2,1)}, bf16[2,2,4,32,1024]{4,3,2,1,0:T(8,128)(2,1)}) custom-call(s32[41]{0:T(128)} %concatenate.13.meta.table, bf16[128,1024]{1,0:T(8,128)(2,1)} %get-tuple-element.197.own, bf16[128,1024]{1,0:T(8,128)(2,1)} %copy-done.25, ...), custom_call_target="tpu_custom_call" | custom-call | flops 1 | bytes 1 | tf_op jit(solution)/shard_map/pallas_call | solution.py:816
  160.5 1.1 collective-permute-start.26
  161.6 5.4 %all-to-all-start.3 = ((bf16[8,128,128]{2,1,0:T(8,128)(2,1)}), bf16[8,128,128]{2,1,0:T(8,128)(2,1)S(1)}, u32[]{:S(2)}, u32[]{:S(2)}) async-start(bf16[8,128,128]{2,1,0:T(8,128)(2,1)} %get-tuple-element.215), calls=%async_computation.3 | async-start | bytes 524288 | tf_op jit(solution)/shard_map/all_to_all | solution.py:338
  167.0 4.7 %shard_map.427 = (bf16[2,128,1024]{2,1,0:T(8,128)(2,1)}, bf16[2,128,1024]{2,1,0:T(8,128)(2,1)}) custom-call(bf16[512,1024]{1,0:T(8,128)(2,1)} %get-tuple-element.217.hidden_ref, bf16[4,512,512]{2,1,0:T(8,128)(2,1)} %bitcast.144, bf16[4,512,512]{2,1,0:T(8,128)(2,1)} %copy-done.7), custom_call_target="tpu_custom_call" | custom-call | flops 1 | bytes 1 | tf_op jit(solution)/shard_map/pallas_call | solution.py:816
  171.7 8.7 %all-to-all-done.3 = bf16[8,128,128]{2,1,0:T(8,128)(2,1)S(1)} async-done(((bf16[8,128,128]{2,1,0:T(8,128)(2,1)}), bf16[8,128,128]{2,1,0:T(8,128)(2,1)S(1)}, u32[]{:S(2)}, u32[]{:S(2)}) %all-to-all-start.3) | async-done | bytes 262176 | tf_op jit(solution)/shard_map/all_to_all | solution.py:338
  181.4 11.9 %shard_map.428 = (bf16[2,8,32,512]{3,2,1,0:T(8,128)(2,1)}, bf16[2,8,32,512]{3,2,1,0:T(8,128)(2,1)}, bf16[4,128,1024]{2,1,0:T(8,128)(2,1)}, bf16[4,128,1024]{2,1,0:T(8,128)(2,1)}) custom-call(s32[41]{0:T(128)} %concatenate.13.meta.table, f32[2]{0:T(128)} %multiply_exponential_fusion.slopes, bf16[1024,128]{1,0:T(8,128)(2,1)} %bitcast.149, ...), custom_call_target="tpu_custom_call" | custom-call | flops 8999999488 | bytes 8999999488 | tf_op jit(solution)/shard_map/pallas_call | solution.py:816
  193.8 1.4 collective-permute-start.28
  195.4 1.2 collective-permute-start.31
  197.0 1.2 fusion.15
  199.9 1.2 collective-permute-start.29
  201.0 2.5 collective-permute-done.31
  203.5 2.2 collective-permute-done.30
  206.5 6.5 %all-to-all-start.4 = ((bf16[8,32,512]{2,1,0:T(8,128)(2,1)}), bf16[8,32,512]{2,1,0:T(8,128)(2,1)S(1)}, u32[]{:S(2)}, u32[]{:S(2)}) async-start(bf16[8,32,512]{2,1,0:T(8,128)(2,1)} %add_convert_fusion.7), calls=%async_computation.4 | async-start | bytes 524288 | tf_op jit(solution)/shard_map/all_to_all | solution.py:338
  213.0 1.6 fusion.29
  214.7 1.2 collective-permute-start.34
  216.7 1.5 collective-permute-start.36
  218.2 1.7 fusion.16
  219.9 1.2 collective-permute-start.32
  222.0 1.7 slice.205
  223.7 2.0 collective-permute-done.36.refs_2_
  225.7 3.0 %all-to-all-done.4.qkv_ref.refs_1_ = bf16[8,32,512]{2,1,0:T(8,128)(2,1)S(1)} async-done(((bf16[8,32,512]{2,1,0:T(8,128)(2,1)}), bf16[8,32,512]{2,1,0:T(8,128)(2,1)S(1)}, u32[]{:S(2)}, u32[]{:S(2)}) %all-to-all-start.4) | async-done | bytes 262176 | tf_op jit(solution)/shard_map/all_to_all | solution.py:338
  228.7 1.1 copy-done
  229.8 1.4 shard_map.429
  232.5 7.6 %all-to-all-start.5 = ((f32[32,1,128]{2,1,0:T(1,128)}), f32[32,1,128]{2,1,0:T(1,128)S(1)}, u32[]{:S(2)}, u32[]{:S(2)}) async-start(f32[32,1,128]{2,1,0:T(1,128)} %get-tuple-element.252), calls=%async_computation.6 | async-start | bytes 32768 | tf_op jit(solution)/shard_map/all_to_all | solution.py:338
  240.1 1.1 fusion.19
  241.2 1.2 collective-permute-start.37
  242.4 1.2 collective-permute-start.38
  243.6 1.3 collective-permute-start.39
  244.8 5.6 %all-to-all-start.6 = ((bf16[8,32,512]{2,1,0:T(8,128)(2,1)}), bf16[8,32,512]{2,1,0:T(8,128)(2,1)}, u32[]{:S(2)}, u32[]{:S(2)}) async-start(bf16[8,32,512]{2,1,0:T(8,128)(2,1)} %bitcast.146), calls=%async_computation.7 | async-start | bytes 524288 | tf_op jit(solution)/shard_map/all_to_all | solution.py:338
  250.5 4.5 %shard_map.430 = (f32[1,1]{1,0:T(1,128)}, f32[32,3072]{1,0:T(8,128)}, f32[32,3072]{1,0:T(8,128)}, f32[32,3072]{1,0:T(8,128)}, f32[32,3072]{1,0:T(8,128)}, /*inde...) custom-call(f32[32,1,128]{2,1,0:T(1,128)} %copy-done.35, ...), custom_call_target="tpu_custom_call" | custom-call | flops 1 | bytes 1 | tf_op jit(solution)/shard_map/pallas_call | solution.py:816
  255.0 2.0 fusion.21
  256.9 3.3 %shard_map.431 = (f32[32,4096]{1,0:T(8,128)}, f32[32,4096]{1,0:T(8,128)}, f32[32,4096]{1,0:T(8,128)}, f32[32,4096]{1,0:T(8,128)}) custom-call(f32[32,1,128]{2,1,0:T(1,128)} %copy-done.35, bf16[8,32,512]{2,1,0:T(8,128)(2,1)} %all-to-all-done.6.up_ref, f32[32,4096]{1,0:T(8,128)} %refs_0_.1, f32[32,4096]{1,0:T(8,128)} %refs_1_.1, f32[32,4096]{1,0:T(8,128)} %refs_2_.1), custom_call_target="tpu_custom_call" | custom-call | flops 1 | bytes 1 | tf_op jit(solution)/shard_map/pallas_call | solution.py:816
  260.2 4.7 %collective-permute-done.38 = bf16[128,1024]{1,0:T(8,128)(2,1)S(1)} collective-permute-done((bf16[128,1024]{1,0:T(8,128)(2,1)}, bf16[128,1024]{1,0:T(8,128)(2,1)S(1)}, u32[]{:S(2)}, u32[]{:S(2)}) %collective-permute-start.38) | collective-permute-done | bytes 262176 | tf_op jit(solution)/shard_map/ppermute | solution.py:334
  264.9 2.5 collective-permute-done.39
  (193 shorter events, 29.6 us)
Async XLA Ops:
  7.2 8.9 %copy-start.5 = (bf16[1,128,1024]{2,1,0:T(8,128)(2,1)S(1)}, bf16[1,128,1024]{2,1,0:T(8,128)(2,1)}, u32[]{:S(2)}) copy-start(bf16[1,128,1024]{2,1,0:T(8,128)(2,1)} %param.22) | copy-start | bytes 786436
  7.2 13.5 %copy-start.9 = (bf16[1,128,1024]{2,1,0:T(8,128)(2,1)S(1)}, bf16[1,128,1024]{2,1,0:T(8,128)(2,1)}, u32[]{:S(2)}) copy-start(bf16[1,128,1024]{2,1,0:T(8,128)(2,1)} %param.23) | copy-start | bytes 786436
  10.3 30.5 %copy-start.30 = (bf16[2,128,512]{2,1,0:T(8,128)(2,1)S(1)}, bf16[2,128,512]{2,1,0:T(8,128)(2,1)}, u32[]{:S(2)}) copy-start(bf16[2,128,512]{2,1,0:T(8,128)(2,1)} %get-tuple-element.161) | copy-start | bytes 786436
  10.3 18.8 %all-to-all-start = ((bf16[8,32,512]{2,1,0:T(8,128)(2,1)}), bf16[8,32,512]{2,1,0:T(8,128)(2,1)S(1)}, u32[]{:S(2)}, u32[]{:S(2)}) async-start(bf16[8,32,512]{2,1,0:T(8,128)(2,1)} %get-tuple-element.159), calls=%async_computation | async-start | bytes 524288 | tf_op jit(solution)/shard_map/all_to_all | solution.py:338
  16.2 25.6 %copy-start.31 = (bf16[128,256]{1,0:T(8,128)(2,1)S(1)}, bf16[128,256]{1,0:T(8,128)(2,1)}, u32[]{:S(2)}) copy-start(bf16[128,256]{1,0:T(8,128)(2,1)} %get-tuple-element.168) | copy-start | bytes 196612
  16.2 25.5 %collective-permute-start.1 = (bf16[128,768]{1,0:T(8,128)(2,1)S(1)}, bf16[128,768]{1,0:T(8,128)(2,1)S(1)}, u32[]{:S(2)}, u32[]{:S(2)}) collective-permute-start(bf16[128,768]{1,0:T(8,128)(2,1)S(1)} %slice.226), channel_id=1, source_target_pairs={{0,24},{8,0},{16,8},{24,16},{1,25},{9,1},{17,9},{25,17},{2,26},{10... | collective-permute-start | bytes 589832 | tf_op jit(solution)/shard_map/ppermute | solution.py:334
  16.2 25.4 %collective-permute-start.2 = (bf16[128,768]{1,0:T(8,128)(2,1)S(1)}, bf16[128,768]{1,0:T(8,128)(2,1)S(1)}, u32[]{:S(2)}, u32[]{:S(2)}) collective-permute-start(bf16[128,768]{1,0:T(8,128)(2,1)S(1)} %slice.226), channel_id=1, source_target_pairs={{0,16},{8,24},{16,0},{24,8},{1,17},{9,25},{17,1},{25,9},{2,18},{10... | collective-permute-start | bytes 589832 | tf_op jit(solution)/shard_map/ppermute | solution.py:334
  18.6 23.1 %collective-permute-start.3 = (bf16[128,768]{1,0:T(8,128)(2,1)S(1)}, bf16[128,768]{1,0:T(8,128)(2,1)S(1)}, u32[]{:S(2)}, u32[]{:S(2)}) collective-permute-start(bf16[128,768]{1,0:T(8,128)(2,1)S(1)} %slice.226), channel_id=1, source_target_pairs={{0,8},{8,16},{16,24},{24,0},{1,9},{9,17},{17,25},{25,1},{2,10},{10... | collective-permute-start | bytes 589832 | tf_op jit(solution)/shard_map/ppermute | solution.py:334
  20.7 20.9 %collective-permute-start = (bf16[2,128,1024]{2,1,0:T(8,128)(2,1)S(1)}, bf16[2,128,1024]{2,1,0:T(8,128)(2,1)S(1)}, u32[]{:S(2)}, u32[]{:S(2)}) collective-permute-start(bf16[2,128,1024]{2,1,0:T(8,128)(2,1)S(1)} %pad_maximum_fusion.2), channel_id=1, source_target_pairs={{0,4},{4,0},{1,5},{5,1},{2,6},{6,2},{3,7},{7,3},{8,12},{12,8},{9,1... | collective-permute-start | bytes 1572872 | tf_op jit(solution)/shard_map/ppermute | solution.py:330
  29.1 28.2 %copy-start.24 = (bf16[8,32,512]{2,1,0:T(8,128)(2,1)}, bf16[8,32,512]{2,1,0:T(8,128)(2,1)S(1)}, u32[]{:S(2)}) copy-start(bf16[8,32,512]{2,1,0:T(8,128)(2,1)S(1)} %all-to-all-done.refs_9_) | copy-start | bytes 786436
  29.1 11.7 %all-to-all-start.1 = ((bf16[8,32,512]{2,1,0:T(8,128)(2,1)}), bf16[8,32,512]{2,1,0:T(8,128)(2,1)S(1)}, u32[]{:S(2)}, u32[]{:S(2)}) async-start(bf16[8,32,512]{2,1,0:T(8,128)(2,1)} %get-tuple-element.160), calls=%async_computation.1 | async-start | bytes 524288 | tf_op jit(solution)/shard_map/all_to_all | solution.py:338
  35.5 75.2 %all-gather.3.cloned.1.call-start = ((), (), s32[]{:S(2)}) async-start(), calls=%async_computation.9 | async-start | bytes 2621440 | tf_op jit(solution)/shard_map/all_gather | solution.py:880
  41.7 28.0 %copy-start.23 = (bf16[128,1024]{1,0:T(8,128)(2,1)}, bf16[128,1024]{1,0:T(8,128)(2,1)S(1)}, u32[]{:S(2)}) copy-start(bf16[128,1024]{1,0:T(8,128)(2,1)S(1)} %get-tuple-element.306.refs_1_) | copy-start | bytes 786436
  41.8 6.8 %collective-permute-start.9 = (bf16[3,128,256]{2,1,0:T(8,128)(2,1)S(1)}, bf16[3,128,256]{2,1,0:T(8,128)(2,1)S(1)}, u32[]{:S(2)}, u32[]{:S(2)}) collective-permute-start(bf16[3,128,256]{2,1,0:T(8,128)(2,1)S(1)} %pad_maximum_fusion.8), channel_id=1, source_target_pairs={{0,24},{8,0},{16,8},{24,16},{1,25},{9,1},{17,9},{25,17},{2,26},{10... | collective-permute-start | bytes 589832 | tf_op jit(solution)/shard_map/ppermute | solution.py:334
  41.9 15.4 %collective-permute-start.10 = (bf16[3,128,256]{2,1,0:T(8,128)(2,1)S(1)}, bf16[3,128,256]{2,1,0:T(8,128)(2,1)}, u32[]{:S(2)}, u32[]{:S(2)}) collective-permute-start(bf16[3,128,256]{2,1,0:T(8,128)(2,1)S(1)} %pad_maximum_fusion.8), channel_id=1, source_target_pairs={{0,16},{8,24},{16,0},{24,8},{1,17},{9,25},{17,1},{25,9},{2,18},{10... | collective-permute-start | bytes 589832 | tf_op jit(solution)/shard_map/ppermute | solution.py:334
  45.1 24.5 %collective-permute-start.8 = (bf16[3,128,768]{2,1,0:T(8,128)(2,1)S(1)}, bf16[3,128,768]{2,1,0:T(8,128)(2,1)}, u32[]{:S(2)}, u32[]{:S(2)}) collective-permute-start(bf16[3,128,768]{2,1,0:T(8,128)(2,1)S(1)} %pad_maximum_fusion), channel_id=1, source_target_pairs={{0,4},{4,0},{1,5},{5,1},{2,6},{6,2},{3,7},{7,3},{8,12},{12,8},{9,1... | collective-permute-start | bytes 1769480 | tf_op jit(solution)/shard_map/ppermute | solution.py:330
  45.4 15.5 %collective-permute-start.4 = (bf16[8,32,512]{2,1,0:T(8,128)(2,1)S(1)}, bf16[8,32,512]{2,1,0:T(8,128)(2,1)}, u32[]{:S(2)}, u32[]{:S(2)}) collective-permute-start(bf16[8,32,512]{2,1,0:T(8,128)(2,1)S(1)} %all-to-all-done.refs_9_), channel_id=1, source_target_pairs={{0,2},{2,0},{1,3},{3,1},{4,6},{6,4},{5,7},{7,5},{8,10},{10,8},{9,1... | collective-permute-start | bytes 786440 | tf_op jit(solution)/shard_map/ppermute | solution.py:330
  46.0 35.9 %copy-start.8 = (bf16[2,128,1024]{2,1,0:T(8,128)(2,1)}, bf16[2,128,1024]{2,1,0:T(8,128)(2,1)S(1)}, u32[]{:S(2)}) copy-start(bf16[2,128,1024]{2,1,0:T(8,128)(2,1)S(1)} %pad_maximum_fusion.3.cot_0) | copy-start | bytes 1572868
  46.0 23.6 %collective-permute-start.7 = (bf16[2,128,1024]{2,1,0:T(8,128)(2,1)S(1)}, bf16[2,128,1024]{2,1,0:T(8,128)(2,1)S(1)}, u32[]{:S(2)}, u32[]{:S(2)}) collective-permute-start(bf16[2,128,1024]{2,1,0:T(8,128)(2,1)S(1)} %pad_maximum_fusion.3.cot_0), channel_id=1, source_target_pairs={{0,2},{2,0},{1,3},{3,1},{4,6},{6,4},{5,7},{7,5},{8,10},{10,8},{9,1... | collective-permute-start | bytes 1572872 | tf_op jit(solution)/shard_map/ppermute | solution.py:330
  47.0 175.0 %reduce-scatter.2.cloned.1.call-start = ((), (), s32[]{:S(2)}) async-start(), calls=%async_computation.8 | async-start | bytes 2703360 | tf_op jit(solution)/shard_map/reduce_scatter | solution.py:960
  48.6 21.1 %copy-start.38 = (bf16[3,128,256]{2,1,0:T(8,128)(2,1)}, bf16[3,128,256]{2,1,0:T(8,128)(2,1)S(1)}, u32[]{:S(2)}) copy-start(bf16[3,128,256]{2,1,0:T(8,128)(2,1)S(1)} %collective-permute-done.9.refs_6_) | copy-start | bytes 589828
  48.6 20.9 %collective-permute-start.11 = (bf16[3,128,256]{2,1,0:T(8,128)(2,1)S(1)}, bf16[3,128,256]{2,1,0:T(8,128)(2,1)S(1)}, u32[]{:S(2)}, u32[]{:S(2)}) collective-permute-start(bf16[3,128,256]{2,1,0:T(8,128)(2,1)S(1)} %pad_maximum_fusion.8), channel_id=1, source_target_pairs={{0,8},{8,16},{16,24},{24,0},{1,9},{9,17},{17,25},{25,1},{2,10},{10... | collective-permute-start | bytes 589832 | tf_op jit(solution)/shard_map/ppermute | solution.py:334
  57.3 12.2 %collective-permute-start.5 = (bf16[8,32,512]{2,1,0:T(8,128)(2,1)S(1)}, bf16[8,32,512]{2,1,0:T(8,128)(2,1)S(1)}, u32[]{:S(2)}, u32[]{:S(2)}) collective-permute-start(bf16[8,32,512]{2,1,0:T(8,128)(2,1)S(1)} %all-to-all-done.refs_9_), channel_id=1, source_target_pairs={{0,1},{1,0},{2,3},{3,2},{4,5},{5,4},{6,7},{7,6},{8,9},{9,8},{10,11... | collective-permute-start | bytes 786440 | tf_op jit(solution)/shard_map/ppermute | solution.py:330
  60.9 8.7 %collective-permute-start.6 = (bf16[8,32,512]{2,1,0:T(8,128)(2,1)}, bf16[8,32,512]{2,1,0:T(8,128)(2,1)S(1)}, u32[]{:S(2)}, u32[]{:S(2)}) collective-permute-start(bf16[8,32,512]{2,1,0:T(8,128)(2,1)} %collective-permute-done.4.refs_10_), channel_id=1, source_target_pairs={{0,1},{1,0},{2,3},{3,2},{4,5},{5,4},{6,7},{7,6},{8,9},{9,8},{10,11... | collective-permute-start | bytes 786440 | tf_op jit(solution)/shard_map/ppermute | solution.py:330
  69.6 12.3 %copy-start.13 = (bf16[2,128,1024]{2,1,0:T(8,128)(2,1)}, bf16[2,128,1024]{2,1,0:T(8,128)(2,1)S(1)}, u32[]{:S(2)}) copy-start(bf16[2,128,1024]{2,1,0:T(8,128)(2,1)S(1)} %collective-permute-done.7.cot_1) | copy-start | bytes 1572868
  69.6 12.3 %collective-permute-start.12 = (bf16[4,128,256]{2,1,0:T(8,128)(2,1)S(1)}, bf16[4,128,256]{2,1,0:T(8,128)(2,1)S(1)}, u32[]{:S(2)}, u32[]{:S(2)}) collective-permute-start(bf16[4,128,256]{2,1,0:T(8,128)(2,1)S(1)} %pad_maximum_fusion.5), channel_id=1, source_target_pairs={{0,4},{4,0},{1,5},{5,1},{2,6},{6,2},{3,7},{7,3},{8,12},{12,8},{9,1... | collective-permute-start | bytes 786440 | tf_op jit(solution)/shard_map/ppermute | solution.py:330
  82.0 24.1 %copy-start.12 = (bf16[2,4,128,256]{3,2,1,0:T(8,128)(2,1)}, bf16[2,4,128,256]{3,2,1,0:T(8,128)(2,1)S(1)}, u32[]{:S(2)}) copy-start(bf16[2,4,128,256]{3,2,1,0:T(8,128)(2,1)S(1)} %pad_maximum_fusion.4.own_ref) | copy-start | bytes 1572868
  82.0 20.0 %collective-permute-start.13 = (bf16[2,4,128,256]{3,2,1,0:T(8,128)(2,1)S(1)}, bf16[2,4,128,256]{3,2,1,0:T(8,128)(2,1)S(1)}, u32[]{:S(2)}, u32[]{:S(2)}) collective-permute-start(bf16[2,4,128,256]{3,2,1,0:T(8,128)(2,1)S(1)} %pad_maximum_fusion.4.own_ref), channel_id=1, source_target_pairs={{0,2},{2,0},{1,3},{3,1},{4,6},{6,4},{5,7},{7,5},{8,10},{10,8},{9,1... | collective-permute-start | bytes 1572872 | tf_op jit(solution)/shard_map/ppermute | solution.py:330
  82.7 19.3 %collective-permute-start.14 = (bf16[2,4,128,256]{3,2,1,0:T(8,128)(2,1)S(1)}, bf16[2,4,128,256]{3,2,1,0:T(8,128)(2,1)S(1)}, u32[]{:S(2)}, u32[]{:S(2)}) collective-permute-start(bf16[2,4,128,256]{3,2,1,0:T(8,128)(2,1)S(1)} %pad_maximum_fusion.4.own_ref), channel_id=1, source_target_pairs={{0,1},{1,0},{2,3},{3,2},{4,5},{5,4},{6,7},{7,6},{8,9},{9,8},{10,11... | collective-permute-start | bytes 1572872 | tf_op jit(solution)/shard_map/ppermute | solution.py:330
  102.0 4.0 %collective-permute-start.15 = (bf16[2,4,128,256]{3,2,1,0:T(8,128)(2,1)S(1)}, bf16[2,4,128,256]{3,2,1,0:T(8,128)(2,1)S(1)}, u32[]{:S(2)}, u32[]{:S(2)}) collective-permute-start(bf16[2,4,128,256]{3,2,1,0:T(8,128)(2,1)S(1)} %collective-permute-done.13.x_ref), channel_id=1, source_target_pairs={{0,1},{1,0},{2,3},{3,2},{4,5},{5,4},{6,7},{7,6},{8,9},{9,8},{10,11... | collective-permute-start | bytes 1572872 | tf_op jit(solution)/shard_map/ppermute | solution.py:330
  110.7 14.8 %collective-permute-start.20 = (bf16[4,512,512]{2,1,0:T(8,128)(2,1)}, bf16[4,512,512]{2,1,0:T(8,128)(2,1)S(1)}, u32[]{:S(2)}, u32[]{:S(2)}) collective-permute-start(bf16[4,512,512]{2,1,0:T(8,128)(2,1)} %bitcast.142), channel_id=1, source_target_pairs={{0,1},{1,0},{2,3},{3,2},{4,5},{5,4},{6,7},{7,6},{8,9},{9,8},{10,11... | collective-permute-start | bytes 6291464 | tf_op jit(solution)/shard_map/ppermute | solution.py:330
  112.1 8.0 %collective-permute-start.16 = (bf16[128,1024]{1,0:T(8,128)(2,1)}, bf16[128,1024]{1,0:T(8,128)(2,1)S(1)}, u32[]{:S(2)}, u32[]{:S(2)}) collective-permute-start(bf16[128,1024]{1,0:T(8,128)(2,1)} %get-tuple-element.188.m_own), channel_id=1, source_target_pairs={{0,4},{4,0},{1,5},{5,1},{2,6},{6,2},{3,7},{7,3},{8,12},{12,8},{9,1... | collective-permute-start | bytes 786440 | tf_op jit(solution)/shard_map/ppermute | solution.py:330
  112.2 7.9 %collective-permute-start.17 = (bf16[128,1024]{1,0:T(8,128)(2,1)}, bf16[128,1024]{1,0:T(8,128)(2,1)S(1)}, u32[]{:S(2)}, u32[]{:S(2)}) collective-permute-start(bf16[128,1024]{1,0:T(8,128)(2,1)} %get-tuple-element.188.m_own), channel_id=1, source_target_pairs={{0,2},{2,0},{1,3},{3,1},{4,6},{6,4},{5,7},{7,5},{8,10},{10,8},{9,1... | collective-permute-start | bytes 786440 | tf_op jit(solution)/shard_map/ppermute | solution.py:330
  120.1 3.9 %collective-permute-start.18 = (bf16[64,1024]{1,0:T(8,128)(2,1)S(1)}, bf16[64,1024]{1,0:T(8,128)(2,1)S(1)}, u32[]{:S(2)}, u32[]{:S(2)}) collective-permute-start(bf16[64,1024]{1,0:T(8,128)(2,1)S(1)} %slice.181), channel_id=1, source_target_pairs={{0,4},{4,0},{1,5},{5,1},{2,6},{6,2},{3,7},{7,3},{8,12},{12,8},{9,1... | collective-permute-start | bytes 393224 | tf_op jit(solution)/shard_map/ppermute | solution.py:330
  121.3 4.2 %collective-permute-start.19 = (bf16[64,1024]{1,0:T(8,128)(2,1)S(1)}, bf16[64,1024]{1,0:T(8,128)(2,1)S(1)}, u32[]{:S(2)}, u32[]{:S(2)}) collective-permute-start(bf16[64,1024]{1,0:T(8,128)(2,1)S(1)} %slice.182), channel_id=1, source_target_pairs={{0,2},{2,0},{1,3},{3,1},{4,6},{6,4},{5,7},{7,5},{8,10},{10,8},{9,1... | collective-permute-start | bytes 393224 | tf_op jit(solution)/shard_map/ppermute | solution.py:330
  135.8 9.9 %copy-start.28 = (bf16[128,1024]{1,0:T(8,128)(2,1)S(1)}, bf16[128,1024]{1,0:T(8,128)(2,1)}, u32[]{:S(2)}) copy-start(bf16[128,1024]{1,0:T(8,128)(2,1)} %get-tuple-element.205) | copy-start | bytes 786436
  135.8 7.1 %collective-permute-start.21 = (bf16[64,1024]{1,0:T(8,128)(2,1)S(1)}, bf16[64,1024]{1,0:T(8,128)(2,1)S(1)}, u32[]{:S(2)}, u32[]{:S(2)}) collective-permute-start(bf16[64,1024]{1,0:T(8,128)(2,1)S(1)} %get-tuple-element.309), channel_id=1, source_target_pairs={{0,4},{4,0},{1,5},{5,1},{2,6},{6,2},{3,7},{7,3},{8,12},{12,8},{9,1... | collective-permute-start | bytes 393224 | tf_op jit(solution)/shard_map/ppermute | solution.py:330
  136.2 6.7 %collective-permute-start.22 = (bf16[64,1024]{1,0:T(8,128)(2,1)S(1)}, bf16[64,1024]{1,0:T(8,128)(2,1)S(1)}, u32[]{:S(2)}, u32[]{:S(2)}) collective-permute-start(bf16[64,1024]{1,0:T(8,128)(2,1)S(1)} %get-tuple-element.308), channel_id=1, source_target_pairs={{0,2},{2,0},{1,3},{3,1},{4,6},{6,4},{5,7},{7,5},{8,10},{10,8},{9,1... | collective-permute-start | bytes 393224 | tf_op jit(solution)/shard_map/ppermute | solution.py:330
  142.8 6.9 %collective-permute-start.25 = (bf16[4,528,512]{2,1,0:T(8,128)(2,1)}, bf16[4,528,512]{2,1,0:T(8,128)(2,1)S(1)}, u32[]{:S(2)}, u32[]{:S(2)}) collective-permute-start(bf16[4,528,512]{2,1,0:T(8,128)(2,1)} %get-tuple-element.211), channel_id=1, source_target_pairs={{0,1},{1,0},{2,3},{3,2},{4,5},{5,4},{6,7},{7,6},{8,9},{9,8},{10,11... | collective-permute-start | bytes 6488072 | tf_op jit(solution)/shard_map/ppermute | solution.py:330
  145.8 8.0 %collective-permute-start.23 = (bf16[128,1024]{1,0:T(8,128)(2,1)S(1)}, bf16[128,1024]{1,0:T(8,128)(2,1)S(1)}, u32[]{:S(2)}, u32[]{:S(2)}) collective-permute-start(bf16[128,1024]{1,0:T(8,128)(2,1)S(1)} %pad_maximum_fusion.7), channel_id=1, source_target_pairs={{0,2},{2,0},{1,3},{3,1},{4,6},{6,4},{5,7},{7,5},{8,10},{10,8},{9,1... | collective-permute-start | bytes 786440 | tf_op jit(solution)/shard_map/ppermute | solution.py:330
  146.6 7.6 %collective-permute-start.24 = (bf16[128,1024]{1,0:T(8,128)(2,1)S(1)}, bf16[128,1024]{1,0:T(8,128)(2,1)S(1)}, u32[]{:S(2)}, u32[]{:S(2)}) collective-permute-start(bf16[128,1024]{1,0:T(8,128)(2,1)S(1)} %pad_maximum_fusion.6), channel_id=1, source_target_pairs={{0,4},{4,0},{1,5},{5,1},{2,6},{6,2},{3,7},{7,3},{8,12},{12,8},{9,1... | collective-permute-start | bytes 786440 | tf_op jit(solution)/shard_map/ppermute | solution.py:330
  160.5 19.9 %collective-permute-start.26 = (bf16[2,2,4,32,1024]{4,3,2,1,0:T(8,128)(2,1)}, bf16[2,2,4,32,1024]{4,3,2,1,0:T(8,128)(2,1)S(1)}, u32[]{:S(2)}, u32[]{:S(2)}) collective-permute-start(bf16[2,2,4,32,1024]{4,3,2,1,0:T(8,128)(2,1)} %get-tuple-element.216), channel_id=1, source_target_pairs={{0,1},{1,0},{2,3},{3,2},{4,5},{5,4},{6,7},{7,6},{8,9},{9,8},{10,11... | collective-permute-start | bytes 3145736 | tf_op jit(solution)/shard_map/ppermute | solution.py:330
  161.6 18.7 %all-to-all-start.3 = ((bf16[8,128,128]{2,1,0:T(8,128)(2,1)}), bf16[8,128,128]{2,1,0:T(8,128)(2,1)S(1)}, u32[]{:S(2)}, u32[]{:S(2)}) async-start(bf16[8,128,128]{2,1,0:T(8,128)(2,1)} %get-tuple-element.215), calls=%async_computation.3 | async-start | bytes 524288 | tf_op jit(solution)/shard_map/all_to_all | solution.py:338
  167.0 13.4 %copy-start.15 = (bf16[2,2,4,32,1024]{4,3,2,1,0:T(8,128)(2,1)S(1)}, bf16[2,2,4,32,1024]{4,3,2,1,0:T(8,128)(2,1)}, u32[]{:S(2)}) copy-start(bf16[2,2,4,32,1024]{4,3,2,1,0:T(8,128)(2,1)} %get-tuple-element.234) | copy-start | bytes 3145732
  180.8 13.0 %collective-permute-start.27 = (bf16[2,4,32,1024]{3,2,1,0:T(8,128)(2,1)S(1)}, bf16[2,4,32,1024]{3,2,1,0:T(8,128)(2,1)S(1)}, u32[]{:S(2)}, u32[]{:S(2)}) collective-permute-start(bf16[2,4,32,1024]{3,2,1,0:T(8,128)(2,1)S(1)} %get-tuple-element.297), channel_id=1, source_target_pairs={{0,2},{2,0},{1,3},{3,1},{4,6},{6,4},{5,7},{7,5},{8,10},{10,8},{9,1... | collective-permute-start | bytes 1572872 | tf_op jit(solution)/shard_map/ppermute | solution.py:330
  193.8 3.2 %collective-permute-start.28 = (bf16[2,8,32,512]{3,2,1,0:T(8,128)(2,1)}, bf16[2,8,32,512]{3,2,1,0:T(8,128)(2,1)S(1)}, u32[]{:S(2)}, u32[]{:S(2)}) collective-permute-start(bf16[2,8,32,512]{3,2,1,0:T(8,128)(2,1)} %get-tuple-element.237), channel_id=1, source_target_pairs={{0,1},{1,0},{2,3},{3,2},{4,5},{5,4},{6,7},{7,6},{8,9},{9,8},{10,11... | collective-permute-start | bytes 1572872 | tf_op jit(solution)/shard_map/ppermute | solution.py:330
  195.4 22.8 %copy-start.19 = (bf16[2,128,1024]{2,1,0:T(8,128)(2,1)S(1)}, bf16[2,128,1024]{2,1,0:T(8,128)(2,1)}, u32[]{:S(2)}) copy-start(bf16[2,128,1024]{2,1,0:T(8,128)(2,1)} %get-tuple-element.220) | copy-start | bytes 1572868
  195.4 8.1 %collective-permute-start.31 = (bf16[4,32,1024]{2,1,0:T(8,128)(2,1)S(1)}, bf16[4,32,1024]{2,1,0:T(8,128)(2,1)}, u32[]{:S(2)}, u32[]{:S(2)}) collective-permute-start(bf16[4,32,1024]{2,1,0:T(8,128)(2,1)S(1)} %get-tuple-element.299), channel_id=1, source_target_pairs={{0,4},{4,0},{1,5},{5,1},{2,6},{6,2},{3,7},{7,3},{8,12},{12,8},{9,1... | collective-permute-start | bytes 786440 | tf_op jit(solution)/shard_map/ppermute | solution.py:330
  198.1 30.6 %copy-start.3 = (s32[41]{0:T(128)S(1)}, s32[41]{0:T(128)}, u32[]{:S(2)}) copy-start(s32[41]{0:T(128)} %concatenate.13.meta.table) | copy-start | bytes 496
  198.2 7.6 %collective-permute-start.30 = (bf16[8,32,512]{2,1,0:T(8,128)(2,1)S(1)}, bf16[8,32,512]{2,1,0:T(8,128)(2,1)S(1)}, u32[]{:S(2)}, u32[]{:S(2)}) collective-permute-start(bf16[8,32,512]{2,1,0:T(8,128)(2,1)S(1)} %get-tuple-element.300), channel_id=1, source_target_pairs={{0,2},{2,0},{1,3},{3,1},{4,6},{6,4},{5,7},{7,5},{8,10},{10,8},{9,1... | collective-permute-start | bytes 786440 | tf_op jit(solution)/shard_map/ppermute | solution.py:330
  198.9 29.8 %collective-permute-start.33 = (bf16[4,128,1024]{2,1,0:T(8,128)(2,1)}, bf16[4,128,1024]{2,1,0:T(8,128)(2,1)S(1)}, u32[]{:S(2)}, u32[]{:S(2)}) collective-permute-start(bf16[4,128,1024]{2,1,0:T(8,128)(2,1)} %get-tuple-element.244), channel_id=1, source_target_pairs={{0,4},{4,0},{1,5},{5,1},{2,6},{6,2},{3,7},{7,3},{8,12},{12,8},{9,1... | collective-permute-start | bytes 3145736 | tf_op jit(solution)/shard_map/ppermute | solution.py:330
  199.9 18.4 %collective-permute-start.29 = (bf16[2,128,1024]{2,1,0:T(8,128)(2,1)}, bf16[2,128,1024]{2,1,0:T(8,128)(2,1)}, u32[]{:S(2)}, u32[]{:S(2)}) collective-permute-start(bf16[2,128,1024]{2,1,0:T(8,128)(2,1)} %get-tuple-element.238), channel_id=1, source_target_pairs={{0,2},{2,0},{1,3},{3,1},{4,6},{6,4},{5,7},{7,5},{8,10},{10,8},{9,1... | collective-permute-start | bytes 1572872 | tf_op jit(solution)/shard_map/ppermute | solution.py:330
  201.0 39.0 %copy-start.14 = (bf16[4,128,1024]{2,1,0:T(8,128)(2,1)S(1)}, bf16[4,128,1024]{2,1,0:T(8,128)(2,1)}, u32[]{:S(2)}) copy-start(bf16[4,128,1024]{2,1,0:T(8,128)(2,1)} %get-tuple-element.255) | copy-start | bytes 3145732
  206.5 22.2 %all-to-all-start.4 = ((bf16[8,32,512]{2,1,0:T(8,128)(2,1)}), bf16[8,32,512]{2,1,0:T(8,128)(2,1)S(1)}, u32[]{:S(2)}, u32[]{:S(2)}) async-start(bf16[8,32,512]{2,1,0:T(8,128)(2,1)} %add_convert_fusion.7), calls=%async_computation.4 | async-start | bytes 524288 | tf_op jit(solution)/shard_map/all_to_all | solution.py:338
  214.7 9.0 %collective-permute-start.34 = (bf16[32,1024]{1,0:T(8,128)(2,1)}, bf16[32,1024]{1,0:T(8,128)(2,1)S(1)}, u32[]{:S(2)}, u32[]{:S(2)}) collective-permute-start(bf16[32,1024]{1,0:T(8,128)(2,1)} %get-tuple-element.305), channel_id=1, source_target_pairs={{0,8},{8,16},{16,24},{24,0},{1,9},{9,17},{17,25},{25,1},{2,10},{10... | collective-permute-start | bytes 196616 | tf_op jit(solution)/shard_map/ppermute | solution.py:334
  215.8 7.8 %collective-permute-start.35 = (bf16[32,1024]{1,0:T(8,128)(2,1)}, bf16[32,1024]{1,0:T(8,128)(2,1)S(1)}, u32[]{:S(2)}, u32[]{:S(2)}) collective-permute-start(bf16[32,1024]{1,0:T(8,128)(2,1)} %get-tuple-element.304), channel_id=1, source_target_pairs={{0,16},{8,24},{16,0},{24,8},{1,17},{9,25},{17,1},{25,9},{2,18},{10... | collective-permute-start | bytes 196616 | tf_op jit(solution)/shard_map/ppermute | solution.py:334
  216.7 8.9 %collective-permute-start.36 = (bf16[32,1024]{1,0:T(8,128)(2,1)S(1)}, bf16[32,1024]{1,0:T(8,128)(2,1)S(1)}, u32[]{:S(2)}, u32[]{:S(2)}) collective-permute-start(bf16[32,1024]{1,0:T(8,128)(2,1)S(1)} %get-tuple-element.303), channel_id=1, source_target_pairs={{0,24},{8,0},{16,8},{24,16},{1,25},{9,1},{17,9},{25,17},{2,26},{10... | collective-permute-start | bytes 196616 | tf_op jit(solution)/shard_map/ppermute | solution.py:334
  219.9 30.5 %collective-permute-start.32 = (bf16[128,1024]{1,0:T(8,128)(2,1)}, bf16[128,1024]{1,0:T(8,128)(2,1)}, u32[]{:S(2)}, u32[]{:S(2)}) collective-permute-start(bf16[128,1024]{1,0:T(8,128)(2,1)} %fusion.16), channel_id=1, source_target_pairs={{0,4},{4,0},{1,5},{5,1},{2,6},{6,2},{3,7},{7,3},{8,12},{12,8},{9,1... | collective-permute-start | bytes 786440 | tf_op jit(solution)/shard_map/ppermute | solution.py:330
  228.7 21.8 %copy-start.1 = (bf16[8,32,512]{2,1,0:T(8,128)(2,1)}, bf16[8,32,512]{2,1,0:T(8,128)(2,1)S(1)}, u32[]{:S(2)}) copy-start(bf16[8,32,512]{2,1,0:T(8,128)(2,1)S(1)} %all-to-all-done.4.qkv_ref.refs_1_) | copy-start | bytes 786436
  232.5 12.3 %all-to-all-start.5 = ((f32[32,1,128]{2,1,0:T(1,128)}), f32[32,1,128]{2,1,0:T(1,128)S(1)}, u32[]{:S(2)}, u32[]{:S(2)}) async-start(f32[32,1,128]{2,1,0:T(1,128)} %get-tuple-element.252), calls=%async_computation.6 | async-start | bytes 32768 | tf_op jit(solution)/shard_map/all_to_all | solution.py:338
  241.2 19.0 %collective-permute-start.37 = (bf16[128,1024]{1,0:T(8,128)(2,1)}, bf16[128,1024]{1,0:T(8,128)(2,1)S(1)}, u32[]{:S(2)}, u32[]{:S(2)}) collective-permute-start(bf16[128,1024]{1,0:T(8,128)(2,1)} %get-tuple-element.295), channel_id=1, source_target_pairs={{0,8},{8,16},{16,24},{24,0},{1,9},{9,17},{17,25},{25,1},{2,10},{10... | collective-permute-start | bytes 786440 | tf_op jit(solution)/shard_map/ppermute | solution.py:334
  242.4 22.5 %collective-permute-start.38 = (bf16[128,1024]{1,0:T(8,128)(2,1)}, bf16[128,1024]{1,0:T(8,128)(2,1)S(1)}, u32[]{:S(2)}, u32[]{:S(2)}) collective-permute-start(bf16[128,1024]{1,0:T(8,128)(2,1)} %get-tuple-element.294), channel_id=1, source_target_pairs={{0,16},{8,24},{16,0},{24,8},{1,17},{9,25},{17,1},{25,9},{2,18},{10... | collective-permute-start | bytes 786440 | tf_op jit(solution)/shard_map/ppermute | solution.py:334
  243.6 23.9 %collective-permute-start.39 = (bf16[128,1024]{1,0:T(8,128)(2,1)}, bf16[128,1024]{1,0:T(8,128)(2,1)S(1)}, u32[]{:S(2)}, u32[]{:S(2)}) collective-permute-start(bf16[128,1024]{1,0:T(8,128)(2,1)} %get-tuple-element.293), channel_id=1, source_target_pairs={{0,24},{8,0},{16,8},{24,16},{1,25},{9,1},{17,9},{25,17},{2,26},{10... | collective-permute-start | bytes 786440 | tf_op jit(solution)/shard_map/ppermute | solution.py:334
  244.8 12.1 %all-to-all-start.6 = ((bf16[8,32,512]{2,1,0:T(8,128)(2,1)}), bf16[8,32,512]{2,1,0:T(8,128)(2,1)}, u32[]{:S(2)}, u32[]{:S(2)}) async-start(bf16[8,32,512]{2,1,0:T(8,128)(2,1)} %bitcast.146), calls=%async_computation.7 | async-start | bytes 524288 | tf_op jit(solution)/shard_map/all_to_all | solution.py:338
  (26 other events, 85.7 us)
Sparse Core Ops, SparseCore 0:
  47.1 50.5 all-gather.2
  151.9 48.9 reduce-scatter.1

commit v2 on v1

--- a/solution.py
+++ b/solution.py
@@ -403,18 +403,15 @@
     pieces = refs[n_refs : n_refs + 4]
     start_ref = refs[n_refs + 4]
     att_ref, att_t, qkv_ref, lse_ref, normed, x_ref, w_ref, vec_ref, extra = refs[n_refs + 5 :]
-    n_line = (n_refs - 3) // 2 + 1
-    own, pair, pair_line = refs[0], refs[1], refs[2]
-    line, rest = refs[3 : 2 + n_line], refs[2 + n_line : 1 + 2 * n_line]
+    n_line = n_refs // 2
+    own, pair, pair_line, line = refs[0], refs[1], refs[2 : 1 + n_line], refs[1 + n_line : n_refs]
     n_blocks = 2 * n_line
-    cut = line[0].shape[1]
 
     def block_part(b, span):
         z, other = b % n_line, b // n_line
         if z == 0:
             return (pair if other else own)[span, :]
-        first = pair_line[z - 1, span, :] if other else line[z - 1][span, :]
-        return jnp.concatenate([first, rest[z - 1][other, span, :]], 1)
+        return pair_line[z - 1][span, :] if other else line[z - 1][span, :]
 
     f32, low = jnp.float32, jnp.bfloat16
     n_ctx, rows, _ = pieces[0].shape
@@ -826,7 +823,7 @@
 
 def attend_forward(table, slopes, blocks, pieces, start, cols):
     tokens, width = blocks[0].shape
-    seq = tokens * (len(blocks) - 1)
+    seq = tokens * len(blocks)
     f32, low = jnp.float32, jnp.bfloat16
     shapes = [
         ((seq, cols), low), ((cols, seq), f32), ((seq, 3 * cols), low), ((8, seq), f32),
@@ -864,9 +861,7 @@
     field = field_low.astype(f32)
     cot_low = out_grad[0]
 
-    cut = width - width // 4
-    field_cut = field_low[:, :cut]
-    line = [shift(field_cut, "z", nz, k) for k in range(1, nz)]
+    line = [shift(field_low, "z", nz, k) for k in range(1, nz)]
     own_two = exchange(jnp.stack([field_low, cot_low]), "y")
     shapes = [((n_ctx, rows, 3 * cols + 128), low), ((8, rows, ff), low), ((n_half, ff_own, ff), low), ((tokens, width // 4), low)]
     packed = [pairs, w_qkv, vectors, segments, up_bias.reshape(1, ff_own), w_up, w_down, w_out]
@@ -874,13 +869,12 @@
     first_got = swap(first_send, ctx)
     up_part = swap(after(up_send, first_got), plane).reshape(8 * rows, ff)
     ff_send = jnp.concatenate([up_part, down_part.reshape(n_half * ff_own, ff)], 0)
-    ff_send, first_got, own_two, out_low, *line = gate(ff_send, first_got, own_two, out_low, *line)
+    ff_send, first_got, own_two, out_low = gate(ff_send, first_got, own_two, out_low)
     pair_own, cot_y = own_two[0], own_two[1]
 
     ff_all = lax.all_gather(ff_send, "z", axis=0)
-    pair_line = exchange(jnp.stack(line), "y")
-    rest_own = jnp.stack([field_low[:, cut:], pair_own[:, cut:], out_low])
-    rest = [shift(rest_own, "z", nz, k) for k in range(1, nz)]
+    pair_line = [exchange(v, "y") for v in line]
+    rest = [shift(out_low, "z", nz, k) for k in range(1, nz)]
     first_x = exchange(first_got, "x")
     first_c = exchange(first_got, "c")
     first_cx = exchange(first_x, "c")
@@ -906,14 +900,14 @@
     table = jnp.concatenate([near_block.reshape(-1), block_slot, piece_f, here]).astype(jnp.int32)
     head_ids = (ctx_i * heads_own + jnp.arange(heads_own)).astype(f32)
     slopes = jnp.exp2(-8.0 * (head_ids + 1.0) / HEADS)
-    out_z = jnp.stack([out_low] + [v[2] for v in rest])
-    first_x, first_c, first_cx, cot_x, table, start, pair_line, slopes, out_z, *rest = gate(
-        first_x, first_c, first_cx, cot_x, table, start, pair_line, slopes, out_z, *rest
+    out_z = jnp.stack([out_low] + rest)
+    first_x, first_c, first_cx, cot_x, table, start, slopes, out_z, *pair_line = gate(
+        first_x, first_c, first_cx, cot_x, table, start, slopes, out_z, *pair_line
     )
 
     out_y = exchange(out_z, "y")
     pieces = (first_got, first_x, first_c, first_cx)
-    blocks = [field_low, pair_own, pair_line] + line + rest
+    blocks = [field_low, pair_own] + pair_line + line
     attended, att_t, qkv_low, lse, normed_one, seq_rows, qkv_w, vec = attend_forward(
         table, slopes, blocks, pieces, start, cols
     )

time: 277 us -> 272 us (0.982)
  waiting for transfers between devices: 66.8 us -> 57.2 us
  blocking collectives: 12.4 us -> 16.4 us
    all_to_all x6, starting transfers between devices: 37.4 us -> 45.9 us  [swap(): return lax.all_to_all(v, axes, 0, 0, tiled=True)]
    ppermute x12, waiting for transfers between devices: 22.8 us -> 14.5 us  [shift(): return lax.ppermute(v, axis, [(i, (i - k) % n_line) for i in range(n_line)])]
    ppermute x28 -> x30, starting transfers between devices: 34.5 us -> 29.4 us  [exchange(): return lax.ppermute(v, axis, [(0, 1), (1, 0)])]
    all_to_all x1, blocking collectives: 12.4 us -> 16.4 us  [swap(): return lax.all_to_all(v, axes, 0, 0, tiled=True)]
    all_to_all x6, waiting for transfers between devices: 23.3 us -> 20 us  [swap(): return lax.all_to_all(v, axes, 0, 0, tiled=True)]
    ppermute x28 -> x30, waiting for transfers between devices: 20.7 us -> 22.7 us  [exchange(): return lax.ppermute(v, axis, [(0, 1), (1, 0)])]
  transfers between devices with their start and end apart: 48 -> 50, of which waited for: 21 -> 21; matrix products, arithmetic and copies ran while one was open for 8% -> 8% of each run, Pallas kernels for 19% -> 19%
where the time goes in v2:
time: 272 us; the launch traced here: 271 us
  starting transfers between devices  89.3 us (33%)
  Pallas kernels  62.7 us (23%)
  waiting for transfers between devices  57.2 us (21%)
  other arithmetic  17.3 us (6%)
  blocking collectives  16.4 us (6%)
  between operations  15.3 us (6%)
  local copies, waits for them, and re-layouts  12.4 us (5%)
    pallas_call x11, Pallas kernels, call(): pl.pallas_call(kernel, out_shape=[jax.ShapeDtypeStruct(s, d) for s, d in...  62.7 us
    all_to_all x6, starting transfers between devices, swap(): return lax.all_to_all(v, axes, 0, 0, tiled=True)  45.9 us
    ppermute x30, starting transfers between devices, exchange(): return lax.ppermute(v, axis, [(0, 1), (1, 0)])  29.4 us
    ppermute x30, waiting for transfers between devices, exchange(): return lax.ppermute(v, axis, [(0, 1), (1, 0)])  22.7 us
    all_to_all x6, waiting for transfers between devices, swap(): return lax.all_to_all(v, axes, 0, 0, tiled=True)  20 us
    all_to_all x1, blocking collectives, swap(): return lax.all_to_all(v, axes, 0, 0, tiled=True)  16.4 us
    ppermute x12, waiting for transfers between devices, shift(): return lax.ppermute(v, axis, [(i, (i - k) % n_line) for i in range(n_line)])  14.5 us
    ppermute x12, starting transfers between devices, shift(): return lax.ppermute(v, axis, [(i, (i - k) % n_line) for i in range(n_line)])  13.9 us
  transfers between devices with their start and end apart: 50, of which 21 were waited for; matrix products, arithmetic and copies ran while one was open for 8% of the time, Pallas kernels for 19%

profile of v2, /device:TPU:11, one launch (start us, length us, event | category | flops | bytes accessed | tf_op | source)
XLA Modules:
  0.0 270.7 jit_solution(1119826642334307659)
XLA Ops:
  7.9 2.4 shard_map.421
  10.3 5.9 %all-to-all-start = ((bf16[8,32,512]{2,1,0:T(8,128)(2,1)}), bf16[8,32,512]{2,1,0:T(8,128)(2,1)S(1)}, u32[]{:S(2)}, u32[]{:S(2)}) async-start(bf16[8,32,512]{2,1,0:T(8,128)(2,1)} %get-tuple-element.155), calls=%async_computation | async-start | bytes 524288 | tf_op jit(solution)/shard_map/all_to_all | solution.py:338
  16.2 1.2 collective-permute-start
  17.5 2.1 collective-permute-start.10
  19.5 1.5 collective-permute-start.8
  21.0 5.0 %all-to-all-done.refs_8_ = bf16[8,32,512]{2,1,0:T(8,128)(2,1)S(1)} async-done(((bf16[8,32,512]{2,1,0:T(8,128)(2,1)}), bf16[8,32,512]{2,1,0:T(8,128)(2,1)S(1)}, u32[]{:S(2)}, u32[]{:S(2)}) %all-to-all-start) | async-done | bytes 262176 | tf_op jit(solution)/shard_map/all_to_all | solution.py:338
  26.0 14.4 %all-to-all-start.1 = ((bf16[8,32,512]{2,1,0:T(8,128)(2,1)}), bf16[8,32,512]{2,1,0:T(8,128)(2,1)S(1)}, u32[]{:S(2)}, u32[]{:S(2)}) async-start(bf16[8,32,512]{2,1,0:T(8,128)(2,1)} %get-tuple-element.156), calls=%async_computation.1 | async-start | bytes 524288 | tf_op jit(solution)/shard_map/all_to_all | solution.py:338
  41.1 1.2 collective-permute-start.11
  42.4 3.3 %all-to-all-done.1 = bf16[8,32,512]{2,1,0:T(8,128)(2,1)S(1)} async-done(((bf16[8,32,512]{2,1,0:T(8,128)(2,1)}), bf16[8,32,512]{2,1,0:T(8,128)(2,1)S(1)}, u32[]{:S(2)}, u32[]{:S(2)}) %all-to-all-start.1) | async-done | bytes 262176 | tf_op jit(solution)/shard_map/all_to_all | solution.py:338
  49.9 1.9 collective-permute-start.5
  51.8 1.3 collective-permute-start.7
  54.0 2.0 collective-permute-done.6
  56.1 3.3 %collective-permute-done.7 = bf16[128,256]{1,0:T(8,128)(2,1)S(1)} collective-permute-done((bf16[128,256]{1,0:T(8,128)(2,1)S(1)}, bf16[128,256]{1,0:T(8,128)(2,1)S(1)}, u32[]{:S(2)}, u32[]{:S(2)}) %collective-permute-start.7) | collective-permute-done | bytes 65568 | tf_op jit(solution)/shard_map/ppermute | solution.py:334
  59.4 3.2 %collective-permute-start.2 = (bf16[8,32,512]{2,1,0:T(8,128)(2,1)S(1)}, bf16[8,32,512]{2,1,0:T(8,128)(2,1)S(1)}, u32[]{:S(2)}, u32[]{:S(2)}) collective-permute-start(bf16[8,32,512]{2,1,0:T(8,128)(2,1)S(1)} %all-to-all-done.refs_8_), channel_id=1, source_target_pairs={{0,1},{1,0},{2,3},{3,2},{4,5},{5,4},{6,7},{7,6},{8,9},{9,8},{10,11... | collective-permute-start | bytes 786440 | tf_op jit(solution)/shard_map/ppermute | solution.py:330
  62.7 1.1 convert_reduce_fusion
  64.2 1.0 collective-permute-done.4.cot_1
  66.1 11.4 %shard_map.422 = (bf16[1024,128]{1,0:T(8,128)(2,1)}, f32[128,1024]{1,0:T(8,128)}, bf16[1024,384]{1,0:T(8,128)(2,1)}, f32[8,1024]{1,0:T(8,128)}, bf16[1024,1024]{...) custom-call(s32[41]{0:T(128)} %concatenate.13.meta.table, ...), custom_call_target="tpu_custom_call" | custom-call | flops 8999999488 | bytes 8999999488 | tf_op jit(solution)/shard_map/pallas_call | solution.py:813
  77.7 4.2 %collective-permute-start.16 = (bf16[2,4,128,256]{3,2,1,0:T(8,128)(2,1)S(1)}, bf16[2,4,128,256]{3,2,1,0:T(8,128)(2,1)S(1)}, u32[]{:S(2)}, u32[]{:S(2)}) collective-permute-start(bf16[2,4,128,256]{3,2,1,0:T(8,128)(2,1)S(1)} %pad_maximum_fusion.3.own_ref), channel_id=1, source_target_pairs={{0,1},{1,0},{2,3},{3,2},{4,5},{5,4},{6,7},{7,6},{8,9},{9,8},{10,11... | collective-permute-start | bytes 1572872 | tf_op jit(solution)/shard_map/ppermute | solution.py:330
  81.8 16.4 %all_to_all.35.att = bf16[8,128,128]{2,1,0:T(8,128)(2,1)} all-to-all(bf16[8,128,128]{2,1,0:T(8,128)(2,1)} %bitcast.147), channel_id=1, replica_groups=mesh['z'=4,'y'=2,'x'=2,'c'=2] {'z','y'}, dimensions={0} | all-to-all | bytes 524288 | tf_op jit(solution)/shard_map/all_to_all | solution.py:338
  98.8 1.5 collective-permute-done.17.cx_ref
  101.1 4.0 %shard_map.423 = (f32[128,1024]{1,0:T(8,128)}, bf16[128,1024]{1,0:T(8,128)(2,1)}, bf16[1024,1024]{1,0:T(8,128)(2,1)}) custom-call(s32[41]{0:T(128)} %concatenate.13.meta.table, bf16[8,128,128]{2,1,0:T(8,128)(2,1)} %all_to_all.35.att, bf16[2,4,128,256]{3,2,1,0:T(8,128)(2,1)} %copy-done.12, bf16[2,4,128,256]{3,2,1,0:T(8,128)(2,1)} %copy-done.20, ...), custom_call_target="tpu_custom_call" | custom-call | flops 1 | bytes 1 | tf_op jit(solution)/shard_map/pallas_call | solution.py:813
  107.9 6.5 %collective-permute-done.18.m_y = bf16[128,1024]{1,0:T(8,128)(2,1)S(1)} collective-permute-done((bf16[128,1024]{1,0:T(8,128)(2,1)}, bf16[128,1024]{1,0:T(8,128)(2,1)S(1)}, u32[]{:S(2)}, u32[]{:S(2)}) %collective-permute-start.18) | collective-permute-done | bytes 262176 | tf_op jit(solution)/shard_map/ppermute | solution.py:330
  114.4 1.2 collective-permute-start.20
  117.0 1.3 collective-permute-done.20.m_d0
  118.3 1.5 collective-permute-done.21.m_d1
  121.2 7.9 %shard_map.424 = (bf16[128,1024]{1,0:T(8,128)(2,1)}, bf16[128,1024]{1,0:T(8,128)(2,1)}, bf16[128,1024]{1,0:T(8,128)(2,1)}, bf16[128,1024]{1,0:T(8,128)(2,1)}, bf...) custom-call(bf16[128,1024]{1,0:T(8,128)(2,1)} %get-tuple-element.180.m_own, ...), custom_call_target="tpu_custom_call" | custom-call | flops 1 | bytes 1 | tf_op jit(solution)/shard_map/pallas_call | solution.py:813
  131.2 5.9 %shard_map.425 = (bf16[4,528,512]{2,1,0:T(8,128)(2,1)}, bf16[4,528,512]{2,1,0:T(8,128)(2,1)}) custom-call(bf16[512,1024]{1,0:T(8,128)(2,1)} %get-tuple-element.192.mlp_ref, bf16[512,1024]{1,0:T(8,128)(2,1)} %get-tuple-element.193.pre_ref, bf16[512,1024]{1,0:T(8,128)(2,1)} %get-tuple-element.209.hidden_ref, bf16[2,128,1024]{2,1,0:T(8,128)(2,1)} %copy-done.8, ...), custom_call_target="tpu_custom_call" | custom-call | flops 1 | bytes 1 | tf_op jit(solution)/shard_map/pallas_call | solution.py:813
  137.1 2.9 %collective-permute-start.27 = (bf16[4,528,512]{2,1,0:T(8,128)(2,1)}, bf16[4,528,512]{2,1,0:T(8,128)(2,1)S(1)}, u32[]{:S(2)}, u32[]{:S(2)}) collective-permute-start(bf16[4,528,512]{2,1,0:T(8,128)(2,1)} %get-tuple-element.203), channel_id=1, source_target_pairs={{0,1},{1,0},{2,3},{3,2},{4,5},{5,4},{6,7},{7,6},{8,9},{9,8},{10,11... | collective-permute-start | bytes 6488072 | tf_op jit(solution)/shard_map/ppermute | solution.py:330
  140.9 1.4 collective-permute-start.26
  142.3 1.8 collective-permute-done.27
  144.1 1.9 add_convert_fusion
  146.0 2.1 collective-permute-done.25.got_x
  149.2 5.5 %shard_map.426 = (f32[128,1024]{1,0:T(8,128)}, bf16[8,128,128]{2,1,0:T(8,128)(2,1)}, f32[8,1024]{1,0:T(8,128)}, bf16[2,2,4,32,1024]{4,3,2,1,0:T(8,128)(2,1)}, bf16[2,2,4,32,1024]{4,3,2,1,0:T(8,128)(2,1)}) custom-call(s32[41]{0:T(128)} %concatenate.13.meta.table, bf16[128,1024]{1,0:T(8,128)(2,1)} %get-tuple-element.189.own, bf16[128,1024]{1,0:T(8,128)(2,1)} %copy-done.24, ...), custom_call_target="tpu_custom_call" | custom-call | flops 1 | bytes 1 | tf_op jit(solution)/shard_map/pallas_call | solution.py:813
  154.7 1.1 collective-permute-start.28
  155.9 5.9 %all-to-all-start.3 = ((bf16[8,128,128]{2,1,0:T(8,128)(2,1)}), bf16[8,128,128]{2,1,0:T(8,128)(2,1)S(1)}, u32[]{:S(2)}, u32[]{:S(2)}) async-start(bf16[8,128,128]{2,1,0:T(8,128)(2,1)} %get-tuple-element.207), calls=%async_computation.3 | async-start | bytes 524288 | tf_op jit(solution)/shard_map/all_to_all | solution.py:338
  161.8 4.7 %shard_map.427 = (bf16[2,128,1024]{2,1,0:T(8,128)(2,1)}, bf16[2,128,1024]{2,1,0:T(8,128)(2,1)}) custom-call(bf16[512,1024]{1,0:T(8,128)(2,1)} %get-tuple-element.209.hidden_ref, bf16[4,512,512]{2,1,0:T(8,128)(2,1)} %bitcast.136, bf16[4,512,512]{2,1,0:T(8,128)(2,1)} %copy-done.5), custom_call_target="tpu_custom_call" | custom-call | flops 1 | bytes 1 | tf_op jit(solution)/shard_map/pallas_call | solution.py:813
  166.5 8.6 %all-to-all-done.3 = bf16[8,128,128]{2,1,0:T(8,128)(2,1)S(1)} async-done(((bf16[8,128,128]{2,1,0:T(8,128)(2,1)}), bf16[8,128,128]{2,1,0:T(8,128)(2,1)S(1)}, u32[]{:S(2)}, u32[]{:S(2)}) %all-to-all-start.3) | async-done | bytes 262176 | tf_op jit(solution)/shard_map/all_to_all | solution.py:338
  176.3 11.9 %shard_map.428 = (bf16[2,8,32,512]{3,2,1,0:T(8,128)(2,1)}, bf16[2,8,32,512]{3,2,1,0:T(8,128)(2,1)}, bf16[4,128,1024]{2,1,0:T(8,128)(2,1)}, bf16[4,128,1024]{2,1,0:T(8,128)(2,1)}) custom-call(s32[41]{0:T(128)} %concatenate.13.meta.table, f32[2]{0:T(128)} %multiply_exponential_fusion.slopes, bf16[1024,128]{1,0:T(8,128)(2,1)} %bitcast.146, ...), custom_call_target="tpu_custom_call" | custom-call | flops 8999999488 | bytes 8999999488 | tf_op jit(solution)/shard_map/pallas_call | solution.py:813
  188.2 1.8 collective-permute-start.30
  191.7 1.2 fusion.15
  195.2 3.0 %collective-permute-done.33 = bf16[4,32,1024]{2,1,0:T(8,128)(2,1)} collective-permute-done((bf16[4,32,1024]{2,1,0:T(8,128)(2,1)S(1)}, bf16[4,32,1024]{2,1,0:T(8,128)(2,1)}, u32[]{:S(2)}, u32[]{:S(2)}) %collective-permute-start.33) | collective-permute-done | bytes 262176 | tf_op jit(solution)/shard_map/ppermute | solution.py:330
  198.3 2.2 collective-permute-done.32
  201.2 6.5 %all-to-all-start.4 = ((bf16[8,32,512]{2,1,0:T(8,128)(2,1)}), bf16[8,32,512]{2,1,0:T(8,128)(2,1)S(1)}, u32[]{:S(2)}, u32[]{:S(2)}) async-start(bf16[8,32,512]{2,1,0:T(8,128)(2,1)} %add_convert_fusion.7), calls=%async_computation.4 | async-start | bytes 524288 | tf_op jit(solution)/shard_map/all_to_all | solution.py:338
  207.8 1.6 fusion.29
  209.4 1.2 collective-permute-start.36
  211.6 1.4 collective-permute-start.38
  213.0 1.7 fusion.16
  214.7 1.2 collective-permute-start.34
  216.8 1.7 slice.181
  218.4 2.0 collective-permute-done.38.refs_2_
  220.4 3.0 %all-to-all-done.4.qkv_ref.refs_1_ = bf16[8,32,512]{2,1,0:T(8,128)(2,1)S(1)} async-done(((bf16[8,32,512]{2,1,0:T(8,128)(2,1)}), bf16[8,32,512]{2,1,0:T(8,128)(2,1)S(1)}, u32[]{:S(2)}, u32[]{:S(2)}) %all-to-all-start.4) | async-done | bytes 262176 | tf_op jit(solution)/shard_map/all_to_all | solution.py:338
  223.5 1.1 copy-done
  224.6 1.4 shard_map.429
  227.2 7.6 %all-to-all-start.5 = ((f32[32,1,128]{2,1,0:T(1,128)}), f32[32,1,128]{2,1,0:T(1,128)S(1)}, u32[]{:S(2)}, u32[]{:S(2)}) async-start(f32[32,1,128]{2,1,0:T(1,128)} %get-tuple-element.244), calls=%async_computation.6 | async-start | bytes 32768 | tf_op jit(solution)/shard_map/all_to_all | solution.py:338
  234.9 1.1 fusion.19
  236.0 1.2 collective-permute-start.39
  237.1 1.2 collective-permute-start.40
  238.3 1.3 collective-permute-start.41
  239.6 5.6 %all-to-all-start.6 = ((bf16[8,32,512]{2,1,0:T(8,128)(2,1)}), bf16[8,32,512]{2,1,0:T(8,128)(2,1)}, u32[]{:S(2)}, u32[]{:S(2)}) async-start(bf16[8,32,512]{2,1,0:T(8,128)(2,1)} %bitcast.143), calls=%async_computation.7 | async-start | bytes 524288 | tf_op jit(solution)/shard_map/all_to_all | solution.py:338
  245.3 4.5 %shard_map.430 = (f32[1,1]{1,0:T(1,128)}, f32[32,3072]{1,0:T(8,128)}, f32[32,3072]{1,0:T(8,128)}, f32[32,3072]{1,0:T(8,128)}, f32[32,3072]{1,0:T(8,128)}, /*inde...) custom-call(f32[32,1,128]{2,1,0:T(1,128)} %copy-done.30, ...), custom_call_target="tpu_custom_call" | custom-call | flops 1 | bytes 1 | tf_op jit(solution)/shard_map/pallas_call | solution.py:813
  249.8 2.0 fusion.21
  251.7 3.3 %shard_map.431 = (f32[32,4096]{1,0:T(8,128)}, f32[32,4096]{1,0:T(8,128)}, f32[32,4096]{1,0:T(8,128)}, f32[32,4096]{1,0:T(8,128)}) custom-call(f32[32,1,128]{2,1,0:T(1,128)} %copy-done.30, bf16[8,32,512]{2,1,0:T(8,128)(2,1)} %all-to-all-done.6.up_ref, f32[32,4096]{1,0:T(8,128)} %refs_0_.1, f32[32,4096]{1,0:T(8,128)} %refs_1_.1, f32[32,4096]{1,0:T(8,128)} %refs_2_.1), custom_call_target="tpu_custom_call" | custom-call | flops 1 | bytes 1 | tf_op jit(solution)/shard_map/pallas_call | solution.py:813
  255.0 4.7 %collective-permute-done.40 = bf16[128,1024]{1,0:T(8,128)(2,1)S(1)} collective-permute-done((bf16[128,1024]{1,0:T(8,128)(2,1)}, bf16[128,1024]{1,0:T(8,128)(2,1)S(1)}, u32[]{:S(2)}, u32[]{:S(2)}) %collective-permute-start.40) | collective-permute-done | bytes 262176 | tf_op jit(solution)/shard_map/ppermute | solution.py:334
  259.6 2.5 collective-permute-done.41
  (189 shorter events, 29.1 us)
Async XLA Ops:
  10.3 35.4 %copy-start.29 = (bf16[2,128,512]{2,1,0:T(8,128)(2,1)S(1)}, bf16[2,128,512]{2,1,0:T(8,128)(2,1)}, u32[]{:S(2)}) copy-start(bf16[2,128,512]{2,1,0:T(8,128)(2,1)} %get-tuple-element.157) | copy-start | bytes 786436
  10.3 15.7 %all-to-all-start = ((bf16[8,32,512]{2,1,0:T(8,128)(2,1)}), bf16[8,32,512]{2,1,0:T(8,128)(2,1)S(1)}, u32[]{:S(2)}, u32[]{:S(2)}) async-start(bf16[8,32,512]{2,1,0:T(8,128)(2,1)} %get-tuple-element.155), calls=%async_computation | async-start | bytes 524288 | tf_op jit(solution)/shard_map/all_to_all | solution.py:338
  16.2 30.3 %collective-permute-start = (bf16[2,128,1024]{2,1,0:T(8,128)(2,1)S(1)}, bf16[2,128,1024]{2,1,0:T(8,128)(2,1)S(1)}, u32[]{:S(2)}, u32[]{:S(2)}) collective-permute-start(bf16[2,128,1024]{2,1,0:T(8,128)(2,1)S(1)} %pad_maximum_fusion.1), channel_id=1, source_target_pairs={{0,4},{4,0},{1,5},{5,1},{2,6},{6,2},{3,7},{7,3},{8,12},{12,8},{9,1... | collective-permute-start | bytes 1572872 | tf_op jit(solution)/shard_map/ppermute | solution.py:330
  17.5 23.7 %collective-permute-start.10 = (bf16[128,1024]{1,0:T(8,128)(2,1)S(1)}, bf16[128,1024]{1,0:T(8,128)(2,1)S(1)}, u32[]{:S(2)}, u32[]{:S(2)}) collective-permute-start(bf16[128,1024]{1,0:T(8,128)(2,1)S(1)} %bitcast.139), channel_id=1, source_target_pairs={{0,16},{8,24},{16,0},{24,8},{1,17},{9,25},{17,1},{25,9},{2,18},{10... | collective-permute-start | bytes 786440 | tf_op jit(solution)/shard_map/ppermute | solution.py:334
  19.5 30.3 %collective-permute-start.12 = (bf16[128,1024]{1,0:T(8,128)(2,1)S(1)}, bf16[128,1024]{1,0:T(8,128)(2,1)S(1)}, u32[]{:S(2)}, u32[]{:S(2)}) collective-permute-start(bf16[128,1024]{1,0:T(8,128)(2,1)S(1)} %bitcast.140), channel_id=1, source_target_pairs={{0,8},{8,16},{16,24},{24,0},{1,9},{9,17},{17,25},{25,1},{2,10},{10... | collective-permute-start | bytes 786440 | tf_op jit(solution)/shard_map/ppermute | solution.py:334
  19.5 32.3 %collective-permute-start.8 = (bf16[128,1024]{1,0:T(8,128)(2,1)S(1)}, bf16[128,1024]{1,0:T(8,128)(2,1)S(1)}, u32[]{:S(2)}, u32[]{:S(2)}) collective-permute-start(bf16[128,1024]{1,0:T(8,128)(2,1)S(1)} %bitcast.141), channel_id=1, source_target_pairs={{0,24},{8,0},{16,8},{24,16},{1,25},{9,1},{17,9},{25,17},{2,26},{10... | collective-permute-start | bytes 786440 | tf_op jit(solution)/shard_map/ppermute | solution.py:334
  26.0 33.4 %copy-start.23 = (bf16[8,32,512]{2,1,0:T(8,128)(2,1)}, bf16[8,32,512]{2,1,0:T(8,128)(2,1)S(1)}, u32[]{:S(2)}) copy-start(bf16[8,32,512]{2,1,0:T(8,128)(2,1)S(1)} %all-to-all-done.refs_8_) | copy-start | bytes 786436
  26.0 23.9 %copy-start.33 = (bf16[128,256]{1,0:T(8,128)(2,1)S(1)}, bf16[128,256]{1,0:T(8,128)(2,1)}, u32[]{:S(2)}) copy-start(bf16[128,256]{1,0:T(8,128)(2,1)} %get-tuple-element.161) | copy-start | bytes 196612
  26.0 19.7 %all-to-all-start.1 = ((bf16[8,32,512]{2,1,0:T(8,128)(2,1)}), bf16[8,32,512]{2,1,0:T(8,128)(2,1)S(1)}, u32[]{:S(2)}, u32[]{:S(2)}) async-start(bf16[8,32,512]{2,1,0:T(8,128)(2,1)} %get-tuple-element.156), calls=%async_computation.1 | async-start | bytes 524288 | tf_op jit(solution)/shard_map/all_to_all | solution.py:338
  40.4 64.7 %all-gather.3.cloned.1.call-start = ((), (), s32[]{:S(2)}) async-start(), calls=%async_computation.9 | async-start | bytes 2621440 | tf_op jit(solution)/shard_map/all_gather | solution.py:875
  41.1 24.9 %copy-start.35 = (bf16[128,1024]{1,0:T(8,128)(2,1)}, bf16[128,1024]{1,0:T(8,128)(2,1)S(1)}, u32[]{:S(2)}) copy-start(bf16[128,1024]{1,0:T(8,128)(2,1)S(1)} %collective-permute-done.10.refs_6_) | copy-start | bytes 786436
  41.1 10.7 %collective-permute-start.11 = (bf16[128,1024]{1,0:T(8,128)(2,1)S(1)}, bf16[128,1024]{1,0:T(8,128)(2,1)}, u32[]{:S(2)}, u32[]{:S(2)}) collective-permute-start(bf16[128,1024]{1,0:T(8,128)(2,1)S(1)} %collective-permute-done.10.refs_6_), channel_id=1, source_target_pairs={{0,4},{4,0},{1,5},{5,1},{2,6},{6,2},{3,7},{7,3},{8,12},{12,8},{9,1... | collective-permute-start | bytes 786440 | tf_op jit(solution)/shard_map/ppermute | solution.py:330
  46.8 15.8 %collective-permute-start.1 = (bf16[8,32,512]{2,1,0:T(8,128)(2,1)S(1)}, bf16[8,32,512]{2,1,0:T(8,128)(2,1)S(1)}, u32[]{:S(2)}, u32[]{:S(2)}) collective-permute-start(bf16[8,32,512]{2,1,0:T(8,128)(2,1)S(1)} %all-to-all-done.refs_8_), channel_id=1, source_target_pairs={{0,2},{2,0},{1,3},{3,1},{4,6},{6,4},{5,7},{7,5},{8,10},{10,8},{9,1... | collective-permute-start | bytes 786440 | tf_op jit(solution)/shard_map/ppermute | solution.py:330
  47.4 169.4 %reduce-scatter.2.cloned.1.call-start = ((), (), s32[]{:S(2)}) async-start(), calls=%async_computation.8 | async-start | bytes 2703360 | tf_op jit(solution)/shard_map/reduce_scatter | solution.py:954
  48.2 29.3 %copy-start.8 = (bf16[2,128,1024]{2,1,0:T(8,128)(2,1)}, bf16[2,128,1024]{2,1,0:T(8,128)(2,1)S(1)}, u32[]{:S(2)}) copy-start(bf16[2,128,1024]{2,1,0:T(8,128)(2,1)S(1)} %pad_maximum_fusion.2.cot_0) | copy-start | bytes 1572868
  48.7 16.6 %collective-permute-start.4 = (bf16[2,128,1024]{2,1,0:T(8,128)(2,1)S(1)}, bf16[2,128,1024]{2,1,0:T(8,128)(2,1)S(1)}, u32[]{:S(2)}, u32[]{:S(2)}) collective-permute-start(bf16[2,128,1024]{2,1,0:T(8,128)(2,1)S(1)} %pad_maximum_fusion.2.cot_0), channel_id=1, source_target_pairs={{0,2},{2,0},{1,3},{3,1},{4,6},{6,4},{5,7},{7,5},{8,10},{10,8},{9,1... | collective-permute-start | bytes 1572872 | tf_op jit(solution)/shard_map/ppermute | solution.py:330
  49.9 16.1 %copy-start.36 = (bf16[128,1024]{1,0:T(8,128)(2,1)}, bf16[128,1024]{1,0:T(8,128)(2,1)S(1)}, u32[]{:S(2)}) copy-start(bf16[128,1024]{1,0:T(8,128)(2,1)S(1)} %collective-permute-done.12.refs_7_) | copy-start | bytes 786436
  49.9 3.9 %collective-permute-start.5 = (bf16[128,256]{1,0:T(8,128)(2,1)S(1)}, bf16[128,256]{1,0:T(8,128)(2,1)S(1)}, u32[]{:S(2)}, u32[]{:S(2)}) collective-permute-start(bf16[128,256]{1,0:T(8,128)(2,1)S(1)} %copy-done.33), channel_id=1, source_target_pairs={{0,24},{8,0},{16,8},{24,16},{1,25},{9,1},{17,9},{25,17},{2,26},{10... | collective-permute-start | bytes 196616 | tf_op jit(solution)/shard_map/ppermute | solution.py:334
  51.8 14.2 %copy-start.37 = (bf16[128,1024]{1,0:T(8,128)(2,1)}, bf16[128,1024]{1,0:T(8,128)(2,1)S(1)}, u32[]{:S(2)}) copy-start(bf16[128,1024]{1,0:T(8,128)(2,1)S(1)} %collective-permute-done.8.refs_5_) | copy-start | bytes 786436
  51.8 4.1 %collective-permute-start.6 = (bf16[128,256]{1,0:T(8,128)(2,1)S(1)}, bf16[128,256]{1,0:T(8,128)(2,1)S(1)}, u32[]{:S(2)}, u32[]{:S(2)}) collective-permute-start(bf16[128,256]{1,0:T(8,128)(2,1)S(1)} %copy-done.33), channel_id=1, source_target_pairs={{0,16},{8,24},{16,0},{24,8},{1,17},{9,25},{17,1},{25,9},{2,18},{10... | collective-permute-start | bytes 196616 | tf_op jit(solution)/shard_map/ppermute | solution.py:334
  51.8 7.5 %collective-permute-start.7 = (bf16[128,256]{1,0:T(8,128)(2,1)S(1)}, bf16[128,256]{1,0:T(8,128)(2,1)S(1)}, u32[]{:S(2)}, u32[]{:S(2)}) collective-permute-start(bf16[128,256]{1,0:T(8,128)(2,1)S(1)} %copy-done.33), channel_id=1, source_target_pairs={{0,8},{8,16},{16,24},{24,0},{1,9},{9,17},{17,25},{25,1},{2,10},{10... | collective-permute-start | bytes 196616 | tf_op jit(solution)/shard_map/ppermute | solution.py:334
  53.8 10.0 %collective-permute-start.13 = (bf16[128,1024]{1,0:T(8,128)(2,1)S(1)}, bf16[128,1024]{1,0:T(8,128)(2,1)S(1)}, u32[]{:S(2)}, u32[]{:S(2)}) collective-permute-start(bf16[128,1024]{1,0:T(8,128)(2,1)S(1)} %collective-permute-done.12.refs_7_), channel_id=1, source_target_pairs={{0,4},{4,0},{1,5},{5,1},{2,6},{6,2},{3,7},{7,3},{8,12},{12,8},{9,1... | collective-permute-start | bytes 786440 | tf_op jit(solution)/shard_map/ppermute | solution.py:330
  55.9 8.3 %collective-permute-start.9 = (bf16[128,1024]{1,0:T(8,128)(2,1)S(1)}, bf16[128,1024]{1,0:T(8,128)(2,1)S(1)}, u32[]{:S(2)}, u32[]{:S(2)}) collective-permute-start(bf16[128,1024]{1,0:T(8,128)(2,1)S(1)} %collective-permute-done.8.refs_5_), channel_id=1, source_target_pairs={{0,4},{4,0},{1,5},{5,1},{2,6},{6,2},{3,7},{7,3},{8,12},{12,8},{9,1... | collective-permute-start | bytes 786440 | tf_op jit(solution)/shard_map/ppermute | solution.py:330
  59.4 4.9 %collective-permute-start.2 = (bf16[8,32,512]{2,1,0:T(8,128)(2,1)S(1)}, bf16[8,32,512]{2,1,0:T(8,128)(2,1)S(1)}, u32[]{:S(2)}, u32[]{:S(2)}) collective-permute-start(bf16[8,32,512]{2,1,0:T(8,128)(2,1)S(1)} %all-to-all-done.refs_8_), channel_id=1, source_target_pairs={{0,1},{1,0},{2,3},{3,2},{4,5},{5,4},{6,7},{7,6},{8,9},{9,8},{10,11... | collective-permute-start | bytes 786440 | tf_op jit(solution)/shard_map/ppermute | solution.py:330
  62.6 2.6 collective-permute-start.3
  65.3 12.2 %copy-start.13 = (bf16[2,128,1024]{2,1,0:T(8,128)(2,1)}, bf16[2,128,1024]{2,1,0:T(8,128)(2,1)S(1)}, u32[]{:S(2)}) copy-start(bf16[2,128,1024]{2,1,0:T(8,128)(2,1)S(1)} %collective-permute-done.4.cot_1) | copy-start | bytes 1572868
  66.0 11.5 %collective-permute-start.14 = (bf16[4,128,256]{2,1,0:T(8,128)(2,1)S(1)}, bf16[4,128,256]{2,1,0:T(8,128)(2,1)S(1)}, u32[]{:S(2)}, u32[]{:S(2)}) collective-permute-start(bf16[4,128,256]{2,1,0:T(8,128)(2,1)S(1)} %pad_maximum_fusion.4), channel_id=1, source_target_pairs={{0,4},{4,0},{1,5},{5,1},{2,6},{6,2},{3,7},{7,3},{8,12},{12,8},{9,1... | collective-permute-start | bytes 786440 | tf_op jit(solution)/shard_map/ppermute | solution.py:330
  77.6 22.8 %copy-start.12 = (bf16[2,4,128,256]{3,2,1,0:T(8,128)(2,1)}, bf16[2,4,128,256]{3,2,1,0:T(8,128)(2,1)S(1)}, u32[]{:S(2)}) copy-start(bf16[2,4,128,256]{3,2,1,0:T(8,128)(2,1)S(1)} %pad_maximum_fusion.3.own_ref) | copy-start | bytes 1572868
  77.6 20.6 %collective-permute-start.15 = (bf16[2,4,128,256]{3,2,1,0:T(8,128)(2,1)S(1)}, bf16[2,4,128,256]{3,2,1,0:T(8,128)(2,1)S(1)}, u32[]{:S(2)}, u32[]{:S(2)}) collective-permute-start(bf16[2,4,128,256]{3,2,1,0:T(8,128)(2,1)S(1)} %pad_maximum_fusion.3.own_ref), channel_id=1, source_target_pairs={{0,2},{2,0},{1,3},{3,1},{4,6},{6,4},{5,7},{7,5},{8,10},{10,8},{9,1... | collective-permute-start | bytes 1572872 | tf_op jit(solution)/shard_map/ppermute | solution.py:330
  77.7 20.6 %collective-permute-start.16 = (bf16[2,4,128,256]{3,2,1,0:T(8,128)(2,1)S(1)}, bf16[2,4,128,256]{3,2,1,0:T(8,128)(2,1)S(1)}, u32[]{:S(2)}, u32[]{:S(2)}) collective-permute-start(bf16[2,4,128,256]{3,2,1,0:T(8,128)(2,1)S(1)} %pad_maximum_fusion.3.own_ref), channel_id=1, source_target_pairs={{0,1},{1,0},{2,3},{3,2},{4,5},{5,4},{6,7},{7,6},{8,9},{9,8},{10,11... | collective-permute-start | bytes 1572872 | tf_op jit(solution)/shard_map/ppermute | solution.py:330
  98.2 2.1 collective-permute-start.17
  105.1 14.7 %collective-permute-start.22 = (bf16[4,512,512]{2,1,0:T(8,128)(2,1)}, bf16[4,512,512]{2,1,0:T(8,128)(2,1)S(1)}, u32[]{:S(2)}, u32[]{:S(2)}) collective-permute-start(bf16[4,512,512]{2,1,0:T(8,128)(2,1)} %bitcast.134), channel_id=1, source_target_pairs={{0,1},{1,0},{2,3},{3,2},{4,5},{5,4},{6,7},{7,6},{8,9},{9,8},{10,11... | collective-permute-start | bytes 6291464 | tf_op jit(solution)/shard_map/ppermute | solution.py:330
  106.4 8.0 %collective-permute-start.18 = (bf16[128,1024]{1,0:T(8,128)(2,1)}, bf16[128,1024]{1,0:T(8,128)(2,1)S(1)}, u32[]{:S(2)}, u32[]{:S(2)}) collective-permute-start(bf16[128,1024]{1,0:T(8,128)(2,1)} %get-tuple-element.180.m_own), channel_id=1, source_target_pairs={{0,4},{4,0},{1,5},{5,1},{2,6},{6,2},{3,7},{7,3},{8,12},{12,8},{9,1... | collective-permute-start | bytes 786440 | tf_op jit(solution)/shard_map/ppermute | solution.py:330
  106.4 8.0 %collective-permute-start.19 = (bf16[128,1024]{1,0:T(8,128)(2,1)}, bf16[128,1024]{1,0:T(8,128)(2,1)S(1)}, u32[]{:S(2)}, u32[]{:S(2)}) collective-permute-start(bf16[128,1024]{1,0:T(8,128)(2,1)} %get-tuple-element.180.m_own), channel_id=1, source_target_pairs={{0,2},{2,0},{1,3},{3,1},{4,6},{6,4},{5,7},{7,5},{8,10},{10,8},{9,1... | collective-permute-start | bytes 786440 | tf_op jit(solution)/shard_map/ppermute | solution.py:330
  114.4 3.9 %collective-permute-start.20 = (bf16[64,1024]{1,0:T(8,128)(2,1)S(1)}, bf16[64,1024]{1,0:T(8,128)(2,1)S(1)}, u32[]{:S(2)}, u32[]{:S(2)}) collective-permute-start(bf16[64,1024]{1,0:T(8,128)(2,1)S(1)} %slice.157), channel_id=1, source_target_pairs={{0,4},{4,0},{1,5},{5,1},{2,6},{6,2},{3,7},{7,3},{8,12},{12,8},{9,1... | collective-permute-start | bytes 393224 | tf_op jit(solution)/shard_map/ppermute | solution.py:330
  115.7 4.2 %collective-permute-start.21 = (bf16[64,1024]{1,0:T(8,128)(2,1)S(1)}, bf16[64,1024]{1,0:T(8,128)(2,1)S(1)}, u32[]{:S(2)}, u32[]{:S(2)}) collective-permute-start(bf16[64,1024]{1,0:T(8,128)(2,1)S(1)} %slice.158), channel_id=1, source_target_pairs={{0,2},{2,0},{1,3},{3,1},{4,6},{6,4},{5,7},{7,5},{8,10},{10,8},{9,1... | collective-permute-start | bytes 393224 | tf_op jit(solution)/shard_map/ppermute | solution.py:330
  130.1 7.0 %collective-permute-start.23 = (bf16[64,1024]{1,0:T(8,128)(2,1)S(1)}, bf16[64,1024]{1,0:T(8,128)(2,1)S(1)}, u32[]{:S(2)}, u32[]{:S(2)}) collective-permute-start(bf16[64,1024]{1,0:T(8,128)(2,1)S(1)} %get-tuple-element.301), channel_id=1, source_target_pairs={{0,4},{4,0},{1,5},{5,1},{2,6},{6,2},{3,7},{7,3},{8,12},{12,8},{9,1... | collective-permute-start | bytes 393224 | tf_op jit(solution)/shard_map/ppermute | solution.py:330
  130.5 6.6 %collective-permute-start.24 = (bf16[64,1024]{1,0:T(8,128)(2,1)S(1)}, bf16[64,1024]{1,0:T(8,128)(2,1)S(1)}, u32[]{:S(2)}, u32[]{:S(2)}) collective-permute-start(bf16[64,1024]{1,0:T(8,128)(2,1)S(1)} %get-tuple-element.300), channel_id=1, source_target_pairs={{0,2},{2,0},{1,3},{3,1},{4,6},{6,4},{5,7},{7,5},{8,10},{10,8},{9,1... | collective-permute-start | bytes 393224 | tf_op jit(solution)/shard_map/ppermute | solution.py:330
  137.1 7.0 %collective-permute-start.27 = (bf16[4,528,512]{2,1,0:T(8,128)(2,1)}, bf16[4,528,512]{2,1,0:T(8,128)(2,1)S(1)}, u32[]{:S(2)}, u32[]{:S(2)}) collective-permute-start(bf16[4,528,512]{2,1,0:T(8,128)(2,1)} %get-tuple-element.203), channel_id=1, source_target_pairs={{0,1},{1,0},{2,3},{3,2},{4,5},{5,4},{6,7},{7,6},{8,9},{9,8},{10,11... | collective-permute-start | bytes 6488072 | tf_op jit(solution)/shard_map/ppermute | solution.py:330
  140.2 8.0 %collective-permute-start.25 = (bf16[128,1024]{1,0:T(8,128)(2,1)S(1)}, bf16[128,1024]{1,0:T(8,128)(2,1)S(1)}, u32[]{:S(2)}, u32[]{:S(2)}) collective-permute-start(bf16[128,1024]{1,0:T(8,128)(2,1)S(1)} %pad_maximum_fusion.6), channel_id=1, source_target_pairs={{0,2},{2,0},{1,3},{3,1},{4,6},{6,4},{5,7},{7,5},{8,10},{10,8},{9,1... | collective-permute-start | bytes 786440 | tf_op jit(solution)/shard_map/ppermute | solution.py:330
  140.9 7.6 %collective-permute-start.26 = (bf16[128,1024]{1,0:T(8,128)(2,1)S(1)}, bf16[128,1024]{1,0:T(8,128)(2,1)S(1)}, u32[]{:S(2)}, u32[]{:S(2)}) collective-permute-start(bf16[128,1024]{1,0:T(8,128)(2,1)S(1)} %pad_maximum_fusion.5), channel_id=1, source_target_pairs={{0,4},{4,0},{1,5},{5,1},{2,6},{6,2},{3,7},{7,3},{8,12},{12,8},{9,1... | collective-permute-start | bytes 786440 | tf_op jit(solution)/shard_map/ppermute | solution.py:330
  154.7 20.4 %collective-permute-start.28 = (bf16[2,2,4,32,1024]{4,3,2,1,0:T(8,128)(2,1)}, bf16[2,2,4,32,1024]{4,3,2,1,0:T(8,128)(2,1)S(1)}, u32[]{:S(2)}, u32[]{:S(2)}) collective-permute-start(bf16[2,2,4,32,1024]{4,3,2,1,0:T(8,128)(2,1)} %get-tuple-element.208), channel_id=1, source_target_pairs={{0,1},{1,0},{2,3},{3,2},{4,5},{5,4},{6,7},{7,6},{8,9},{9,8},{10,11... | collective-permute-start | bytes 3145736 | tf_op jit(solution)/shard_map/ppermute | solution.py:330
  155.9 19.2 %all-to-all-start.3 = ((bf16[8,128,128]{2,1,0:T(8,128)(2,1)}), bf16[8,128,128]{2,1,0:T(8,128)(2,1)S(1)}, u32[]{:S(2)}, u32[]{:S(2)}) async-start(bf16[8,128,128]{2,1,0:T(8,128)(2,1)} %get-tuple-element.207), calls=%async_computation.3 | async-start | bytes 524288 | tf_op jit(solution)/shard_map/all_to_all | solution.py:338
  161.8 13.3 %copy-start.15 = (bf16[2,2,4,32,1024]{4,3,2,1,0:T(8,128)(2,1)S(1)}, bf16[2,2,4,32,1024]{4,3,2,1,0:T(8,128)(2,1)}, u32[]{:S(2)}) copy-start(bf16[2,2,4,32,1024]{4,3,2,1,0:T(8,128)(2,1)} %get-tuple-element.226) | copy-start | bytes 3145732
  175.6 12.6 %collective-permute-start.29 = (bf16[2,4,32,1024]{3,2,1,0:T(8,128)(2,1)S(1)}, bf16[2,4,32,1024]{3,2,1,0:T(8,128)(2,1)S(1)}, u32[]{:S(2)}, u32[]{:S(2)}) collective-permute-start(bf16[2,4,32,1024]{3,2,1,0:T(8,128)(2,1)S(1)} %get-tuple-element.289), channel_id=1, source_target_pairs={{0,2},{2,0},{1,3},{3,1},{4,6},{6,4},{5,7},{7,5},{8,10},{10,8},{9,1... | collective-permute-start | bytes 1572872 | tf_op jit(solution)/shard_map/ppermute | solution.py:330
  188.2 3.5 %collective-permute-start.30 = (bf16[2,8,32,512]{3,2,1,0:T(8,128)(2,1)}, bf16[2,8,32,512]{3,2,1,0:T(8,128)(2,1)S(1)}, u32[]{:S(2)}, u32[]{:S(2)}) collective-permute-start(bf16[2,8,32,512]{3,2,1,0:T(8,128)(2,1)} %get-tuple-element.229), channel_id=1, source_target_pairs={{0,1},{1,0},{2,3},{3,2},{4,5},{5,4},{6,7},{7,6},{8,9},{9,8},{10,11... | collective-permute-start | bytes 1572872 | tf_op jit(solution)/shard_map/ppermute | solution.py:330
  190.1 22.8 %copy-start.19 = (bf16[2,128,1024]{2,1,0:T(8,128)(2,1)S(1)}, bf16[2,128,1024]{2,1,0:T(8,128)(2,1)}, u32[]{:S(2)}) copy-start(bf16[2,128,1024]{2,1,0:T(8,128)(2,1)} %get-tuple-element.212) | copy-start | bytes 1572868
  190.2 8.1 %collective-permute-start.33 = (bf16[4,32,1024]{2,1,0:T(8,128)(2,1)S(1)}, bf16[4,32,1024]{2,1,0:T(8,128)(2,1)}, u32[]{:S(2)}, u32[]{:S(2)}) collective-permute-start(bf16[4,32,1024]{2,1,0:T(8,128)(2,1)S(1)} %get-tuple-element.291), channel_id=1, source_target_pairs={{0,4},{4,0},{1,5},{5,1},{2,6},{6,2},{3,7},{7,3},{8,12},{12,8},{9,1... | collective-permute-start | bytes 786440 | tf_op jit(solution)/shard_map/ppermute | solution.py:330
  192.9 30.6 %copy-start.3 = (s32[41]{0:T(128)S(1)}, s32[41]{0:T(128)}, u32[]{:S(2)}) copy-start(s32[41]{0:T(128)} %concatenate.13.meta.table) | copy-start | bytes 496
  192.9 7.6 %collective-permute-start.32 = (bf16[8,32,512]{2,1,0:T(8,128)(2,1)S(1)}, bf16[8,32,512]{2,1,0:T(8,128)(2,1)S(1)}, u32[]{:S(2)}, u32[]{:S(2)}) collective-permute-start(bf16[8,32,512]{2,1,0:T(8,128)(2,1)S(1)} %get-tuple-element.292), channel_id=1, source_target_pairs={{0,2},{2,0},{1,3},{3,1},{4,6},{6,4},{5,7},{7,5},{8,10},{10,8},{9,1... | collective-permute-start | bytes 786440 | tf_op jit(solution)/shard_map/ppermute | solution.py:330
  193.7 29.7 %collective-permute-start.35 = (bf16[4,128,1024]{2,1,0:T(8,128)(2,1)}, bf16[4,128,1024]{2,1,0:T(8,128)(2,1)S(1)}, u32[]{:S(2)}, u32[]{:S(2)}) collective-permute-start(bf16[4,128,1024]{2,1,0:T(8,128)(2,1)} %get-tuple-element.236), channel_id=1, source_target_pairs={{0,4},{4,0},{1,5},{5,1},{2,6},{6,2},{3,7},{7,3},{8,12},{12,8},{9,1... | collective-permute-start | bytes 3145736 | tf_op jit(solution)/shard_map/ppermute | solution.py:330
  194.6 18.3 %collective-permute-start.31 = (bf16[2,128,1024]{2,1,0:T(8,128)(2,1)}, bf16[2,128,1024]{2,1,0:T(8,128)(2,1)}, u32[]{:S(2)}, u32[]{:S(2)}) collective-permute-start(bf16[2,128,1024]{2,1,0:T(8,128)(2,1)} %get-tuple-element.230), channel_id=1, source_target_pairs={{0,2},{2,0},{1,3},{3,1},{4,6},{6,4},{5,7},{7,5},{8,10},{10,8},{9,1... | collective-permute-start | bytes 1572872 | tf_op jit(solution)/shard_map/ppermute | solution.py:330
  195.2 39.6 %copy-start.14 = (bf16[4,128,1024]{2,1,0:T(8,128)(2,1)S(1)}, bf16[4,128,1024]{2,1,0:T(8,128)(2,1)}, u32[]{:S(2)}) copy-start(bf16[4,128,1024]{2,1,0:T(8,128)(2,1)} %get-tuple-element.247) | copy-start | bytes 3145732
  201.2 22.2 %all-to-all-start.4 = ((bf16[8,32,512]{2,1,0:T(8,128)(2,1)}), bf16[8,32,512]{2,1,0:T(8,128)(2,1)S(1)}, u32[]{:S(2)}, u32[]{:S(2)}) async-start(bf16[8,32,512]{2,1,0:T(8,128)(2,1)} %add_convert_fusion.7), calls=%async_computation.4 | async-start | bytes 524288 | tf_op jit(solution)/shard_map/all_to_all | solution.py:338
  209.4 9.0 %collective-permute-start.36 = (bf16[32,1024]{1,0:T(8,128)(2,1)}, bf16[32,1024]{1,0:T(8,128)(2,1)S(1)}, u32[]{:S(2)}, u32[]{:S(2)}) collective-permute-start(bf16[32,1024]{1,0:T(8,128)(2,1)} %get-tuple-element.297), channel_id=1, source_target_pairs={{0,8},{8,16},{16,24},{24,0},{1,9},{9,17},{17,25},{25,1},{2,10},{10... | collective-permute-start | bytes 196616 | tf_op jit(solution)/shard_map/ppermute | solution.py:334
  210.6 7.8 %collective-permute-start.37 = (bf16[32,1024]{1,0:T(8,128)(2,1)}, bf16[32,1024]{1,0:T(8,128)(2,1)S(1)}, u32[]{:S(2)}, u32[]{:S(2)}) collective-permute-start(bf16[32,1024]{1,0:T(8,128)(2,1)} %get-tuple-element.296), channel_id=1, source_target_pairs={{0,16},{8,24},{16,0},{24,8},{1,17},{9,25},{17,1},{25,9},{2,18},{10... | collective-permute-start | bytes 196616 | tf_op jit(solution)/shard_map/ppermute | solution.py:334
  211.6 8.9 %collective-permute-start.38 = (bf16[32,1024]{1,0:T(8,128)(2,1)S(1)}, bf16[32,1024]{1,0:T(8,128)(2,1)S(1)}, u32[]{:S(2)}, u32[]{:S(2)}) collective-permute-start(bf16[32,1024]{1,0:T(8,128)(2,1)S(1)} %get-tuple-element.295), channel_id=1, source_target_pairs={{0,24},{8,0},{16,8},{24,16},{1,25},{9,1},{17,9},{25,17},{2,26},{10... | collective-permute-start | bytes 196616 | tf_op jit(solution)/shard_map/ppermute | solution.py:334
  214.7 30.5 %collective-permute-start.34 = (bf16[128,1024]{1,0:T(8,128)(2,1)}, bf16[128,1024]{1,0:T(8,128)(2,1)}, u32[]{:S(2)}, u32[]{:S(2)}) collective-permute-start(bf16[128,1024]{1,0:T(8,128)(2,1)} %fusion.16), channel_id=1, source_target_pairs={{0,4},{4,0},{1,5},{5,1},{2,6},{6,2},{3,7},{7,3},{8,12},{12,8},{9,1... | collective-permute-start | bytes 786440 | tf_op jit(solution)/shard_map/ppermute | solution.py:330
  223.4 21.8 %copy-start.1 = (bf16[8,32,512]{2,1,0:T(8,128)(2,1)}, bf16[8,32,512]{2,1,0:T(8,128)(2,1)S(1)}, u32[]{:S(2)}) copy-start(bf16[8,32,512]{2,1,0:T(8,128)(2,1)S(1)} %all-to-all-done.4.qkv_ref.refs_1_) | copy-start | bytes 786436
  227.2 12.3 %all-to-all-start.5 = ((f32[32,1,128]{2,1,0:T(1,128)}), f32[32,1,128]{2,1,0:T(1,128)S(1)}, u32[]{:S(2)}, u32[]{:S(2)}) async-start(f32[32,1,128]{2,1,0:T(1,128)} %get-tuple-element.244), calls=%async_computation.6 | async-start | bytes 32768 | tf_op jit(solution)/shard_map/all_to_all | solution.py:338
  236.0 19.0 %collective-permute-start.39 = (bf16[128,1024]{1,0:T(8,128)(2,1)}, bf16[128,1024]{1,0:T(8,128)(2,1)S(1)}, u32[]{:S(2)}, u32[]{:S(2)}) collective-permute-start(bf16[128,1024]{1,0:T(8,128)(2,1)} %get-tuple-element.287), channel_id=1, source_target_pairs={{0,8},{8,16},{16,24},{24,0},{1,9},{9,17},{17,25},{25,1},{2,10},{10... | collective-permute-start | bytes 786440 | tf_op jit(solution)/shard_map/ppermute | solution.py:334
  237.1 22.5 %collective-permute-start.40 = (bf16[128,1024]{1,0:T(8,128)(2,1)}, bf16[128,1024]{1,0:T(8,128)(2,1)S(1)}, u32[]{:S(2)}, u32[]{:S(2)}) collective-permute-start(bf16[128,1024]{1,0:T(8,128)(2,1)} %get-tuple-element.286), channel_id=1, source_target_pairs={{0,16},{8,24},{16,0},{24,8},{1,17},{9,25},{17,1},{25,9},{2,18},{10... | collective-permute-start | bytes 786440 | tf_op jit(solution)/shard_map/ppermute | solution.py:334
  238.3 23.9 %collective-permute-start.41 = (bf16[128,1024]{1,0:T(8,128)(2,1)}, bf16[128,1024]{1,0:T(8,128)(2,1)S(1)}, u32[]{:S(2)}, u32[]{:S(2)}) collective-permute-start(bf16[128,1024]{1,0:T(8,128)(2,1)} %get-tuple-element.285), channel_id=1, source_target_pairs={{0,24},{8,0},{16,8},{24,16},{1,25},{9,1},{17,9},{25,17},{2,26},{10... | collective-permute-start | bytes 786440 | tf_op jit(solution)/shard_map/ppermute | solution.py:334
  239.6 12.1 %all-to-all-start.6 = ((bf16[8,32,512]{2,1,0:T(8,128)(2,1)}), bf16[8,32,512]{2,1,0:T(8,128)(2,1)}, u32[]{:S(2)}, u32[]{:S(2)}) async-start(bf16[8,32,512]{2,1,0:T(8,128)(2,1)} %bitcast.143), calls=%async_computation.7 | async-start | bytes 524288 | tf_op jit(solution)/shard_map/all_to_all | solution.py:338
  (28 other events, 101.6 us)
Sparse Core Ops, SparseCore 0:
  47.5 49.6 all-gather.2
  146.2 50.0 reduce-scatter.1

commit v3 on v2

--- a/solution.py
+++ b/solution.py
@@ -925,7 +925,6 @@
 
     mlp_y = exchange(mlp_low, "y")
     mlp_x = exchange(mlp_low, "x")
-    mlp_y, mlp_x = gate(mlp_y, mlp_x)
     mlp_d0 = exchange(mlp_x[:half], "y")
     mlp_d1 = exchange(mlp_y[half:], "x")
     ff_other = exchange(after(ff_all, mlp_low), "c")
@@ -999,7 +998,6 @@
     out_two = add_low(out_c[0], out_x_got[0])
     out_y_got = exchange(add_low(out_c[1], out_x_got[1]), "y")
     in_got = exchange(after(in_give, qkv_c), "y")
-    result_x = exchange(after(result_give, qkv_c), "x")
     qkv_x_got, qkv_c, out_y_got = gate(qkv_x_got, qkv_c, out_y_got)
     qkv_x = add_low(qkv_c, qkv_x_got)
 
@@ -1008,7 +1006,7 @@
     out_own = add_low(out_two[0], out_y_got[0])
     out_moved = [shift(add_low(out_two[k], out_y_got[k]), "z", nz, -k) for k in range(1, nz)]
     up_send = after(ff_sum, qkv_x)[: 8 * rows].reshape(8, rows, ff)
-    result_x = after(result_x, qkv_x)
+    result_x = exchange(after(result_give, qkv_x), "x")
     result_y = exchange(add_low(result_keep[1], result_x[1]), "y")
     qkv_got, in_got, up_send, *out_moved = gate(qkv_got, in_got, up_send, *out_moved)
     shapes = [((4 * n_ctx, 1, 128), f32), ((rows, width), f32), ((8, rows), f32)]

time: 272 us -> 270 us (level)
    all_to_all x6, waiting for transfers between devices: 20 us -> 16.4 us  [swap(): return lax.all_to_all(v, axes, 0, 0, tiled=True)]
    unnamed x84 -> x86, local copies, waits for them, and re-layouts: 6.09 us -> 6.12 us
  transfers between devices with their start and end apart: 50 -> 50, of which waited for: 21 -> 23; matrix products, arithmetic and copies ran while one was open for 8% -> 8% of each run, Pallas kernels for 19% -> 18%
where the time goes in v3:
time: 270 us; the launch traced here: 269 us
  starting transfers between devices  88.6 us (33%)
  Pallas kernels  63.2 us (23%)
  waiting for transfers between devices  55.9 us (21%)
  other arithmetic  17.4 us (6%)
  blocking collectives  16.4 us (6%)
  between operations  15.3 us (6%)
  local copies, waits for them, and re-layouts  12.5 us (5%)
    pallas_call x11, Pallas kernels, call(): pl.pallas_call(kernel, out_shape=[jax.ShapeDtypeStruct(s, d) for s, d in...  63.2 us
    all_to_all x6, starting transfers between devices, swap(): return lax.all_to_all(v, axes, 0, 0, tiled=True)  45.1 us
    ppermute x30, starting transfers between devices, exchange(): return lax.ppermute(v, axis, [(0, 1), (1, 0)])  29.5 us
    ppermute x30, waiting for transfers between devices, exchange(): return lax.ppermute(v, axis, [(0, 1), (1, 0)])  24.9 us
    all_to_all x6, waiting for transfers between devices, swap(): return lax.all_to_all(v, axes, 0, 0, tiled=True)  16.4 us
    all_to_all x1, blocking collectives, swap(): return lax.all_to_all(v, axes, 0, 0, tiled=True)  16.4 us
    ppermute x12, waiting for transfers between devices, shift(): return lax.ppermute(v, axis, [(i, (i - k) % n_line) for i in range(n_line)])  14.5 us
    ppermute x12, starting transfers between devices, shift(): return lax.ppermute(v, axis, [(i, (i - k) % n_line) for i in range(n_line)])  14 us
  transfers between devices with their start and end apart: 50, of which 23 were waited for; matrix products, arithmetic and copies ran while one was open for 8% of the time, Pallas kernels for 18%

profile of v3, /device:TPU:11, one launch (start us, length us, event | category | flops | bytes accessed | tf_op | source)
XLA Modules:
  0.0 269.1 jit_solution(13669793896225380487)
XLA Ops:
  7.9 2.4 shard_map.421
  10.3 5.9 %all-to-all-start = ((bf16[8,32,512]{2,1,0:T(8,128)(2,1)}), bf16[8,32,512]{2,1,0:T(8,128)(2,1)S(1)}, u32[]{:S(2)}, u32[]{:S(2)}) async-start(bf16[8,32,512]{2,1,0:T(8,128)(2,1)} %get-tuple-element.152), calls=%async_computation | async-start | bytes 524288 | tf_op jit(solution)/shard_map/all_to_all | solution.py:338
  16.2 1.2 collective-permute-start
  17.5 2.1 collective-permute-start.10
  19.5 1.5 collective-permute-start.8
  21.0 5.0 %all-to-all-done.refs_8_ = bf16[8,32,512]{2,1,0:T(8,128)(2,1)S(1)} async-done(((bf16[8,32,512]{2,1,0:T(8,128)(2,1)}), bf16[8,32,512]{2,1,0:T(8,128)(2,1)S(1)}, u32[]{:S(2)}, u32[]{:S(2)}) %all-to-all-start) | async-done | bytes 262176 | tf_op jit(solution)/shard_map/all_to_all | solution.py:338
  26.0 14.4 %all-to-all-start.1 = ((bf16[8,32,512]{2,1,0:T(8,128)(2,1)}), bf16[8,32,512]{2,1,0:T(8,128)(2,1)S(1)}, u32[]{:S(2)}, u32[]{:S(2)}) async-start(bf16[8,32,512]{2,1,0:T(8,128)(2,1)} %get-tuple-element.153), calls=%async_computation.1 | async-start | bytes 524288 | tf_op jit(solution)/shard_map/all_to_all | solution.py:338
  41.2 1.2 collective-permute-start.11
  42.4 3.3 %all-to-all-done.1 = bf16[8,32,512]{2,1,0:T(8,128)(2,1)S(1)} async-done(((bf16[8,32,512]{2,1,0:T(8,128)(2,1)}), bf16[8,32,512]{2,1,0:T(8,128)(2,1)S(1)}, u32[]{:S(2)}, u32[]{:S(2)}) %all-to-all-start.1) | async-done | bytes 262176 | tf_op jit(solution)/shard_map/all_to_all | solution.py:338
  49.9 1.9 collective-permute-start.5
  51.8 1.3 collective-permute-start.7
  54.0 2.0 collective-permute-done.6
  56.1 3.3 %collective-permute-done.7 = bf16[128,256]{1,0:T(8,128)(2,1)S(1)} collective-permute-done((bf16[128,256]{1,0:T(8,128)(2,1)S(1)}, bf16[128,256]{1,0:T(8,128)(2,1)S(1)}, u32[]{:S(2)}, u32[]{:S(2)}) %collective-permute-start.7) | collective-permute-done | bytes 65568 | tf_op jit(solution)/shard_map/ppermute | solution.py:334
  59.4 3.2 %collective-permute-start.2 = (bf16[8,32,512]{2,1,0:T(8,128)(2,1)S(1)}, bf16[8,32,512]{2,1,0:T(8,128)(2,1)S(1)}, u32[]{:S(2)}, u32[]{:S(2)}) collective-permute-start(bf16[8,32,512]{2,1,0:T(8,128)(2,1)S(1)} %all-to-all-done.refs_8_), channel_id=1, source_target_pairs={{0,1},{1,0},{2,3},{3,2},{4,5},{5,4},{6,7},{7,6},{8,9},{9,8},{10,11... | collective-permute-start | bytes 786440 | tf_op jit(solution)/shard_map/ppermute | solution.py:330
  62.7 1.1 convert_reduce_fusion
  64.2 1.0 collective-permute-done.4.cot_1
  66.1 11.4 %shard_map.422 = (bf16[1024,128]{1,0:T(8,128)(2,1)}, f32[128,1024]{1,0:T(8,128)}, bf16[1024,384]{1,0:T(8,128)(2,1)}, f32[8,1024]{1,0:T(8,128)}, bf16[1024,1024]{...) custom-call(s32[41]{0:T(128)} %concatenate.13.meta.table, ...), custom_call_target="tpu_custom_call" | custom-call | flops 8999999488 | bytes 8999999488 | tf_op jit(solution)/shard_map/pallas_call | solution.py:813
  77.7 4.2 %collective-permute-start.16 = (bf16[2,4,128,256]{3,2,1,0:T(8,128)(2,1)S(1)}, bf16[2,4,128,256]{3,2,1,0:T(8,128)(2,1)S(1)}, u32[]{:S(2)}, u32[]{:S(2)}) collective-permute-start(bf16[2,4,128,256]{3,2,1,0:T(8,128)(2,1)S(1)} %pad_maximum_fusion.3.own_ref), channel_id=1, source_target_pairs={{0,1},{1,0},{2,3},{3,2},{4,5},{5,4},{6,7},{7,6},{8,9},{9,8},{10,11... | collective-permute-start | bytes 1572872 | tf_op jit(solution)/shard_map/ppermute | solution.py:330
  81.8 16.4 %all_to_all.35.att = bf16[8,128,128]{2,1,0:T(8,128)(2,1)} all-to-all(bf16[8,128,128]{2,1,0:T(8,128)(2,1)} %bitcast.149), channel_id=1, replica_groups=mesh['z'=4,'y'=2,'x'=2,'c'=2] {'z','y'}, dimensions={0} | all-to-all | bytes 524288 | tf_op jit(solution)/shard_map/all_to_all | solution.py:338
  98.8 1.5 collective-permute-done.17.cx_ref
  101.1 3.9 %shard_map.423 = (f32[128,1024]{1,0:T(8,128)}, bf16[128,1024]{1,0:T(8,128)(2,1)}, bf16[1024,1024]{1,0:T(8,128)(2,1)}) custom-call(s32[41]{0:T(128)} %concatenate.13.meta.table, bf16[8,128,128]{2,1,0:T(8,128)(2,1)} %all_to_all.35.att, bf16[2,4,128,256]{3,2,1,0:T(8,128)(2,1)} %copy-done.12, bf16[2,4,128,256]{3,2,1,0:T(8,128)(2,1)} %copy-done.20, ...), custom_call_target="tpu_custom_call" | custom-call | flops 1 | bytes 1 | tf_op jit(solution)/shard_map/pallas_call | solution.py:813
  107.9 6.5 %collective-permute-done.19.m_x = bf16[128,1024]{1,0:T(8,128)(2,1)S(1)} collective-permute-done((bf16[128,1024]{1,0:T(8,128)(2,1)}, bf16[128,1024]{1,0:T(8,128)(2,1)S(1)}, u32[]{:S(2)}, u32[]{:S(2)}) %collective-permute-start.19) | collective-permute-done | bytes 262176 | tf_op jit(solution)/shard_map/ppermute | solution.py:330
  116.2 2.1 collective-permute-done.20.m_d0
  120.4 7.9 %shard_map.424 = (bf16[128,1024]{1,0:T(8,128)(2,1)}, bf16[128,1024]{1,0:T(8,128)(2,1)}, bf16[128,1024]{1,0:T(8,128)(2,1)}, bf16[128,1024]{1,0:T(8,128)(2,1)}, bf...) custom-call(bf16[128,1024]{1,0:T(8,128)(2,1)} %get-tuple-element.177.m_own, ...), custom_call_target="tpu_custom_call" | custom-call | flops 1 | bytes 1 | tf_op jit(solution)/shard_map/pallas_call | solution.py:813
  129.2 1.1 collective-permute-start.23
  131.2 5.9 %shard_map.425 = (bf16[4,528,512]{2,1,0:T(8,128)(2,1)}, bf16[4,528,512]{2,1,0:T(8,128)(2,1)}) custom-call(bf16[512,1024]{1,0:T(8,128)(2,1)} %get-tuple-element.187.mlp_ref, bf16[512,1024]{1,0:T(8,128)(2,1)} %get-tuple-element.188.pre_ref, bf16[512,1024]{1,0:T(8,128)(2,1)} %get-tuple-element.204.hidden_ref, bf16[2,128,1024]{2,1,0:T(8,128)(2,1)} %copy-done.8, ...), custom_call_target="tpu_custom_call" | custom-call | flops 1 | bytes 1 | tf_op jit(solution)/shard_map/pallas_call | solution.py:813
  137.1 2.7 %collective-permute-start.27 = (bf16[4,528,512]{2,1,0:T(8,128)(2,1)}, bf16[4,528,512]{2,1,0:T(8,128)(2,1)S(1)}, u32[]{:S(2)}, u32[]{:S(2)}) collective-permute-start(bf16[4,528,512]{2,1,0:T(8,128)(2,1)} %get-tuple-element.198), channel_id=1, source_target_pairs={{0,1},{1,0},{2,3},{3,2},{4,5},{5,4},{6,7},{7,6},{8,9},{9,8},{10,11... | collective-permute-start | bytes 6488072 | tf_op jit(solution)/shard_map/ppermute | solution.py:330
  141.2 2.7 %collective-permute-done.27 = bf16[4,528,512]{2,1,0:T(8,128)(2,1)S(1)} collective-permute-done((bf16[4,528,512]{2,1,0:T(8,128)(2,1)}, bf16[4,528,512]{2,1,0:T(8,128)(2,1)S(1)}, u32[]{:S(2)}, u32[]{:S(2)}) %collective-permute-start.27) | collective-permute-done | bytes 2162720 | tf_op jit(solution)/shard_map/ppermute | solution.py:330
  143.9 1.9 add_convert_fusion
  145.8 2.1 collective-permute-done.25.got_x
  149.1 5.6 %shard_map.426 = (f32[128,1024]{1,0:T(8,128)}, bf16[8,128,128]{2,1,0:T(8,128)(2,1)}, f32[8,1024]{1,0:T(8,128)}, bf16[2,2,4,32,1024]{4,3,2,1,0:T(8,128)(2,1)}, bf16[2,2,4,32,1024]{4,3,2,1,0:T(8,128)(2,1)}) custom-call(s32[41]{0:T(128)} %concatenate.13.meta.table, bf16[128,1024]{1,0:T(8,128)(2,1)} %get-tuple-element.184.own, bf16[128,1024]{1,0:T(8,128)(2,1)} %copy-done.25, ...), custom_call_target="tpu_custom_call" | custom-call | flops 1 | bytes 1 | tf_op jit(solution)/shard_map/pallas_call | solution.py:813
  154.7 1.1 collective-permute-start.28
  155.8 5.1 %all-to-all-start.3 = ((bf16[8,128,128]{2,1,0:T(8,128)(2,1)}), bf16[8,128,128]{2,1,0:T(8,128)(2,1)S(1)}, u32[]{:S(2)}, u32[]{:S(2)}) async-start(bf16[8,128,128]{2,1,0:T(8,128)(2,1)} %get-tuple-element.202), calls=%async_computation.3 | async-start | bytes 524288 | tf_op jit(solution)/shard_map/all_to_all | solution.py:338
  161.0 5.1 %shard_map.427 = (bf16[2,128,1024]{2,1,0:T(8,128)(2,1)}, bf16[2,128,1024]{2,1,0:T(8,128)(2,1)}) custom-call(bf16[512,1024]{1,0:T(8,128)(2,1)} %get-tuple-element.204.hidden_ref, bf16[4,512,512]{2,1,0:T(8,128)(2,1)} %bitcast.138, bf16[4,512,512]{2,1,0:T(8,128)(2,1)} %copy-done.5), custom_call_target="tpu_custom_call" | custom-call | flops 1 | bytes 1 | tf_op jit(solution)/shard_map/pallas_call | solution.py:813
  166.0 7.0 %all-to-all-done.3 = bf16[8,128,128]{2,1,0:T(8,128)(2,1)S(1)} async-done(((bf16[8,128,128]{2,1,0:T(8,128)(2,1)}), bf16[8,128,128]{2,1,0:T(8,128)(2,1)S(1)}, u32[]{:S(2)}, u32[]{:S(2)}) %all-to-all-start.3) | async-done | bytes 262176 | tf_op jit(solution)/shard_map/all_to_all | solution.py:338
  173.4 2.1 collective-permute-start.29
  175.5 11.9 %shard_map.428 = (bf16[2,8,32,512]{3,2,1,0:T(8,128)(2,1)}, bf16[2,8,32,512]{3,2,1,0:T(8,128)(2,1)}, bf16[4,128,1024]{2,1,0:T(8,128)(2,1)}, bf16[4,128,1024]{2,1,0:T(8,128)(2,1)}) custom-call(s32[41]{0:T(128)} %concatenate.13.meta.table, f32[2]{0:T(128)} %multiply_exponential_fusion.slopes, bf16[1024,128]{1,0:T(8,128)(2,1)} %bitcast.148, ...), custom_call_target="tpu_custom_call" | custom-call | flops 8999999488 | bytes 8999999488 | tf_op jit(solution)/shard_map/pallas_call | solution.py:813
  190.2 1.2 fusion.15
  191.4 1.5 collective-permute-start.31
  192.9 3.8 %collective-permute-done.32 = bf16[4,32,1024]{2,1,0:T(8,128)(2,1)S(1)} collective-permute-done((bf16[4,32,1024]{2,1,0:T(8,128)(2,1)S(1)}, bf16[4,32,1024]{2,1,0:T(8,128)(2,1)S(1)}, u32[]{:S(2)}, u32[]{:S(2)}) %collective-permute-start.32) | collective-permute-done | bytes 262176 | tf_op jit(solution)/shard_map/ppermute | solution.py:330
  196.7 2.3 collective-permute-done.31
  199.9 1.5 collective-permute-start.33
  201.4 6.4 %all-to-all-start.4 = ((bf16[8,32,512]{2,1,0:T(8,128)(2,1)}), bf16[8,32,512]{2,1,0:T(8,128)(2,1)S(1)}, u32[]{:S(2)}, u32[]{:S(2)}) async-start(bf16[8,32,512]{2,1,0:T(8,128)(2,1)} %add_convert_fusion.7), calls=%async_computation.4 | async-start | bytes 524288 | tf_op jit(solution)/shard_map/all_to_all | solution.py:338
  207.9 1.6 fusion.29
  209.5 1.2 collective-permute-start.36
  211.7 1.4 collective-permute-start.38
  213.1 1.7 fusion.16
  214.8 1.2 collective-permute-start.34
  216.9 1.7 slice.181
  218.9 1.8 collective-permute-done.38.refs_2_
  220.7 1.2 all-to-all-done.4.qkv_ref.refs_1_
  221.9 1.1 copy-done
  223.1 1.4 shard_map.429
  225.7 7.6 %all-to-all-start.5 = ((f32[32,1,128]{2,1,0:T(1,128)}), f32[32,1,128]{2,1,0:T(1,128)S(1)}, u32[]{:S(2)}, u32[]{:S(2)}) async-start(f32[32,1,128]{2,1,0:T(1,128)} %get-tuple-element.238), calls=%async_computation.6 | async-start | bytes 32768 | tf_op jit(solution)/shard_map/all_to_all | solution.py:338
  233.3 1.1 fusion.19
  234.4 1.2 collective-permute-start.39
  235.7 1.0 collective-permute-start.40
  236.7 1.4 collective-permute-start.41
  238.1 5.7 %all-to-all-start.6 = ((bf16[8,32,512]{2,1,0:T(8,128)(2,1)}), bf16[8,32,512]{2,1,0:T(8,128)(2,1)}, u32[]{:S(2)}, u32[]{:S(2)}) async-start(bf16[8,32,512]{2,1,0:T(8,128)(2,1)} %bitcast.145), calls=%async_computation.7 | async-start | bytes 524288 | tf_op jit(solution)/shard_map/all_to_all | solution.py:338
  243.8 4.5 %shard_map.430 = (f32[1,1]{1,0:T(1,128)}, f32[32,3072]{1,0:T(8,128)}, f32[32,3072]{1,0:T(8,128)}, f32[32,3072]{1,0:T(8,128)}, f32[32,3072]{1,0:T(8,128)}, /*inde...) custom-call(f32[32,1,128]{2,1,0:T(1,128)} %copy-done.31, ...), custom_call_target="tpu_custom_call" | custom-call | flops 1 | bytes 1 | tf_op jit(solution)/shard_map/pallas_call | solution.py:813
  248.3 2.0 fusion.21
  250.3 3.3 %shard_map.431 = (f32[32,4096]{1,0:T(8,128)}, f32[32,4096]{1,0:T(8,128)}, f32[32,4096]{1,0:T(8,128)}, f32[32,4096]{1,0:T(8,128)}) custom-call(f32[32,1,128]{2,1,0:T(1,128)} %copy-done.31, bf16[8,32,512]{2,1,0:T(8,128)(2,1)} %all-to-all-done.6.up_ref, f32[32,4096]{1,0:T(8,128)} %refs_0_.1, f32[32,4096]{1,0:T(8,128)} %refs_1_.1, f32[32,4096]{1,0:T(8,128)} %refs_2_.1), custom_call_target="tpu_custom_call" | custom-call | flops 1 | bytes 1 | tf_op jit(solution)/shard_map/pallas_call | solution.py:813
  253.5 4.6 %collective-permute-done.40 = bf16[128,1024]{1,0:T(8,128)(2,1)S(1)} collective-permute-done((bf16[128,1024]{1,0:T(8,128)(2,1)}, bf16[128,1024]{1,0:T(8,128)(2,1)S(1)}, u32[]{:S(2)}, u32[]{:S(2)}) %collective-permute-start.40) | collective-permute-done | bytes 262176 | tf_op jit(solution)/shard_map/ppermute | solution.py:334
  258.2 2.4 collective-permute-done.41
  (191 shorter events, 29.0 us)
Async XLA Ops:
  10.3 35.4 %copy-start.30 = (bf16[2,128,512]{2,1,0:T(8,128)(2,1)S(1)}, bf16[2,128,512]{2,1,0:T(8,128)(2,1)}, u32[]{:S(2)}) copy-start(bf16[2,128,512]{2,1,0:T(8,128)(2,1)} %get-tuple-element.154) | copy-start | bytes 786436
  10.3 15.7 %all-to-all-start = ((bf16[8,32,512]{2,1,0:T(8,128)(2,1)}), bf16[8,32,512]{2,1,0:T(8,128)(2,1)S(1)}, u32[]{:S(2)}, u32[]{:S(2)}) async-start(bf16[8,32,512]{2,1,0:T(8,128)(2,1)} %get-tuple-element.152), calls=%async_computation | async-start | bytes 524288 | tf_op jit(solution)/shard_map/all_to_all | solution.py:338
  16.2 30.3 %collective-permute-start = (bf16[2,128,1024]{2,1,0:T(8,128)(2,1)S(1)}, bf16[2,128,1024]{2,1,0:T(8,128)(2,1)S(1)}, u32[]{:S(2)}, u32[]{:S(2)}) collective-permute-start(bf16[2,128,1024]{2,1,0:T(8,128)(2,1)S(1)} %pad_maximum_fusion.1), channel_id=1, source_target_pairs={{0,4},{4,0},{1,5},{5,1},{2,6},{6,2},{3,7},{7,3},{8,12},{12,8},{9,1... | collective-permute-start | bytes 1572872 | tf_op jit(solution)/shard_map/ppermute | solution.py:330
  17.5 23.7 %collective-permute-start.10 = (bf16[128,1024]{1,0:T(8,128)(2,1)S(1)}, bf16[128,1024]{1,0:T(8,128)(2,1)S(1)}, u32[]{:S(2)}, u32[]{:S(2)}) collective-permute-start(bf16[128,1024]{1,0:T(8,128)(2,1)S(1)} %bitcast.141), channel_id=1, source_target_pairs={{0,16},{8,24},{16,0},{24,8},{1,17},{9,25},{17,1},{25,9},{2,18},{10... | collective-permute-start | bytes 786440 | tf_op jit(solution)/shard_map/ppermute | solution.py:334
  19.5 30.3 %collective-permute-start.12 = (bf16[128,1024]{1,0:T(8,128)(2,1)S(1)}, bf16[128,1024]{1,0:T(8,128)(2,1)S(1)}, u32[]{:S(2)}, u32[]{:S(2)}) collective-permute-start(bf16[128,1024]{1,0:T(8,128)(2,1)S(1)} %bitcast.142), channel_id=1, source_target_pairs={{0,8},{8,16},{16,24},{24,0},{1,9},{9,17},{17,25},{25,1},{2,10},{10... | collective-permute-start | bytes 786440 | tf_op jit(solution)/shard_map/ppermute | solution.py:334
  19.5 32.3 %collective-permute-start.8 = (bf16[128,1024]{1,0:T(8,128)(2,1)S(1)}, bf16[128,1024]{1,0:T(8,128)(2,1)S(1)}, u32[]{:S(2)}, u32[]{:S(2)}) collective-permute-start(bf16[128,1024]{1,0:T(8,128)(2,1)S(1)} %bitcast.143), channel_id=1, source_target_pairs={{0,24},{8,0},{16,8},{24,16},{1,25},{9,1},{17,9},{25,17},{2,26},{10... | collective-permute-start | bytes 786440 | tf_op jit(solution)/shard_map/ppermute | solution.py:334
  26.0 33.4 %copy-start.23 = (bf16[8,32,512]{2,1,0:T(8,128)(2,1)}, bf16[8,32,512]{2,1,0:T(8,128)(2,1)S(1)}, u32[]{:S(2)}) copy-start(bf16[8,32,512]{2,1,0:T(8,128)(2,1)S(1)} %all-to-all-done.refs_8_) | copy-start | bytes 786436
  26.0 23.9 %copy-start.34 = (bf16[128,256]{1,0:T(8,128)(2,1)S(1)}, bf16[128,256]{1,0:T(8,128)(2,1)}, u32[]{:S(2)}) copy-start(bf16[128,256]{1,0:T(8,128)(2,1)} %get-tuple-element.158) | copy-start | bytes 196612
  26.0 19.7 %all-to-all-start.1 = ((bf16[8,32,512]{2,1,0:T(8,128)(2,1)}), bf16[8,32,512]{2,1,0:T(8,128)(2,1)S(1)}, u32[]{:S(2)}, u32[]{:S(2)}) async-start(bf16[8,32,512]{2,1,0:T(8,128)(2,1)} %get-tuple-element.153), calls=%async_computation.1 | async-start | bytes 524288 | tf_op jit(solution)/shard_map/all_to_all | solution.py:338
  40.4 64.7 %all-gather.3.cloned.1.call-start = ((), (), s32[]{:S(2)}) async-start(), calls=%async_computation.9 | async-start | bytes 2621440 | tf_op jit(solution)/shard_map/all_gather | solution.py:875
  41.2 24.9 %copy-start.36 = (bf16[128,1024]{1,0:T(8,128)(2,1)}, bf16[128,1024]{1,0:T(8,128)(2,1)S(1)}, u32[]{:S(2)}) copy-start(bf16[128,1024]{1,0:T(8,128)(2,1)S(1)} %collective-permute-done.10.refs_6_) | copy-start | bytes 786436
  41.2 10.7 %collective-permute-start.11 = (bf16[128,1024]{1,0:T(8,128)(2,1)S(1)}, bf16[128,1024]{1,0:T(8,128)(2,1)}, u32[]{:S(2)}, u32[]{:S(2)}) collective-permute-start(bf16[128,1024]{1,0:T(8,128)(2,1)S(1)} %collective-permute-done.10.refs_6_), channel_id=1, source_target_pairs={{0,4},{4,0},{1,5},{5,1},{2,6},{6,2},{3,7},{7,3},{8,12},{12,8},{9,1... | collective-permute-start | bytes 786440 | tf_op jit(solution)/shard_map/ppermute | solution.py:330
  46.8 15.8 %collective-permute-start.1 = (bf16[8,32,512]{2,1,0:T(8,128)(2,1)S(1)}, bf16[8,32,512]{2,1,0:T(8,128)(2,1)S(1)}, u32[]{:S(2)}, u32[]{:S(2)}) collective-permute-start(bf16[8,32,512]{2,1,0:T(8,128)(2,1)S(1)} %all-to-all-done.refs_8_), channel_id=1, source_target_pairs={{0,2},{2,0},{1,3},{3,1},{4,6},{6,4},{5,7},{7,5},{8,10},{10,8},{9,1... | collective-permute-start | bytes 786440 | tf_op jit(solution)/shard_map/ppermute | solution.py:330
  47.4 169.5 %reduce-scatter.2.cloned.1.call-start = ((), (), s32[]{:S(2)}) async-start(), calls=%async_computation.8 | async-start | bytes 2703360 | tf_op jit(solution)/shard_map/reduce_scatter | solution.py:953
  48.2 29.3 %copy-start.8 = (bf16[2,128,1024]{2,1,0:T(8,128)(2,1)}, bf16[2,128,1024]{2,1,0:T(8,128)(2,1)S(1)}, u32[]{:S(2)}) copy-start(bf16[2,128,1024]{2,1,0:T(8,128)(2,1)S(1)} %pad_maximum_fusion.2.cot_0) | copy-start | bytes 1572868
  48.7 16.6 %collective-permute-start.4 = (bf16[2,128,1024]{2,1,0:T(8,128)(2,1)S(1)}, bf16[2,128,1024]{2,1,0:T(8,128)(2,1)S(1)}, u32[]{:S(2)}, u32[]{:S(2)}) collective-permute-start(bf16[2,128,1024]{2,1,0:T(8,128)(2,1)S(1)} %pad_maximum_fusion.2.cot_0), channel_id=1, source_target_pairs={{0,2},{2,0},{1,3},{3,1},{4,6},{6,4},{5,7},{7,5},{8,10},{10,8},{9,1... | collective-permute-start | bytes 1572872 | tf_op jit(solution)/shard_map/ppermute | solution.py:330
  49.9 16.1 %copy-start.37 = (bf16[128,1024]{1,0:T(8,128)(2,1)}, bf16[128,1024]{1,0:T(8,128)(2,1)S(1)}, u32[]{:S(2)}) copy-start(bf16[128,1024]{1,0:T(8,128)(2,1)S(1)} %collective-permute-done.12.refs_7_) | copy-start | bytes 786436
  49.9 3.9 %collective-permute-start.5 = (bf16[128,256]{1,0:T(8,128)(2,1)S(1)}, bf16[128,256]{1,0:T(8,128)(2,1)S(1)}, u32[]{:S(2)}, u32[]{:S(2)}) collective-permute-start(bf16[128,256]{1,0:T(8,128)(2,1)S(1)} %copy-done.34), channel_id=1, source_target_pairs={{0,24},{8,0},{16,8},{24,16},{1,25},{9,1},{17,9},{25,17},{2,26},{10... | collective-permute-start | bytes 196616 | tf_op jit(solution)/shard_map/ppermute | solution.py:334
  51.8 14.2 %copy-start.38 = (bf16[128,1024]{1,0:T(8,128)(2,1)}, bf16[128,1024]{1,0:T(8,128)(2,1)S(1)}, u32[]{:S(2)}) copy-start(bf16[128,1024]{1,0:T(8,128)(2,1)S(1)} %collective-permute-done.8.refs_5_) | copy-start | bytes 786436
  51.8 4.1 %collective-permute-start.6 = (bf16[128,256]{1,0:T(8,128)(2,1)S(1)}, bf16[128,256]{1,0:T(8,128)(2,1)S(1)}, u32[]{:S(2)}, u32[]{:S(2)}) collective-permute-start(bf16[128,256]{1,0:T(8,128)(2,1)S(1)} %copy-done.34), channel_id=1, source_target_pairs={{0,16},{8,24},{16,0},{24,8},{1,17},{9,25},{17,1},{25,9},{2,18},{10... | collective-permute-start | bytes 196616 | tf_op jit(solution)/shard_map/ppermute | solution.py:334
  51.8 7.5 %collective-permute-start.7 = (bf16[128,256]{1,0:T(8,128)(2,1)S(1)}, bf16[128,256]{1,0:T(8,128)(2,1)S(1)}, u32[]{:S(2)}, u32[]{:S(2)}) collective-permute-start(bf16[128,256]{1,0:T(8,128)(2,1)S(1)} %copy-done.34), channel_id=1, source_target_pairs={{0,8},{8,16},{16,24},{24,0},{1,9},{9,17},{17,25},{25,1},{2,10},{10... | collective-permute-start | bytes 196616 | tf_op jit(solution)/shard_map/ppermute | solution.py:334
  53.8 10.0 %collective-permute-start.13 = (bf16[128,1024]{1,0:T(8,128)(2,1)S(1)}, bf16[128,1024]{1,0:T(8,128)(2,1)S(1)}, u32[]{:S(2)}, u32[]{:S(2)}) collective-permute-start(bf16[128,1024]{1,0:T(8,128)(2,1)S(1)} %collective-permute-done.12.refs_7_), channel_id=1, source_target_pairs={{0,4},{4,0},{1,5},{5,1},{2,6},{6,2},{3,7},{7,3},{8,12},{12,8},{9,1... | collective-permute-start | bytes 786440 | tf_op jit(solution)/shard_map/ppermute | solution.py:330
  55.9 8.3 %collective-permute-start.9 = (bf16[128,1024]{1,0:T(8,128)(2,1)S(1)}, bf16[128,1024]{1,0:T(8,128)(2,1)S(1)}, u32[]{:S(2)}, u32[]{:S(2)}) collective-permute-start(bf16[128,1024]{1,0:T(8,128)(2,1)S(1)} %collective-permute-done.8.refs_5_), channel_id=1, source_target_pairs={{0,4},{4,0},{1,5},{5,1},{2,6},{6,2},{3,7},{7,3},{8,12},{12,8},{9,1... | collective-permute-start | bytes 786440 | tf_op jit(solution)/shard_map/ppermute | solution.py:330
  59.4 4.9 %collective-permute-start.2 = (bf16[8,32,512]{2,1,0:T(8,128)(2,1)S(1)}, bf16[8,32,512]{2,1,0:T(8,128)(2,1)S(1)}, u32[]{:S(2)}, u32[]{:S(2)}) collective-permute-start(bf16[8,32,512]{2,1,0:T(8,128)(2,1)S(1)} %all-to-all-done.refs_8_), channel_id=1, source_target_pairs={{0,1},{1,0},{2,3},{3,2},{4,5},{5,4},{6,7},{7,6},{8,9},{9,8},{10,11... | collective-permute-start | bytes 786440 | tf_op jit(solution)/shard_map/ppermute | solution.py:330
  62.6 2.6 collective-permute-start.3
  65.3 12.2 %copy-start.13 = (bf16[2,128,1024]{2,1,0:T(8,128)(2,1)}, bf16[2,128,1024]{2,1,0:T(8,128)(2,1)S(1)}, u32[]{:S(2)}) copy-start(bf16[2,128,1024]{2,1,0:T(8,128)(2,1)S(1)} %collective-permute-done.4.cot_1) | copy-start | bytes 1572868
  66.0 11.5 %collective-permute-start.14 = (bf16[4,128,256]{2,1,0:T(8,128)(2,1)S(1)}, bf16[4,128,256]{2,1,0:T(8,128)(2,1)S(1)}, u32[]{:S(2)}, u32[]{:S(2)}) collective-permute-start(bf16[4,128,256]{2,1,0:T(8,128)(2,1)S(1)} %pad_maximum_fusion.4), channel_id=1, source_target_pairs={{0,4},{4,0},{1,5},{5,1},{2,6},{6,2},{3,7},{7,3},{8,12},{12,8},{9,1... | collective-permute-start | bytes 786440 | tf_op jit(solution)/shard_map/ppermute | solution.py:330
  77.6 22.8 %copy-start.12 = (bf16[2,4,128,256]{3,2,1,0:T(8,128)(2,1)}, bf16[2,4,128,256]{3,2,1,0:T(8,128)(2,1)S(1)}, u32[]{:S(2)}) copy-start(bf16[2,4,128,256]{3,2,1,0:T(8,128)(2,1)S(1)} %pad_maximum_fusion.3.own_ref) | copy-start | bytes 1572868
  77.6 20.6 %collective-permute-start.15 = (bf16[2,4,128,256]{3,2,1,0:T(8,128)(2,1)S(1)}, bf16[2,4,128,256]{3,2,1,0:T(8,128)(2,1)S(1)}, u32[]{:S(2)}, u32[]{:S(2)}) collective-permute-start(bf16[2,4,128,256]{3,2,1,0:T(8,128)(2,1)S(1)} %pad_maximum_fusion.3.own_ref), channel_id=1, source_target_pairs={{0,2},{2,0},{1,3},{3,1},{4,6},{6,4},{5,7},{7,5},{8,10},{10,8},{9,1... | collective-permute-start | bytes 1572872 | tf_op jit(solution)/shard_map/ppermute | solution.py:330
  77.7 20.6 %collective-permute-start.16 = (bf16[2,4,128,256]{3,2,1,0:T(8,128)(2,1)S(1)}, bf16[2,4,128,256]{3,2,1,0:T(8,128)(2,1)S(1)}, u32[]{:S(2)}, u32[]{:S(2)}) collective-permute-start(bf16[2,4,128,256]{3,2,1,0:T(8,128)(2,1)S(1)} %pad_maximum_fusion.3.own_ref), channel_id=1, source_target_pairs={{0,1},{1,0},{2,3},{3,2},{4,5},{5,4},{6,7},{7,6},{8,9},{9,8},{10,11... | collective-permute-start | bytes 1572872 | tf_op jit(solution)/shard_map/ppermute | solution.py:330
  98.2 2.1 collective-permute-start.17
  105.1 13.9 %collective-permute-start.22 = (bf16[4,512,512]{2,1,0:T(8,128)(2,1)}, bf16[4,512,512]{2,1,0:T(8,128)(2,1)S(1)}, u32[]{:S(2)}, u32[]{:S(2)}) collective-permute-start(bf16[4,512,512]{2,1,0:T(8,128)(2,1)} %bitcast.136), channel_id=1, source_target_pairs={{0,1},{1,0},{2,3},{3,2},{4,5},{5,4},{6,7},{7,6},{8,9},{9,8},{10,11... | collective-permute-start | bytes 6291464 | tf_op jit(solution)/shard_map/ppermute | solution.py:330
  106.4 8.0 %collective-permute-start.19 = (bf16[128,1024]{1,0:T(8,128)(2,1)}, bf16[128,1024]{1,0:T(8,128)(2,1)S(1)}, u32[]{:S(2)}, u32[]{:S(2)}) collective-permute-start(bf16[128,1024]{1,0:T(8,128)(2,1)} %get-tuple-element.177.m_own), channel_id=1, source_target_pairs={{0,2},{2,0},{1,3},{3,1},{4,6},{6,4},{5,7},{7,5},{8,10},{10,8},{9,1... | collective-permute-start | bytes 786440 | tf_op jit(solution)/shard_map/ppermute | solution.py:330
  107.1 7.7 %collective-permute-start.18 = (bf16[128,1024]{1,0:T(8,128)(2,1)}, bf16[128,1024]{1,0:T(8,128)(2,1)S(1)}, u32[]{:S(2)}, u32[]{:S(2)}) collective-permute-start(bf16[128,1024]{1,0:T(8,128)(2,1)} %get-tuple-element.177.m_own), channel_id=1, source_target_pairs={{0,4},{4,0},{1,5},{5,1},{2,6},{6,2},{3,7},{7,3},{8,12},{12,8},{9,1... | collective-permute-start | bytes 786440 | tf_op jit(solution)/shard_map/ppermute | solution.py:330
  114.4 3.9 %collective-permute-start.20 = (bf16[64,1024]{1,0:T(8,128)(2,1)S(1)}, bf16[64,1024]{1,0:T(8,128)(2,1)S(1)}, u32[]{:S(2)}, u32[]{:S(2)}) collective-permute-start(bf16[64,1024]{1,0:T(8,128)(2,1)S(1)} %slice.202), channel_id=1, source_target_pairs={{0,4},{4,0},{1,5},{5,1},{2,6},{6,2},{3,7},{7,3},{8,12},{12,8},{9,1... | collective-permute-start | bytes 393224 | tf_op jit(solution)/shard_map/ppermute | solution.py:330
  114.8 4.2 %collective-permute-start.21 = (bf16[64,1024]{1,0:T(8,128)(2,1)S(1)}, bf16[64,1024]{1,0:T(8,128)(2,1)S(1)}, u32[]{:S(2)}, u32[]{:S(2)}) collective-permute-start(bf16[64,1024]{1,0:T(8,128)(2,1)S(1)} %slice.203), channel_id=1, source_target_pairs={{0,2},{2,0},{1,3},{3,1},{4,6},{6,4},{5,7},{7,5},{8,10},{10,8},{9,1... | collective-permute-start | bytes 393224 | tf_op jit(solution)/shard_map/ppermute | solution.py:330
  129.2 7.9 %collective-permute-start.23 = (bf16[64,1024]{1,0:T(8,128)(2,1)S(1)}, bf16[64,1024]{1,0:T(8,128)(2,1)S(1)}, u32[]{:S(2)}, u32[]{:S(2)}) collective-permute-start(bf16[64,1024]{1,0:T(8,128)(2,1)S(1)} %get-tuple-element.295), channel_id=1, source_target_pairs={{0,4},{4,0},{1,5},{5,1},{2,6},{6,2},{3,7},{7,3},{8,12},{12,8},{9,1... | collective-permute-start | bytes 393224 | tf_op jit(solution)/shard_map/ppermute | solution.py:330
  130.3 6.8 %collective-permute-start.24 = (bf16[64,1024]{1,0:T(8,128)(2,1)S(1)}, bf16[64,1024]{1,0:T(8,128)(2,1)S(1)}, u32[]{:S(2)}, u32[]{:S(2)}) collective-permute-start(bf16[64,1024]{1,0:T(8,128)(2,1)S(1)} %get-tuple-element.294), channel_id=1, source_target_pairs={{0,2},{2,0},{1,3},{3,1},{4,6},{6,4},{5,7},{7,5},{8,10},{10,8},{9,1... | collective-permute-start | bytes 393224 | tf_op jit(solution)/shard_map/ppermute | solution.py:330
  137.1 6.8 %collective-permute-start.27 = (bf16[4,528,512]{2,1,0:T(8,128)(2,1)}, bf16[4,528,512]{2,1,0:T(8,128)(2,1)S(1)}, u32[]{:S(2)}, u32[]{:S(2)}) collective-permute-start(bf16[4,528,512]{2,1,0:T(8,128)(2,1)} %get-tuple-element.198), channel_id=1, source_target_pairs={{0,1},{1,0},{2,3},{3,2},{4,5},{5,4},{6,7},{7,6},{8,9},{9,8},{10,11... | collective-permute-start | bytes 6488072 | tf_op jit(solution)/shard_map/ppermute | solution.py:330
  140.0 8.0 %collective-permute-start.25 = (bf16[128,1024]{1,0:T(8,128)(2,1)S(1)}, bf16[128,1024]{1,0:T(8,128)(2,1)S(1)}, u32[]{:S(2)}, u32[]{:S(2)}) collective-permute-start(bf16[128,1024]{1,0:T(8,128)(2,1)S(1)} %pad_maximum_fusion.6), channel_id=1, source_target_pairs={{0,2},{2,0},{1,3},{3,1},{4,6},{6,4},{5,7},{7,5},{8,10},{10,8},{9,1... | collective-permute-start | bytes 786440 | tf_op jit(solution)/shard_map/ppermute | solution.py:330
  140.8 7.6 %collective-permute-start.26 = (bf16[128,1024]{1,0:T(8,128)(2,1)S(1)}, bf16[128,1024]{1,0:T(8,128)(2,1)S(1)}, u32[]{:S(2)}, u32[]{:S(2)}) collective-permute-start(bf16[128,1024]{1,0:T(8,128)(2,1)S(1)} %pad_maximum_fusion.5), channel_id=1, source_target_pairs={{0,4},{4,0},{1,5},{5,1},{2,6},{6,2},{3,7},{7,3},{8,12},{12,8},{9,1... | collective-permute-start | bytes 786440 | tf_op jit(solution)/shard_map/ppermute | solution.py:330
  154.7 18.3 %collective-permute-start.28 = (bf16[2,2,4,32,1024]{4,3,2,1,0:T(8,128)(2,1)}, bf16[2,2,4,32,1024]{4,3,2,1,0:T(8,128)(2,1)S(1)}, u32[]{:S(2)}, u32[]{:S(2)}) collective-permute-start(bf16[2,2,4,32,1024]{4,3,2,1,0:T(8,128)(2,1)} %get-tuple-element.203), channel_id=1, source_target_pairs={{0,1},{1,0},{2,3},{3,2},{4,5},{5,4},{6,7},{7,6},{8,9},{9,8},{10,11... | collective-permute-start | bytes 3145736 | tf_op jit(solution)/shard_map/ppermute | solution.py:330
  155.8 17.2 %all-to-all-start.3 = ((bf16[8,128,128]{2,1,0:T(8,128)(2,1)}), bf16[8,128,128]{2,1,0:T(8,128)(2,1)S(1)}, u32[]{:S(2)}, u32[]{:S(2)}) async-start(bf16[8,128,128]{2,1,0:T(8,128)(2,1)} %get-tuple-element.202), calls=%async_computation.3 | async-start | bytes 524288 | tf_op jit(solution)/shard_map/all_to_all | solution.py:338
  173.4 14.0 %collective-permute-start.29 = (bf16[2,4,32,1024]{3,2,1,0:T(8,128)(2,1)S(1)}, bf16[2,4,32,1024]{3,2,1,0:T(8,128)(2,1)S(1)}, u32[]{:S(2)}, u32[]{:S(2)}) collective-permute-start(bf16[2,4,32,1024]{3,2,1,0:T(8,128)(2,1)S(1)} %get-tuple-element.283), channel_id=1, source_target_pairs={{0,2},{2,0},{1,3},{3,1},{4,6},{6,4},{5,7},{7,5},{8,10},{10,8},{9,1... | collective-permute-start | bytes 1572872 | tf_op jit(solution)/shard_map/ppermute | solution.py:330
  187.5 13.9 %copy-start.7 = (bf16[1,128,1024]{2,1,0:T(8,128)(2,1)S(1)}, bf16[1,128,1024]{2,1,0:T(8,128)(2,1)}, u32[]{:S(2)}) copy-start(bf16[1,128,1024]{2,1,0:T(8,128)(2,1)} %param.22) | copy-start | bytes 786436
  187.5 2.7 %collective-permute-start.30 = (bf16[2,8,32,512]{3,2,1,0:T(8,128)(2,1)}, bf16[2,8,32,512]{3,2,1,0:T(8,128)(2,1)S(1)}, u32[]{:S(2)}, u32[]{:S(2)}) collective-permute-start(bf16[2,8,32,512]{3,2,1,0:T(8,128)(2,1)} %get-tuple-element.224), channel_id=1, source_target_pairs={{0,1},{1,0},{2,3},{3,2},{4,5},{5,4},{6,7},{7,6},{8,9},{9,8},{10,11... | collective-permute-start | bytes 1572872 | tf_op jit(solution)/shard_map/ppermute | solution.py:330
  188.6 24.5 %copy-start.19 = (bf16[2,128,1024]{2,1,0:T(8,128)(2,1)S(1)}, bf16[2,128,1024]{2,1,0:T(8,128)(2,1)}, u32[]{:S(2)}) copy-start(bf16[2,128,1024]{2,1,0:T(8,128)(2,1)} %get-tuple-element.207) | copy-start | bytes 1572868
  188.6 8.1 %collective-permute-start.32 = (bf16[4,32,1024]{2,1,0:T(8,128)(2,1)S(1)}, bf16[4,32,1024]{2,1,0:T(8,128)(2,1)S(1)}, u32[]{:S(2)}, u32[]{:S(2)}) collective-permute-start(bf16[4,32,1024]{2,1,0:T(8,128)(2,1)S(1)} %get-tuple-element.285), channel_id=1, source_target_pairs={{0,4},{4,0},{1,5},{5,1},{2,6},{6,2},{3,7},{7,3},{8,12},{12,8},{9,1... | collective-permute-start | bytes 786440 | tf_op jit(solution)/shard_map/ppermute | solution.py:330
  191.4 30.5 %copy-start.3 = (s32[41]{0:T(128)S(1)}, s32[41]{0:T(128)}, u32[]{:S(2)}) copy-start(s32[41]{0:T(128)} %concatenate.13.meta.table) | copy-start | bytes 496
  191.4 7.7 %collective-permute-start.31 = (bf16[8,32,512]{2,1,0:T(8,128)(2,1)S(1)}, bf16[8,32,512]{2,1,0:T(8,128)(2,1)S(1)}, u32[]{:S(2)}, u32[]{:S(2)}) collective-permute-start(bf16[8,32,512]{2,1,0:T(8,128)(2,1)S(1)} %get-tuple-element.287), channel_id=1, source_target_pairs={{0,2},{2,0},{1,3},{3,1},{4,6},{6,4},{5,7},{7,5},{8,10},{10,8},{9,1... | collective-permute-start | bytes 786440 | tf_op jit(solution)/shard_map/ppermute | solution.py:330
  192.9 29.0 %collective-permute-start.35 = (bf16[4,128,1024]{2,1,0:T(8,128)(2,1)}, bf16[4,128,1024]{2,1,0:T(8,128)(2,1)S(1)}, u32[]{:S(2)}, u32[]{:S(2)}) collective-permute-start(bf16[4,128,1024]{2,1,0:T(8,128)(2,1)} %get-tuple-element.230), channel_id=1, source_target_pairs={{0,4},{4,0},{1,5},{5,1},{2,6},{6,2},{3,7},{7,3},{8,12},{12,8},{9,1... | collective-permute-start | bytes 3145736 | tf_op jit(solution)/shard_map/ppermute | solution.py:330
  199.8 33.5 %copy-start.14 = (bf16[4,128,1024]{2,1,0:T(8,128)(2,1)S(1)}, bf16[4,128,1024]{2,1,0:T(8,128)(2,1)}, u32[]{:S(2)}) copy-start(bf16[4,128,1024]{2,1,0:T(8,128)(2,1)} %get-tuple-element.241) | copy-start | bytes 3145732
  199.9 13.3 %collective-permute-start.33 = (bf16[2,128,1024]{2,1,0:T(8,128)(2,1)}, bf16[2,128,1024]{2,1,0:T(8,128)(2,1)}, u32[]{:S(2)}, u32[]{:S(2)}) collective-permute-start(bf16[2,128,1024]{2,1,0:T(8,128)(2,1)} %get-tuple-element.228), channel_id=1, source_target_pairs={{0,2},{2,0},{1,3},{3,1},{4,6},{6,4},{5,7},{7,5},{8,10},{10,8},{9,1... | collective-permute-start | bytes 1572872 | tf_op jit(solution)/shard_map/ppermute | solution.py:330
  201.4 20.5 %all-to-all-start.4 = ((bf16[8,32,512]{2,1,0:T(8,128)(2,1)}), bf16[8,32,512]{2,1,0:T(8,128)(2,1)S(1)}, u32[]{:S(2)}, u32[]{:S(2)}) async-start(bf16[8,32,512]{2,1,0:T(8,128)(2,1)} %add_convert_fusion.7), calls=%async_computation.4 | async-start | bytes 524288 | tf_op jit(solution)/shard_map/all_to_all | solution.py:338
  209.5 9.0 %collective-permute-start.36 = (bf16[32,1024]{1,0:T(8,128)(2,1)}, bf16[32,1024]{1,0:T(8,128)(2,1)S(1)}, u32[]{:S(2)}, u32[]{:S(2)}) collective-permute-start(bf16[32,1024]{1,0:T(8,128)(2,1)} %get-tuple-element.291), channel_id=1, source_target_pairs={{0,8},{8,16},{16,24},{24,0},{1,9},{9,17},{17,25},{25,1},{2,10},{10... | collective-permute-start | bytes 196616 | tf_op jit(solution)/shard_map/ppermute | solution.py:334
  210.7 8.2 %collective-permute-start.37 = (bf16[32,1024]{1,0:T(8,128)(2,1)}, bf16[32,1024]{1,0:T(8,128)(2,1)S(1)}, u32[]{:S(2)}, u32[]{:S(2)}) collective-permute-start(bf16[32,1024]{1,0:T(8,128)(2,1)} %get-tuple-element.290), channel_id=1, source_target_pairs={{0,16},{8,24},{16,0},{24,8},{1,17},{9,25},{17,1},{25,9},{2,18},{10... | collective-permute-start | bytes 196616 | tf_op jit(solution)/shard_map/ppermute | solution.py:334
  211.7 9.0 %collective-permute-start.38 = (bf16[32,1024]{1,0:T(8,128)(2,1)S(1)}, bf16[32,1024]{1,0:T(8,128)(2,1)S(1)}, u32[]{:S(2)}, u32[]{:S(2)}) collective-permute-start(bf16[32,1024]{1,0:T(8,128)(2,1)S(1)} %get-tuple-element.289), channel_id=1, source_target_pairs={{0,24},{8,0},{16,8},{24,16},{1,25},{9,1},{17,9},{25,17},{2,26},{10... | collective-permute-start | bytes 196616 | tf_op jit(solution)/shard_map/ppermute | solution.py:334
  214.8 28.9 %collective-permute-start.34 = (bf16[128,1024]{1,0:T(8,128)(2,1)}, bf16[128,1024]{1,0:T(8,128)(2,1)}, u32[]{:S(2)}, u32[]{:S(2)}) collective-permute-start(bf16[128,1024]{1,0:T(8,128)(2,1)} %fusion.16), channel_id=1, source_target_pairs={{0,4},{4,0},{1,5},{5,1},{2,6},{6,2},{3,7},{7,3},{8,12},{12,8},{9,1... | collective-permute-start | bytes 786440 | tf_op jit(solution)/shard_map/ppermute | solution.py:330
  221.9 21.9 %copy-start.1 = (bf16[8,32,512]{2,1,0:T(8,128)(2,1)}, bf16[8,32,512]{2,1,0:T(8,128)(2,1)S(1)}, u32[]{:S(2)}) copy-start(bf16[8,32,512]{2,1,0:T(8,128)(2,1)S(1)} %all-to-all-done.4.qkv_ref.refs_1_) | copy-start | bytes 786436
  225.7 12.4 %all-to-all-start.5 = ((f32[32,1,128]{2,1,0:T(1,128)}), f32[32,1,128]{2,1,0:T(1,128)S(1)}, u32[]{:S(2)}, u32[]{:S(2)}) async-start(f32[32,1,128]{2,1,0:T(1,128)} %get-tuple-element.238), calls=%async_computation.6 | async-start | bytes 32768 | tf_op jit(solution)/shard_map/all_to_all | solution.py:338
  234.4 19.1 %collective-permute-start.39 = (bf16[128,1024]{1,0:T(8,128)(2,1)}, bf16[128,1024]{1,0:T(8,128)(2,1)S(1)}, u32[]{:S(2)}, u32[]{:S(2)}) collective-permute-start(bf16[128,1024]{1,0:T(8,128)(2,1)} %get-tuple-element.281), channel_id=1, source_target_pairs={{0,8},{8,16},{16,24},{24,0},{1,9},{9,17},{17,25},{25,1},{2,10},{10... | collective-permute-start | bytes 786440 | tf_op jit(solution)/shard_map/ppermute | solution.py:334
  235.7 22.5 %collective-permute-start.40 = (bf16[128,1024]{1,0:T(8,128)(2,1)}, bf16[128,1024]{1,0:T(8,128)(2,1)S(1)}, u32[]{:S(2)}, u32[]{:S(2)}) collective-permute-start(bf16[128,1024]{1,0:T(8,128)(2,1)} %get-tuple-element.280), channel_id=1, source_target_pairs={{0,16},{8,24},{16,0},{24,8},{1,17},{9,25},{17,1},{25,9},{2,18},{10... | collective-permute-start | bytes 786440 | tf_op jit(solution)/shard_map/ppermute | solution.py:334
  236.7 23.9 %collective-permute-start.41 = (bf16[128,1024]{1,0:T(8,128)(2,1)}, bf16[128,1024]{1,0:T(8,128)(2,1)S(1)}, u32[]{:S(2)}, u32[]{:S(2)}) collective-permute-start(bf16[128,1024]{1,0:T(8,128)(2,1)} %get-tuple-element.279), channel_id=1, source_target_pairs={{0,24},{8,0},{16,8},{24,16},{1,25},{9,1},{17,9},{25,17},{2,26},{10... | collective-permute-start | bytes 786440 | tf_op jit(solution)/shard_map/ppermute | solution.py:334
  238.1 12.2 %all-to-all-start.6 = ((bf16[8,32,512]{2,1,0:T(8,128)(2,1)}), bf16[8,32,512]{2,1,0:T(8,128)(2,1)}, u32[]{:S(2)}, u32[]{:S(2)}) async-start(bf16[8,32,512]{2,1,0:T(8,128)(2,1)} %bitcast.145), calls=%async_computation.7 | async-start | bytes 524288 | tf_op jit(solution)/shard_map/all_to_all | solution.py:338
  (29 other events, 109.3 us)
Sparse Core Ops, SparseCore 0:
  47.5 49.6 all-gather.2
  156.0 49.0 reduce-scatter.1
